TPU v7x, 512 devices: a whole 4x4x16 slice. The times are simulated.
512 devices in a mesh: blk: 512 (over x, y, z, core).
Axes of the slice: x: 4, y: 4, z: 16, core: 2. Of those that a mesh axis runs over, the one named last changes fastest.
Arguments:
- embeddings: float32 [262144, 768], P('blk'), may hold values from -2 to 2
- labels: int32 [262144], P('blk'), may hold values from 0 to 255
Outputs:
- scores: float32 [262144, 256], P('blk')
All inputs are finite; a program needn't handle non-finite values.
Results may differ from a plain program's by a relative error of at most 0.00077.
Values sent between devices are 32-bit elements; how exact they have to be, the bound alone decides.
No kernel may reach another device: no remote copies, remote signals or barrier semaphores. Data moves between devices by JAX's collectives and lax.ppermute only.
A program may use at most 64 MiB of HBM per device.

v0:
```python
import jax
import jax.numpy as jnp
from jax import lax
from jax.sharding import PartitionSpec as P

CLUSTERS = 256
STEPS = 6


def shifted(value, axis, by):
    size = lax.axis_size(axis)
    return lax.ppermute(value, axis, [(i, (i + by) % size) for i in range(size)])


def kernel_tile(left, left_norms, right, right_norms):
    inner = lax.dot_general(
        left,
        right,
        (((1,), (1,)), ((), ())),
        precision=lax.Precision.HIGHEST,
        preferred_element_type=jnp.float32,
    )
    return jnp.exp(-(left_norms[:, None] + right_norms[None, :] - 2.0 * inner)).astype(jnp.bfloat16)


def make_onehot(labels, clusters):
    return (labels[:, None] == jnp.arange(clusters, dtype=jnp.int32)[None, :]).astype(jnp.bfloat16)


def mirror_product(kernel, onehot):
    return lax.dot_general(
        kernel, onehot, (((0,), (0,)), ((), ())), preferred_element_type=jnp.float32
    )


def on_device(embeddings, labels):
    row_norms = jnp.sum(embeddings * embeddings, axis=1)
    onehot = make_onehot(labels, CLUSTERS)
    own_kernel = kernel_tile(embeddings, row_norms, embeddings, row_norms)
    scores = jnp.dot(own_kernel, onehot, preferred_element_type=jnp.float32)
    visitor = (embeddings, labels)
    for offset in range(1, STEPS + 1):
        visitor = shifted((visitor[0], visitor[1]), "blk", 1)
        visitor_norms = jnp.sum(visitor[0] * visitor[0], axis=1)
        kernel = kernel_tile(embeddings, row_norms, visitor[0], visitor_norms)
        scores = scores + jnp.dot(
            kernel, make_onehot(visitor[1], CLUSTERS), preferred_element_type=jnp.float32
        )
        mirrored = mirror_product(kernel, onehot)
        scores = scores + shifted(mirrored, "blk", -offset)
    return scores


def solution(mesh):
    placed = (P("blk", None), P("blk"))
    return jax.shard_map(
        on_device, mesh=mesh, in_specs=placed, out_specs=P("blk", None), check_vma=False
    )
```

profile of v0, /device:TPU:0, one launch (start us, length us, event | category | flops | bytes accessed | tf_op | source)
XLA Modules:
  0.0 279.5 jit_solution(2691131867314862082)
XLA Ops:
  2.0 26.5 %collective-permute-done = f32[512,768]{1,0:T(8,128)S(1)} collective-permute-done((f32[512,768]{1,0:T(8,128)}, f32[512,768]{1,0:T(8,128)S(1)}, u32[]{:S(2)}, u32[]{:S(2)}) %collective-permute-start) | collective-permute-done | bytes 1572896 | tf_op jit(solution)/shard_map/ppermute | solution.py:12
  30.5 25.2 %collective-permute-done.3 = f32[512,768]{1,0:T(8,128)S(1)} collective-permute-done((f32[512,768]{1,0:T(8,128)S(1)}, f32[512,768]{1,0:T(8,128)S(1)}, u32[]{:S(2)}, u32[]{:S(2)}) %collective-permute-start.3) | collective-permute-done | bytes 1572896 | tf_op jit(solution)/shard_map/ppermute | solution.py:12
  59.5 23.3 %collective-permute-done.1 = s32[512]{0:T(512)S(1)} collective-permute-done((s32[512]{0:T(512)}, s32[512]{0:T(512)S(1)}, u32[]{:S(2)}, u32[]{:S(2)}) %collective-permute-start.1) | collective-permute-done | bytes 2080 | tf_op jit(solution)/shard_map/ppermute | solution.py:12
  84.8 8.4 %collective-permute-done.4 = s32[512]{0:T(512)S(1)} collective-permute-done((s32[512]{0:T(512)S(1)}, s32[512]{0:T(512)S(1)}, u32[]{:S(2)}, u32[]{:S(2)}) %collective-permute-start.4) | collective-permute-done | bytes 2080 | tf_op jit(solution)/shard_map/ppermute | solution.py:12
  98.6 4.9 %collective-permute-done.7 = s32[512]{0:T(512)S(1)} collective-permute-done((s32[512]{0:T(512)S(1)}, s32[512]{0:T(512)S(1)}, u32[]{:S(2)}, u32[]{:S(2)}) %collective-permute-start.7) | collective-permute-done | bytes 2080 | tf_op jit(solution)/shard_map/ppermute | solution.py:12
  105.4 2.8 fusion.3
  108.2 14.1 %collective-permute-done.10 = s32[512]{0:T(512)S(1)} collective-permute-done((s32[512]{0:T(512)S(1)}, s32[512]{0:T(512)S(1)}, u32[]{:S(2)}, u32[]{:S(2)}) %collective-permute-start.10) | collective-permute-done | bytes 2080 | tf_op jit(solution)/shard_map/ppermute | solution.py:12
  124.7 8.0 %collective-permute-done.13 = s32[512]{0:T(512)S(1)} collective-permute-done((s32[512]{0:T(512)S(1)}, s32[512]{0:T(512)S(1)}, u32[]{:S(2)}, u32[]{:S(2)}) %collective-permute-start.13) | collective-permute-done | bytes 2080 | tf_op jit(solution)/shard_map/ppermute | solution.py:12
  134.7 2.8 exponential_convert_fusion.5
  137.9 9.1 %collective-permute-start.2 = (f32[512,256]{1,0:T(8,128)S(1)}, f32[512,256]{1,0:T(8,128)S(1)}, u32[]{:S(2)}, u32[]{:S(2)}) collective-permute-start(f32[512,256]{1,0:T(8,128)S(1)} %fusion.15), channel_id=1, source_target_pairs={{0,511},{1,0},{2,1},{3,2},{4,3},{5,4},{6,5},{7,6},{8,7},{9,8},{10,... | collective-permute-start | bytes 1572872 | tf_op jit(solution)/shard_map/ppermute | solution.py:12
  147.2 2.1 collective-permute-start.12
  149.3 2.8 exponential_convert_fusion.4
  152.6 2.3 collective-permute-start.5
  155.0 2.8 exponential_convert_fusion.3
  160.6 3.4 %collective-permute-done.5 = f32[512,256]{1,0:T(8,128)S(1)} collective-permute-done((f32[512,256]{1,0:T(8,128)S(1)}, f32[512,256]{1,0:T(8,128)S(1)}, u32[]{:S(2)}, u32[]{:S(2)}) %collective-permute-start.5) | collective-permute-done | bytes 524320 | tf_op jit(solution)/shard_map/ppermute | solution.py:12
  164.5 9.9 %collective-permute-done.12 = f32[512,768]{1,0:T(8,128)S(1)} collective-permute-done((f32[512,768]{1,0:T(8,128)S(1)}, f32[512,768]{1,0:T(8,128)S(1)}, u32[]{:S(2)}, u32[]{:S(2)}) %collective-permute-start.12) | collective-permute-done | bytes 1572896 | tf_op jit(solution)/shard_map/ppermute | solution.py:12
  174.4 2.1 collective-permute-start.15
  177.1 2.8 exponential_convert_fusion.2
  180.3 21.8 %collective-permute-start.11 = (f32[512,256]{1,0:T(8,128)S(1)}, f32[512,256]{1,0:T(8,128)S(1)}, u32[]{:S(2)}, u32[]{:S(2)}) collective-permute-start(f32[512,256]{1,0:T(8,128)S(1)} %fusion.12), channel_id=1, source_target_pairs={{0,508},{1,509},{2,510},{3,511},{4,0},{5,1},{6,2},{7,3},{8,4},{9,5... | collective-permute-start | bytes 1572872 | tf_op jit(solution)/shard_map/ppermute | solution.py:12
  202.3 2.8 exponential_convert_fusion.1
  207.6 2.8 exponential_convert_fusion
  212.7 18.1 %collective-permute-done.11 = f32[512,256]{1,0:T(8,128)S(1)} collective-permute-done((f32[512,256]{1,0:T(8,128)S(1)}, f32[512,256]{1,0:T(8,128)S(1)}, u32[]{:S(2)}, u32[]{:S(2)}) %collective-permute-start.11) | collective-permute-done | bytes 524320 | tf_op jit(solution)/shard_map/ppermute | solution.py:12
  231.2 33.6 %collective-permute-done.14 = f32[512,256]{1,0:T(8,128)S(1)} collective-permute-done((f32[512,256]{1,0:T(8,128)S(1)}, f32[512,256]{1,0:T(8,128)S(1)}, u32[]{:S(2)}, u32[]{:S(2)}) %collective-permute-start.14) | collective-permute-done | bytes 524320 | tf_op jit(solution)/shard_map/ppermute | solution.py:12
  265.2 13.0 %collective-permute-done.17 = f32[512,256]{1,0:T(8,128)S(1)} collective-permute-done((f32[512,256]{1,0:T(8,128)S(1)}, f32[512,256]{1,0:T(8,128)S(1)}, u32[]{:S(2)}, u32[]{:S(2)}) %collective-permute-start.17) | collective-permute-done | bytes 524320 | tf_op jit(solution)/shard_map/ppermute | solution.py:12
  (43 shorter events, 33.9 us)
Async XLA Ops:
  0.0 105.4 %copy-start = (f32[512,768]{1,0:T(8,128)S(1)}, f32[512,768]{1,0:T(8,128)}, u32[]{:S(2)}) copy-start(f32[512,768]{1,0:T(8,128)} %param.2) | copy-start | bytes 4718596
  0.0 28.5 %collective-permute-start = (f32[512,768]{1,0:T(8,128)}, f32[512,768]{1,0:T(8,128)S(1)}, u32[]{:S(2)}, u32[]{:S(2)}) collective-permute-start(f32[512,768]{1,0:T(8,128)} %param.2), channel_id=1, source_target_pairs={{0,1},{1,2},{2,3},{3,4},{4,5},{5,6},{6,7},{7,8},{8,9},{9,10},{10,1... | collective-permute-start | bytes 4718600 | tf_op jit(solution)/shard_map/ppermute | solution.py:12
  28.5 27.2 %collective-permute-start.3 = (f32[512,768]{1,0:T(8,128)S(1)}, f32[512,768]{1,0:T(8,128)S(1)}, u32[]{:S(2)}, u32[]{:S(2)}) collective-permute-start(f32[512,768]{1,0:T(8,128)S(1)} %collective-permute-done), channel_id=1, source_target_pairs={{0,1},{1,2},{2,3},{3,4},{4,5},{5,6},{6,7},{7,8},{8,9},{9,10},{10,1... | collective-permute-start | bytes 4718600 | tf_op jit(solution)/shard_map/ppermute | solution.py:12
  55.7 39.4 %collective-permute-start.6 = (f32[512,768]{1,0:T(8,128)S(1)}, f32[512,768]{1,0:T(8,128)S(1)}, u32[]{:S(2)}, u32[]{:S(2)}) collective-permute-start(f32[512,768]{1,0:T(8,128)S(1)} %collective-permute-done.3), channel_id=1, source_target_pairs={{0,1},{1,2},{2,3},{3,4},{4,5},{5,6},{6,7},{7,8},{8,9},{9,10},{10,1... | collective-permute-start | bytes 4718600 | tf_op jit(solution)/shard_map/ppermute | solution.py:12
  57.6 25.3 %collective-permute-start.1 = (s32[512]{0:T(512)}, s32[512]{0:T(512)S(1)}, u32[]{:S(2)}, u32[]{:S(2)}) collective-permute-start(s32[512]{0:T(512)} %param.3), channel_id=1, source_target_pairs={{0,1},{1,2},{2,3},{3,4},{4,5},{5,6},{6,7},{7,8},{8,9},{9,10},{10,1... | collective-permute-start | bytes 6152 | tf_op jit(solution)/shard_map/ppermute | solution.py:12
  82.9 10.3 %collective-permute-start.4 = (s32[512]{0:T(512)S(1)}, s32[512]{0:T(512)S(1)}, u32[]{:S(2)}, u32[]{:S(2)}) collective-permute-start(s32[512]{0:T(512)S(1)} %collective-permute-done.1), channel_id=1, source_target_pairs={{0,1},{1,2},{2,3},{3,4},{4,5},{5,6},{6,7},{7,8},{8,9},{9,10},{10,1... | collective-permute-start | bytes 6152 | tf_op jit(solution)/shard_map/ppermute | solution.py:12
  93.2 10.3 %collective-permute-start.7 = (s32[512]{0:T(512)S(1)}, s32[512]{0:T(512)S(1)}, u32[]{:S(2)}, u32[]{:S(2)}) collective-permute-start(s32[512]{0:T(512)S(1)} %collective-permute-done.4), channel_id=1, source_target_pairs={{0,1},{1,2},{2,3},{3,4},{4,5},{5,6},{6,7},{7,8},{8,9},{9,10},{10,1... | collective-permute-start | bytes 6152 | tf_op jit(solution)/shard_map/ppermute | solution.py:12
  95.1 52.1 %collective-permute-start.9 = (f32[512,768]{1,0:T(8,128)S(1)}, f32[512,768]{1,0:T(8,128)S(1)}, u32[]{:S(2)}, u32[]{:S(2)}) collective-permute-start(f32[512,768]{1,0:T(8,128)S(1)} %collective-permute-done.6), channel_id=1, source_target_pairs={{0,1},{1,2},{2,3},{3,4},{4,5},{5,6},{6,7},{7,8},{8,9},{9,10},{10,1... | collective-permute-start | bytes 4718600 | tf_op jit(solution)/shard_map/ppermute | solution.py:12
  98.6 25.6 %copy-start.1 = (s32[512]{0:T(512)S(1)}, s32[512]{0:T(512)}, u32[]{:S(2)}) copy-start(s32[512]{0:T(512)} %param.3) | copy-start | bytes 6148
  103.5 18.8 %collective-permute-start.10 = (s32[512]{0:T(512)S(1)}, s32[512]{0:T(512)S(1)}, u32[]{:S(2)}, u32[]{:S(2)}) collective-permute-start(s32[512]{0:T(512)S(1)} %collective-permute-done.7), channel_id=1, source_target_pairs={{0,1},{1,2},{2,3},{3,4},{4,5},{5,6},{6,7},{7,8},{8,9},{9,10},{10,1... | collective-permute-start | bytes 6152 | tf_op jit(solution)/shard_map/ppermute | solution.py:12
  122.3 10.3 %collective-permute-start.13 = (s32[512]{0:T(512)S(1)}, s32[512]{0:T(512)S(1)}, u32[]{:S(2)}, u32[]{:S(2)}) collective-permute-start(s32[512]{0:T(512)S(1)} %collective-permute-done.10), channel_id=1, source_target_pairs={{0,1},{1,2},{2,3},{3,4},{4,5},{5,6},{6,7},{7,8},{8,9},{9,10},{10,1... | collective-permute-start | bytes 6152 | tf_op jit(solution)/shard_map/ppermute | solution.py:12
  132.6 132.6 %collective-permute-start.16 = (s32[512]{0:T(512)S(1)}, s32[512]{0:T(512)S(1)}, u32[]{:S(2)}, u32[]{:S(2)}) collective-permute-start(s32[512]{0:T(512)S(1)} %collective-permute-done.13), channel_id=1, source_target_pairs={{0,1},{1,2},{2,3},{3,4},{4,5},{5,6},{6,7},{7,8},{8,9},{9,10},{10,1... | collective-permute-start | bytes 6152 | tf_op jit(solution)/shard_map/ppermute | solution.py:12
  137.9 22.3 %collective-permute-start.2 = (f32[512,256]{1,0:T(8,128)S(1)}, f32[512,256]{1,0:T(8,128)S(1)}, u32[]{:S(2)}, u32[]{:S(2)}) collective-permute-start(f32[512,256]{1,0:T(8,128)S(1)} %fusion.15), channel_id=1, source_target_pairs={{0,511},{1,0},{2,1},{3,2},{4,3},{5,4},{6,5},{7,6},{8,7},{9,8},{10,... | collective-permute-start | bytes 1572872 | tf_op jit(solution)/shard_map/ppermute | solution.py:12
  147.2 27.2 %collective-permute-start.12 = (f32[512,768]{1,0:T(8,128)S(1)}, f32[512,768]{1,0:T(8,128)S(1)}, u32[]{:S(2)}, u32[]{:S(2)}) collective-permute-start(f32[512,768]{1,0:T(8,128)S(1)} %collective-permute-done.9), channel_id=1, source_target_pairs={{0,1},{1,2},{2,3},{3,4},{4,5},{5,6},{6,7},{7,8},{8,9},{9,10},{10,1... | collective-permute-start | bytes 4718600 | tf_op jit(solution)/shard_map/ppermute | solution.py:12
  152.6 11.5 %collective-permute-start.5 = (f32[512,256]{1,0:T(8,128)S(1)}, f32[512,256]{1,0:T(8,128)S(1)}, u32[]{:S(2)}, u32[]{:S(2)}) collective-permute-start(f32[512,256]{1,0:T(8,128)S(1)} %fusion.14), channel_id=1, source_target_pairs={{0,510},{1,511},{2,0},{3,1},{4,2},{5,3},{6,4},{7,5},{8,6},{9,7},{1... | collective-permute-start | bytes 1572872 | tf_op jit(solution)/shard_map/ppermute | solution.py:12
  158.3 18.2 %collective-permute-start.8 = (f32[512,256]{1,0:T(8,128)S(1)}, f32[512,256]{1,0:T(8,128)S(1)}, u32[]{:S(2)}, u32[]{:S(2)}) collective-permute-start(f32[512,256]{1,0:T(8,128)S(1)} %fusion.13), channel_id=1, source_target_pairs={{0,509},{1,510},{2,511},{3,0},{4,1},{5,2},{6,3},{7,4},{8,5},{9,6},... | collective-permute-start | bytes 1572872 | tf_op jit(solution)/shard_map/ppermute | solution.py:12
  174.4 33.0 %collective-permute-start.15 = (f32[512,768]{1,0:T(8,128)S(1)}, f32[512,768]{1,0:T(8,128)S(1)}, u32[]{:S(2)}, u32[]{:S(2)}) collective-permute-start(f32[512,768]{1,0:T(8,128)S(1)} %collective-permute-done.12), channel_id=1, source_target_pairs={{0,1},{1,2},{2,3},{3,4},{4,5},{5,6},{6,7},{7,8},{8,9},{9,10},{10,1... | collective-permute-start | bytes 4718600 | tf_op jit(solution)/shard_map/ppermute | solution.py:12
  180.3 50.5 %collective-permute-start.11 = (f32[512,256]{1,0:T(8,128)S(1)}, f32[512,256]{1,0:T(8,128)S(1)}, u32[]{:S(2)}, u32[]{:S(2)}) collective-permute-start(f32[512,256]{1,0:T(8,128)S(1)} %fusion.12), channel_id=1, source_target_pairs={{0,508},{1,509},{2,510},{3,511},{4,0},{5,1},{6,2},{7,3},{8,4},{9,5... | collective-permute-start | bytes 1572872 | tf_op jit(solution)/shard_map/ppermute | solution.py:12
  205.5 59.3 %collective-permute-start.14 = (f32[512,256]{1,0:T(8,128)S(1)}, f32[512,256]{1,0:T(8,128)S(1)}, u32[]{:S(2)}, u32[]{:S(2)}) collective-permute-start(f32[512,256]{1,0:T(8,128)S(1)} %fusion.11), channel_id=1, source_target_pairs={{0,507},{1,508},{2,509},{3,510},{4,511},{5,0},{6,1},{7,2},{8,3},{9... | collective-permute-start | bytes 1572872 | tf_op jit(solution)/shard_map/ppermute | solution.py:12
  210.8 67.4 %collective-permute-start.17 = (f32[512,256]{1,0:T(8,128)S(1)}, f32[512,256]{1,0:T(8,128)S(1)}, u32[]{:S(2)}, u32[]{:S(2)}) collective-permute-start(f32[512,256]{1,0:T(8,128)S(1)} %fusion.10), channel_id=1, source_target_pairs={{0,506},{1,507},{2,508},{3,509},{4,510},{5,511},{6,0},{7,1},{8,2},... | collective-permute-start | bytes 1572872 | tf_op jit(solution)/shard_map/ppermute | solution.py:12
where the time goes:
time: 280 us; the launch traced here: 279 us
  waiting for transfers between devices  188 us (67%)
  starting transfers between devices  62.3 us (22%)
  matrix products  25.7 us (9%)
    ppermute x18, waiting for transfers between devices, shifted(): lax.ppermute(value, axis, [(i, (i + by) % size) for i in range(size)])  188 us
    ppermute x18, starting transfers between devices, shifted(): lax.ppermute(value, axis, [(i, (i + by) % size) for i in range(size)])  62.3 us
    dot_general x7, matrix products, kernel_tile(): lax.dot_general(left, right, (((1,), (1,)), ((), ())), precision=lax.Prec...  19.5 us
  transfers between devices with their start and end apart: 18, of which 12 were waited for; matrix products, arithmetic and copies ran while one was open for 10% of the time, Pallas kernels for 0%

commit v1 on v0

v1 whole, which is shorter than its diff:
```python
import jax
import jax.numpy as jnp
from jax import lax
from jax.experimental import pallas as pl
from jax.experimental.pallas import tpu as pltpu
from jax.sharding import PartitionSpec as P

CLUSTERS = 256
TOP = 8


def even_odd(n, even, odd):
    return [(i, (i + (even if i % 2 == 0 else odd)) % n) for i in range(n)]


def pull(value):
    n = lax.axis_size("blk")
    return lax.ppermute(value, "blk", even_odd(n, -2, 2))


def push(value):
    n = lax.axis_size("blk")
    return lax.ppermute(value, "blk", even_odd(n, 2, -2))


def swap(value):
    n = lax.axis_size("blk")
    return lax.ppermute(value, "blk", even_odd(n, 1, -1))


def hot(message_ref, rows):
    cluster = lax.broadcasted_iota(jnp.int32, (CLUSTERS, rows), 0)
    same = cluster == message_ref[0:1, :rows].astype(jnp.int32)
    return jnp.where(same, 1.0, 0.0).astype(jnp.bfloat16)


def kernel_tile(left, right):
    left_norms = jnp.sum(left * left, axis=1, keepdims=True)
    right_norms = jnp.sum(right * right, axis=1, keepdims=True)
    right_norms = jnp.transpose(jnp.broadcast_to(right_norms, (right.shape[0], 128)))[0:1, :]
    inner = lax.dot_general(
        left,
        right,
        (((1,), (1,)), ((), ())),
        precision=lax.Precision.HIGHEST,
        preferred_element_type=jnp.float32,
    )
    return jnp.exp(-(left_norms + right_norms - 2.0 * inner)).astype(jnp.bfloat16)


def left_sums(right_hot, kernel):
    return lax.dot_general(
        right_hot, kernel, (((1,), (1,)), ((), ())), preferred_element_type=jnp.float32
    )


def right_sums(left_hot, kernel):
    return jnp.dot(left_hot, kernel, preferred_element_type=jnp.float32)


def self_body(own_ref, own_out):
    own = own_ref[TOP:, :]
    rows = own.shape[0]
    own_out[...] = left_sums(hot(own_ref, rows), kernel_tile(own, own))


def pair_body(left_ref, right_ref, left_in, right_in, left_out, right_out):
    left, right = left_ref[TOP:, :], right_ref[TOP:, :]
    rows = left.shape[0]
    kernel = kernel_tile(left, right)
    left_out[...] = left_in[...] + left_sums(hot(right_ref, rows), kernel)
    right_out[...] = right_in[...] + right_sums(hot(left_ref, rows), kernel)


def halves(left, left_hot, first_ref, second_ref, total, right_out):
    half = second_ref.shape[0]
    right_hot = hot(first_ref, 2 * half)
    for right, span in (
        (first_ref[TOP:, :], slice(0, half)),
        (second_ref[...], slice(half, 2 * half)),
    ):
        kernel = kernel_tile(left, right)
        total += left_sums(right_hot[:, span], kernel)
        right_out[:, span] += right_sums(left_hot, kernel)
    return total


def visitor_body(
    own_ref, b2_ref, first_ref, second_ref, own_in, for_2_in, own_out, for_2_out, for_y_out
):
    rows = own_ref.shape[0] - TOP
    for_y_out[...] = jnp.zeros_like(for_y_out)
    own_out[...] = halves(
        own_ref[TOP:, :], hot(own_ref, rows), first_ref, second_ref, own_in[...], for_y_out
    )
    for_2_out[...] = halves(
        b2_ref[TOP:, :], hot(b2_ref, rows), first_ref, second_ref, for_2_in[...], for_y_out
    )


def late_body(
    even_ref, bm2_ref, b4_ref, first_ref, second_ref, for_m2_in, for_y_in,
    for_m2_out, for_4_out, for_y_out,
):
    even = even_ref[0] == 1
    bm2, b4 = bm2_ref[TOP:, :], b4_ref[TOP:, :]
    rows = bm2.shape[0]
    kernel = kernel_tile(bm2, b4)
    bm2_hot, b4_hot = hot(bm2_ref, rows), hot(b4_ref, rows)
    for_m2_out[...] = for_m2_in[...] + left_sums(b4_hot, kernel)
    for_4_out[...] = right_sums(bm2_hot, kernel)
    for_y_out[...] = for_y_in[...]
    far = halves(
        jnp.where(even, bm2, b4),
        jnp.where(even, bm2_hot, b4_hot),
        first_ref,
        second_ref,
        jnp.zeros_like(for_y_out),
        for_y_out,
    )
    for_m2_out[...] += jnp.where(even, far, 0.0)
    for_4_out[...] += jnp.where(even, 0.0, far)


def call(body, outs, rows, *args):
    shape = jax.ShapeDtypeStruct((CLUSTERS, rows), jnp.float32)
    vmem = pl.BlockSpec(memory_space=pltpu.VMEM)
    smem = pl.BlockSpec(memory_space=pltpu.SMEM)
    return pl.pallas_call(
        body,
        out_shape=[shape] * outs,
        in_specs=[smem if a.ndim == 1 else vmem for a in args],
        out_specs=[vmem] * outs,
        compiler_params=pltpu.CompilerParams(vmem_limit_bytes=32 * 2**20),
        cost_estimate=pl.CostEstimate(flops=1000, bytes_accessed=1000, transcendentals=0),
    )(*args)


def on_device(embeddings, labels):
    rows, dim = embeddings.shape
    cut = TOP + rows // 2
    is_even = lax.axis_index("blk") % 2 == 0
    zero = jnp.zeros((CLUSTERS, rows), jnp.float32)
    top = jnp.pad(labels.astype(jnp.float32)[None, :], ((0, TOP - 1), (0, dim - rows)))
    own = jnp.concatenate([top, embeddings], axis=0)

    b2 = pull(own)
    (score,) = call(self_body, 1, rows, own)
    later_own, score = lax.optimization_barrier((own, score))
    bm2 = push(later_own)
    b4 = pull(b2)

    score, for_2 = call(pair_body, 2, rows, own, b2, score, zero)
    bm2, score, for_2 = lax.optimization_barrier((bm2, score, for_2))

    first = swap(jnp.where(is_even, b2[:cut], bm2[:cut]))
    second = swap(jnp.where(is_even, b2[cut:], bm2[cut:]))
    for_m2, for_2 = call(pair_body, 2, rows, bm2, b2, zero, for_2)

    first, second, for_2, for_m2 = lax.optimization_barrier((first, second, for_2, for_m2))
    score, for_2, for_y = call(visitor_body, 3, rows, own, b2, first, second, score, for_2)

    b4, score, for_2, for_m2, for_y = lax.optimization_barrier((b4, score, for_2, for_m2, for_y))
    even = is_even.astype(jnp.int32)[None]
    for_m2, for_4, for_y = call(
        late_body, 3, rows, even, bm2, b4, first, second, for_m2, for_y
    )
    back_4 = push(for_4)
    back_y = swap(for_y)
    m2_back = pull(for_m2 + jnp.where(is_even, 0.0, back_y))
    back_4, back_y, for_2 = lax.optimization_barrier((back_4, back_y, for_2))
    back_2 = push(for_2 + jnp.where(is_even, back_y, 0.0) + back_4)
    return (score + m2_back + back_2).T


def solution(mesh):
    placed = (P("blk", None), P("blk"))
    return jax.shard_map(
        on_device, mesh=mesh, in_specs=placed, out_specs=P("blk", None), check_vma=False
    )
```

time: 280 us -> 138 us (0.49)
  waiting for transfers between devices: 188 us -> 48.6 us
  Pallas kernels: 0 us -> 34.7 us
  matrix products: 25.7 us -> 0 us
  starting transfers between devices: 62.3 us -> 42 us
  local copies, waits for them, and re-layouts: 0.01 us -> 4.97 us
  other arithmetic: 2.65 us -> 7.26 us
    ppermute x18 -> x9, waiting for transfers between devices: 188 us -> 48.6 us  [the longest x3 25 us: pull(): return lax.ppermute(value, 'blk', even_odd(n, -2, 2))]
    pallas_call x0 -> x5, Pallas kernels: none -> 34.7 us  [call(): pl.pallas_call(body, out_shape=[shape] * outs, in_specs=[smem if a.ndim =...]
    dot_general x20 -> x0, matrix products: 25.7 us -> none  [the longest x7 19.5 us: kernel_tile(): lax.dot_general(left, right, (((1,), (1,)), ((), ())), precision=lax.Prec...]
    ppermute x18 -> x9, starting transfers between devices: 62.3 us -> 42 us  [the longest x3 29.8 us: pull(): return lax.ppermute(value, 'blk', even_odd(n, -2, 2))]
    select_n x0 -> x2, other arithmetic: none -> 4.66 us  [the longest x1 2.51 us: on_device(): first = swap(jnp.where(is_even, b2[:cut], bm2[:cut]))]
    unnamed x4 -> x16, local copies, waits for them, and re-layouts: 0.01 us -> 3.92 us
  transfers between devices with their start and end apart: 18 -> 9, of which waited for: 12 -> 3; matrix products, arithmetic and copies ran while one was open for 10% -> 4% of each run, Pallas kernels for 0% -> 17%
where the time goes in v1:
time: 138 us
  waiting for transfers between devices  48.6 us (35%)
  starting transfers between devices  42 us (30%)
  Pallas kernels  34.7 us (25%)
  other arithmetic  7.26 us (5%)
  local copies, waits for them, and re-layouts  4.97 us (4%)
    pallas_call x5, Pallas kernels, call(): pl.pallas_call(body, out_shape=[shape] * outs, in_specs=[smem if a.ndim =...  34.7 us
    ppermute x3, starting transfers between devices, pull(): return lax.ppermute(value, 'blk', even_odd(n, -2, 2))  29.8 us
    ppermute x3, waiting for transfers between devices, pull(): return lax.ppermute(value, 'blk', even_odd(n, -2, 2))  25 us
    ppermute x3, waiting for transfers between devices, push(): return lax.ppermute(value, 'blk', even_odd(n, 2, -2))  23.6 us
    ppermute x3, starting transfers between devices, swap(): return lax.ppermute(value, 'blk', even_odd(n, 1, -1))  6.41 us
    ppermute x3, starting transfers between devices, push(): return lax.ppermute(value, 'blk', even_odd(n, 2, -2))  5.75 us
    unnamed x16, local copies, waits for them, and re-layouts  3.92 us
  transfers between devices with their start and end apart: 9, of which 3 were waited for; matrix products, arithmetic and copies ran while one was open for 4% of the time, Pallas kernels for 17%

profile of v1, /device:TPU:0, one launch (start us, length us, event | category | flops | bytes accessed | tf_op | source)
XLA Modules:
  0.0 137.8 jit_solution(9152835794467997388)
XLA Ops:
  0.7 1.5 %select_maximum_fusion.own_ref.left_ref = f32[520,768]{1,0:T(8,128)S(1)} fusion(f32[1,512]{1,0:T(1,128)S(1)} %bitcast.4, f32[512,768]{1,0:T(8,128)} %param.2), kind=kLoop, calls=%fused_computation | loop fusion | flops 1198080 | bytes 3172352 | tf_op jit(solution)/shard_map/concatenate | solution.py:145
  2.2 10.7 %collective-permute-start = (f32[520,768]{1,0:T(8,128)S(1)}, f32[520,768]{1,0:T(8,128)S(1)}, u32[]{:S(2)}, u32[]{:S(2)}) collective-permute-start(f32[520,768]{1,0:T(8,128)S(1)} %select_maximum_fusion.own_ref.left_ref), channel_id=1, source_target_pairs={{0,510},{1,3},{2,0},{3,5},{4,2},{5,7},{6,4},{7,9},{8,6},{9,11},{10... | collective-permute-start | bytes 4792328 | tf_op jit(solution)/shard_map/ppermute | solution.py:18
  12.9 3.0 %shard_map.28.left_in = f32[256,512]{1,0:T(8,128)S(1)} custom-call(f32[520,768]{1,0:T(8,128)S(1)} %select_maximum_fusion.own_ref.left_ref), custom_call_target="tpu_custom_call" | custom-call | flops 1000 | bytes 1000 | tf_op jit(solution)/shard_map/pallas_call | solution.py:129
  16.7 1.9 %collective-permute-start.2 = (f32[520,768]{1,0:T(8,128)S(1)}, f32[520,768]{1,0:T(8,128)}, u32[]{:S(2)}, u32[]{:S(2)}) collective-permute-start(f32[520,768]{1,0:T(8,128)S(1)} %select_maximum_fusion.own_ref.left_ref), channel_id=1, source_target_pairs={{0,2},{1,511},{2,4},{3,1},{4,6},{5,3},{6,8},{7,5},{8,10},{9,7},{10... | collective-permute-start | bytes 4792328 | tf_op jit(solution)/shard_map/ppermute | solution.py:23
  18.6 25.0 %collective-permute-done.right_ref.b2_ref = f32[520,768]{1,0:T(8,128)S(1)} collective-permute-done((f32[520,768]{1,0:T(8,128)S(1)}, f32[520,768]{1,0:T(8,128)S(1)}, u32[]{:S(2)}, u32[]{:S(2)}) %collective-permute-start) | collective-permute-done | bytes 1597472 | tf_op jit(solution)/shard_map/ppermute | solution.py:18
  43.5 9.8 %collective-permute-start.1 = (f32[520,768]{1,0:T(8,128)S(1)}, f32[520,768]{1,0:T(8,128)}, u32[]{:S(2)}, u32[]{:S(2)}) collective-permute-start(f32[520,768]{1,0:T(8,128)S(1)} %collective-permute-done.right_ref.b2_ref), channel_id=1, source_target_pairs={{0,510},{1,3},{2,0},{3,5},{4,2},{5,7},{6,4},{7,9},{8,6},{9,11},{10... | collective-permute-start | bytes 4792328 | tf_op jit(solution)/shard_map/ppermute | solution.py:18
  53.4 1.0 copy-done.3
  54.5 3.3 %shard_map.29 = (f32[256,512]{1,0:T(8,128)S(1)}, f32[256,512]{1,0:T(8,128)S(1)}) custom-call(f32[520,768]{1,0:T(8,128)S(1)} %select_maximum_fusion.own_ref.left_ref, f32[520,768]{1,0:T(8,128)S(1)} %collective-permute-done.right_ref.b2_ref, f32[256,512]{1,0:T(8,128)S(1)} %copy-done.3, f32[256,512]{1,0:T(8,128)S(1)} %broadcast_in_dim.16.right_in.left_in), custom_call_target="tpu_custom_call" | custom-call | flops 1000 | bytes 1000 | tf_op jit(solution)/shard_map/pallas_call | solution.py:129
  57.8 2.5 %slice_select_fusion = f32[264,768]{1,0:T(8,128)} fusion(f32[520,768]{1,0:T(8,128)S(1)} %collective-permute-done.right_ref.b2_ref, f32[520,768]{1,0:T(8,128)} %collective-permute-done.2.left_ref.bm2_ref, pred[]{:T(512)S(6)} %eq.5), kind=kLoop, calls=%fused_computation.2 | loop fusion | flops 202752 | bytes 2433025 | tf_op jit(solution)/shard_map/jit(_where)/select_n | solution.py:156
  60.3 1.9 %collective-permute-start.3 = (f32[264,768]{1,0:T(8,128)}, f32[264,768]{1,0:T(8,128)}, u32[]{:S(2)}, u32[]{:S(2)}) collective-permute-start(f32[264,768]{1,0:T(8,128)} %slice_select_fusion), channel_id=1, source_target_pairs={{0,1},{1,0},{2,3},{3,2},{4,5},{5,4},{6,7},{7,6},{8,9},{9,8},{10,11... | collective-permute-start | bytes 2433032 | tf_op jit(solution)/shard_map/ppermute | solution.py:28
  62.2 2.2 %slice_select_fusion.1 = f32[256,768]{1,0:T(8,128)} fusion(f32[520,768]{1,0:T(8,128)S(1)} %collective-permute-done.right_ref.b2_ref, f32[520,768]{1,0:T(8,128)} %collective-permute-done.2.left_ref.bm2_ref, pred[]{:T(512)S(6)} %eq.5), kind=kLoop, calls=%fused_computation.3 | loop fusion | flops 196608 | bytes 2359297 | tf_op jit(solution)/shard_map/jit(_where)/select_n | solution.py:157
  64.4 2.6 %collective-permute-start.4 = (f32[256,768]{1,0:T(8,128)}, f32[256,768]{1,0:T(8,128)}, u32[]{:S(2)}, u32[]{:S(2)}) collective-permute-start(f32[256,768]{1,0:T(8,128)} %slice_select_fusion.1), channel_id=1, source_target_pairs={{0,1},{1,0},{2,3},{3,2},{4,5},{5,4},{6,7},{7,6},{8,9},{9,8},{10,11... | collective-permute-start | bytes 2359304 | tf_op jit(solution)/shard_map/ppermute | solution.py:28
  67.0 1.0 copy-done.1
  68.0 1.0 copy-done.7
  69.0 4.8 %shard_map.30 = (f32[256,512]{1,0:T(8,128)S(1)}, f32[256,512]{1,0:T(8,128)S(1)}) custom-call(f32[520,768]{1,0:T(8,128)} %collective-permute-done.2.left_ref.bm2_ref, f32[520,768]{1,0:T(8,128)S(1)} %collective-permute-done.right_ref.b2_ref, f32[256,512]{1,0:T(8,128)S(1)} %copy-done.1, f32[256,512]{1,0:T(8,128)S(1)} %copy-done.7), custom_call_target="tpu_custom_call" | custom-call | flops 1000 | bytes 1000 | tf_op jit(solution)/shard_map/pallas_call | solution.py:129
  73.8 12.3 %shard_map.31 = (f32[256,512]{1,0:T(8,128)S(1)}, f32[256,512]{1,0:T(8,128)S(1)}, f32[256,512]{1,0:T(8,128)S(1)}) custom-call(f32[520,768]{1,0:T(8,128)S(1)} %select_maximum_fusion.own_ref.left_ref, f32[520,768]{1,0:T(8,128)S(1)} %collective-permute-done.right_ref.b2_ref, f32[264,768]{1,0:T(8,128)} %collective-permute-done.3.first_ref, ...), custom_call_target="tpu_custom_call" | custom-call | flops 1000 | bytes 1000 | tf_op jit(solution)/shard_map/pallas_call | solution.py:129
  86.2 11.4 %shard_map.32 = (f32[256,512]{1,0:T(8,128)S(1)}, f32[256,512]{1,0:T(8,128)S(1)}, f32[256,512]{1,0:T(8,128)S(1)}) custom-call(s32[1]{0:T(128)} %bitcast.1.even_ref, f32[520,768]{1,0:T(8,128)} %collective-permute-done.2.left_ref.bm2_ref, f32[520,768]{1,0:T(8,128)} %collective-permute-done.1.b4_ref, f32[264,768]{1,0:T(8,128)} %collective-permute-done.3.first_ref, ...), custom_call_target="tpu_custom_call" | custom-call | flops 1000 | bytes 1000 | tf_op jit(solution)/shard_map/pallas_call | solution.py:129
  97.6 1.9 %collective-permute-start.5 = (f32[256,512]{1,0:T(8,128)S(1)}, f32[256,512]{1,0:T(8,128)S(1)}, u32[]{:S(2)}, u32[]{:S(2)}) collective-permute-start(f32[256,512]{1,0:T(8,128)S(1)} %get-tuple-element.53), channel_id=1, source_target_pairs={{0,1},{1,0},{2,3},{3,2},{4,5},{5,4},{6,7},{7,6},{8,9},{9,8},{10,11... | collective-permute-start | bytes 1572872 | tf_op jit(solution)/shard_map/ppermute | solution.py:28
  99.5 1.9 %collective-permute-start.7 = (f32[256,512]{1,0:T(8,128)S(1)}, f32[256,512]{1,0:T(8,128)S(1)}, u32[]{:S(2)}, u32[]{:S(2)}) collective-permute-start(f32[256,512]{1,0:T(8,128)S(1)} %get-tuple-element.54), channel_id=1, source_target_pairs={{0,2},{1,511},{2,4},{3,1},{4,6},{5,3},{6,8},{7,5},{8,10},{9,7},{10... | collective-permute-start | bytes 1572872 | tf_op jit(solution)/shard_map/ppermute | solution.py:23
  101.6 9.4 %collective-permute-start.6 = (f32[256,512]{1,0:T(8,128)S(1)}, f32[256,512]{1,0:T(8,128)S(1)}, u32[]{:S(2)}, u32[]{:S(2)}) collective-permute-start(f32[256,512]{1,0:T(8,128)S(1)} %select_add_fusion), channel_id=1, source_target_pairs={{0,510},{1,3},{2,0},{3,5},{4,2},{5,7},{6,4},{7,9},{8,6},{9,11},{10... | collective-permute-start | bytes 1572872 | tf_op jit(solution)/shard_map/ppermute | solution.py:18
  110.9 9.1 %collective-permute-done.7 = f32[256,512]{1,0:T(8,128)S(1)} collective-permute-done((f32[256,512]{1,0:T(8,128)S(1)}, f32[256,512]{1,0:T(8,128)S(1)}, u32[]{:S(2)}, u32[]{:S(2)}) %collective-permute-start.7) | collective-permute-done | bytes 524320 | tf_op jit(solution)/shard_map/ppermute | solution.py:23
  120.2 1.9 %collective-permute-start.8 = (f32[256,512]{1,0:T(8,128)S(1)}, f32[256,512]{1,0:T(8,128)S(1)}, u32[]{:S(2)}, u32[]{:S(2)}) collective-permute-start(f32[256,512]{1,0:T(8,128)S(1)} %add_add_fusion), channel_id=1, source_target_pairs={{0,2},{1,511},{2,4},{3,1},{4,6},{5,3},{6,8},{7,5},{8,10},{9,7},{10... | collective-permute-start | bytes 1572872 | tf_op jit(solution)/shard_map/ppermute | solution.py:23
  122.1 14.6 %collective-permute-done.8 = f32[256,512]{1,0:T(8,128)S(1)} collective-permute-done((f32[256,512]{1,0:T(8,128)S(1)}, f32[256,512]{1,0:T(8,128)S(1)}, u32[]{:S(2)}, u32[]{:S(2)}) %collective-permute-start.8) | collective-permute-done | bytes 524320 | tf_op jit(solution)/shard_map/ppermute | solution.py:23
  136.8 1.0 copy.3
  (24 shorter events, 2.0 us)
Async XLA Ops:
  2.2 41.3 %collective-permute-start = (f32[520,768]{1,0:T(8,128)S(1)}, f32[520,768]{1,0:T(8,128)S(1)}, u32[]{:S(2)}, u32[]{:S(2)}) collective-permute-start(f32[520,768]{1,0:T(8,128)S(1)} %select_maximum_fusion.own_ref.left_ref), channel_id=1, source_target_pairs={{0,510},{1,3},{2,0},{3,5},{4,2},{5,7},{6,4},{7,9},{8,6},{9,11},{10... | collective-permute-start | bytes 4792328 | tf_op jit(solution)/shard_map/ppermute | solution.py:18
  15.9 0.8 copy-start.2
  16.7 41.1 %collective-permute-start.2 = (f32[520,768]{1,0:T(8,128)S(1)}, f32[520,768]{1,0:T(8,128)}, u32[]{:S(2)}, u32[]{:S(2)}) collective-permute-start(f32[520,768]{1,0:T(8,128)S(1)} %select_maximum_fusion.own_ref.left_ref), channel_id=1, source_target_pairs={{0,2},{1,511},{2,4},{3,1},{4,6},{5,3},{6,8},{7,5},{8,10},{9,7},{10... | collective-permute-start | bytes 4792328 | tf_op jit(solution)/shard_map/ppermute | solution.py:23
  43.5 42.6 %collective-permute-start.1 = (f32[520,768]{1,0:T(8,128)S(1)}, f32[520,768]{1,0:T(8,128)}, u32[]{:S(2)}, u32[]{:S(2)}) collective-permute-start(f32[520,768]{1,0:T(8,128)S(1)} %collective-permute-done.right_ref.b2_ref), channel_id=1, source_target_pairs={{0,510},{1,3},{2,0},{3,5},{4,2},{5,7},{6,4},{7,9},{8,6},{9,11},{10... | collective-permute-start | bytes 4792328 | tf_op jit(solution)/shard_map/ppermute | solution.py:18
  53.4 1.0 copy-start.3
  54.5 3.3 %copy-start = (f32[256,512]{1,0:T(8,128)}, f32[256,512]{1,0:T(8,128)S(1)}, u32[]{:S(2)}) copy-start(f32[256,512]{1,0:T(8,128)S(1)} %broadcast_in_dim.16.right_in.left_in) | copy-start | bytes 1572868
  57.8 6.6 %copy-start.4 = (f32[256,512]{1,0:T(8,128)}, f32[256,512]{1,0:T(8,128)S(1)}, u32[]{:S(2)}) copy-start(f32[256,512]{1,0:T(8,128)S(1)} %get-tuple-element.42.own_in) | copy-start | bytes 1572868
  57.8 6.6 %copy-start.6 = (f32[256,512]{1,0:T(8,128)}, f32[256,512]{1,0:T(8,128)S(1)}, u32[]{:S(2)}) copy-start(f32[256,512]{1,0:T(8,128)S(1)} %get-tuple-element.37.right_in) | copy-start | bytes 1572868
  60.3 13.5 %collective-permute-start.3 = (f32[264,768]{1,0:T(8,128)}, f32[264,768]{1,0:T(8,128)}, u32[]{:S(2)}, u32[]{:S(2)}) collective-permute-start(f32[264,768]{1,0:T(8,128)} %slice_select_fusion), channel_id=1, source_target_pairs={{0,1},{1,0},{2,3},{3,2},{4,5},{5,4},{6,7},{7,6},{8,9},{9,8},{10,11... | collective-permute-start | bytes 2433032 | tf_op jit(solution)/shard_map/ppermute | solution.py:28
  64.4 9.5 %collective-permute-start.4 = (f32[256,768]{1,0:T(8,128)}, f32[256,768]{1,0:T(8,128)}, u32[]{:S(2)}, u32[]{:S(2)}) collective-permute-start(f32[256,768]{1,0:T(8,128)} %slice_select_fusion.1), channel_id=1, source_target_pairs={{0,1},{1,0},{2,3},{3,2},{4,5},{5,4},{6,7},{7,6},{8,9},{9,8},{10,11... | collective-permute-start | bytes 2359304 | tf_op jit(solution)/shard_map/ppermute | solution.py:28
  67.0 1.0 copy-start.1
  68.0 1.0 copy-start.7
  69.0 4.8 %copy-start.5 = (f32[256,512]{1,0:T(8,128)S(1)}, f32[256,512]{1,0:T(8,128)}, u32[]{:S(2)}) copy-start(f32[256,512]{1,0:T(8,128)} %copy-done.4) | copy-start | bytes 1572868
  97.6 3.9 %collective-permute-start.5 = (f32[256,512]{1,0:T(8,128)S(1)}, f32[256,512]{1,0:T(8,128)S(1)}, u32[]{:S(2)}, u32[]{:S(2)}) collective-permute-start(f32[256,512]{1,0:T(8,128)S(1)} %get-tuple-element.53), channel_id=1, source_target_pairs={{0,1},{1,0},{2,3},{3,2},{4,5},{5,4},{6,7},{7,6},{8,9},{9,8},{10,11... | collective-permute-start | bytes 1572872 | tf_op jit(solution)/shard_map/ppermute | solution.py:28
  99.5 20.5 %collective-permute-start.7 = (f32[256,512]{1,0:T(8,128)S(1)}, f32[256,512]{1,0:T(8,128)S(1)}, u32[]{:S(2)}, u32[]{:S(2)}) collective-permute-start(f32[256,512]{1,0:T(8,128)S(1)} %get-tuple-element.54), channel_id=1, source_target_pairs={{0,2},{1,511},{2,4},{3,1},{4,6},{5,3},{6,8},{7,5},{8,10},{9,7},{10... | collective-permute-start | bytes 1572872 | tf_op jit(solution)/shard_map/ppermute | solution.py:23
  101.6 20.5 %collective-permute-start.6 = (f32[256,512]{1,0:T(8,128)S(1)}, f32[256,512]{1,0:T(8,128)S(1)}, u32[]{:S(2)}, u32[]{:S(2)}) collective-permute-start(f32[256,512]{1,0:T(8,128)S(1)} %select_add_fusion), channel_id=1, source_target_pairs={{0,510},{1,3},{2,0},{3,5},{4,2},{5,7},{6,4},{7,9},{8,6},{9,11},{10... | collective-permute-start | bytes 1572872 | tf_op jit(solution)/shard_map/ppermute | solution.py:18
  120.2 16.5 %collective-permute-start.8 = (f32[256,512]{1,0:T(8,128)S(1)}, f32[256,512]{1,0:T(8,128)S(1)}, u32[]{:S(2)}, u32[]{:S(2)}) collective-permute-start(f32[256,512]{1,0:T(8,128)S(1)} %add_add_fusion), channel_id=1, source_target_pairs={{0,2},{1,511},{2,4},{3,1},{4,6},{5,3},{6,8},{7,5},{8,10},{9,7},{10... | collective-permute-start | bytes 1572872 | tf_op jit(solution)/shard_map/ppermute | solution.py:23

commit v2 on v1

v2 whole, which is shorter than its diff:
```python
import jax
import jax.numpy as jnp
from jax import lax
from jax.experimental import pallas as pl
from jax.experimental.pallas import tpu as pltpu
from jax.sharding import PartitionSpec as P

CLUSTERS = 256
TOP = 8
END = 8


def even_odd(n, even, odd):
    return [(i, (i + (even if i % 2 == 0 else odd)) % n) for i in range(n)]


def pull(value):
    n = lax.axis_size("blk")
    return lax.ppermute(value, "blk", even_odd(n, -2, 2))


def push(value):
    n = lax.axis_size("blk")
    return lax.ppermute(value, "blk", even_odd(n, 2, -2))


def swap(value):
    n = lax.axis_size("blk")
    return lax.ppermute(value, "blk", even_odd(n, 1, -1))


def give(value, core):
    n = lax.axis_size("blk")
    return lax.ppermute(value, "blk", [(i, i ^ 1) for i in range(core, n, 2)])


def one_hot(labels):
    cluster = lax.broadcasted_iota(jnp.int32, (CLUSTERS, labels.shape[1]), 0)
    return jnp.where(cluster == labels.astype(jnp.int32), 1.0, 0.0).astype(jnp.bfloat16)


def unpack(message):
    rows = (message.shape[0] - TOP) // 128 * 128
    return message[TOP : TOP + rows, :], one_hot(message[0:1, :rows])


def pack_body(embeddings_ref, labels_ref, message_ref, held, done):
    rows = embeddings_ref.shape[0]
    copy = pltpu.make_async_copy(embeddings_ref, message_ref.at[pl.ds(TOP, rows)], done.at[0])
    copy.start()
    labels = pltpu.make_async_copy(labels_ref, held, done.at[1])
    labels.start()
    message_ref[:TOP, :] = jnp.zeros((TOP, message_ref.shape[1]), jnp.float32)
    message_ref[TOP + rows :, :] = jnp.zeros((END, message_ref.shape[1]), jnp.float32)
    labels.wait()
    message_ref[0:1, :rows] = held[...].astype(jnp.float32)
    copy.wait()


def pack(embeddings, labels):
    rows, dim = embeddings.shape
    return pl.pallas_call(
        pack_body,
        out_shape=pltpu.VMEM((TOP + rows + END, dim), jnp.float32),
        in_specs=[pl.BlockSpec(memory_space=pltpu.HBM)] * 2,
        out_specs=pl.BlockSpec(memory_space=pltpu.VMEM),
        scratch_shapes=[pltpu.VMEM((1, rows), jnp.int32), pltpu.SemaphoreType.DMA((2,))],
        compiler_params=pltpu.CompilerParams(vmem_limit_bytes=16 * 2**20),
    )(
        pltpu.with_memory_space_constraint(embeddings, pltpu.HBM),
        pltpu.with_memory_space_constraint(labels[None, :], pltpu.HBM),
    )


def kernel_tile(left, right):
    left_norms = jnp.sum(left * left, axis=1, keepdims=True)
    right_norms = jnp.sum(right * right, axis=1, keepdims=True)
    right_norms = jnp.transpose(jnp.broadcast_to(right_norms, (right.shape[0], 128)))[0:1, :]
    inner = lax.dot_general(
        left,
        right,
        (((1,), (1,)), ((), ())),
        precision=lax.Precision.HIGHEST,
        preferred_element_type=jnp.float32,
    )
    return jnp.exp(-(left_norms + right_norms - 2.0 * inner)).astype(jnp.bfloat16)


def left_sums(right_hot, kernel):
    return lax.dot_general(
        right_hot, kernel, (((1,), (1,)), ((), ())), preferred_element_type=jnp.float32
    )


def right_sums(left_hot, kernel):
    return jnp.dot(left_hot, kernel, preferred_element_type=jnp.float32)


def self_body(own_ref, own_in, own_out):
    own, own_hot = unpack(own_ref)
    own_out[...] = own_in[...] + left_sums(own_hot, kernel_tile(own, own))


def pair_body(left_ref, right_ref, left_in, right_in, left_out, right_out):
    left, left_hot = unpack(left_ref)
    right, right_hot = unpack(right_ref)
    kernel = kernel_tile(left, right)
    left_out[...] = left_in[...] + left_sums(right_hot, kernel)
    right_out[...] = right_in[...] + right_sums(left_hot, kernel)


def visitor(even_y_ref, odd_y_ref):
    return unpack(even_y_ref[...] + odd_y_ref[...])


def visitor_body(
    even_ref, own_ref, bm2_ref, b2_ref, even_y_ref, odd_y_ref, own_in, for_m2_in, for_2_in,
    own_out, for_m2_out, for_2_out, for_y_out,
):
    y, y_hot = visitor(even_y_ref, odd_y_ref)
    own, own_hot = unpack(own_ref)
    kernel = kernel_tile(own, y)
    own_out[...] = own_in[...] + left_sums(y_hot, kernel)
    for_y_out[...] = right_sums(own_hot, kernel)
    b2, b2_hot = unpack(b2_ref)
    kernel = kernel_tile(b2, y)
    for_2_out[...] = for_2_in[...] + left_sums(y_hot, kernel)
    for_y_out[...] += right_sums(b2_hot, kernel)
    for_m2_out[...] = for_m2_in[...]

    @pl.when(even_ref[0] == 1)
    def _():
        bm2, bm2_hot = unpack(bm2_ref)
        kernel = kernel_tile(bm2, y)
        for_m2_out[...] += left_sums(y_hot, kernel)
        for_y_out[...] += right_sums(bm2_hot, kernel)


def late_body(
    even_ref, bm2_ref, b4_ref, even_y_ref, odd_y_ref, for_m2_in, for_y_in,
    for_m2_out, for_4_out, for_y_out,
):
    b4, b4_hot = unpack(b4_ref)
    bm2, bm2_hot = unpack(bm2_ref)
    kernel = kernel_tile(bm2, b4)
    for_m2_out[...] = for_m2_in[...] + left_sums(b4_hot, kernel)
    for_4_out[...] = right_sums(bm2_hot, kernel)
    for_y_out[...] = for_y_in[...]

    @pl.when(even_ref[0] == 0)
    def _():
        y, y_hot = visitor(even_y_ref, odd_y_ref)
        kernel = kernel_tile(b4, y)
        for_4_out[...] += left_sums(y_hot, kernel)
        for_y_out[...] += right_sums(b4_hot, kernel)


def call(body, outs, *args, flops=1000):
    rows = args[-1].shape[1]
    vmem = pl.BlockSpec(memory_space=pltpu.VMEM)
    smem = pl.BlockSpec(memory_space=pltpu.SMEM)
    return pl.pallas_call(
        body,
        out_shape=[pltpu.VMEM((CLUSTERS, rows), jnp.float32)] * outs,
        in_specs=[smem if a.ndim == 1 else vmem for a in args],
        out_specs=[vmem] * outs,
        compiler_params=pltpu.CompilerParams(vmem_limit_bytes=16 * 2**20),
        cost_estimate=pl.CostEstimate(flops=flops, bytes_accessed=1000, transcendentals=0),
    )(*(a if a.ndim == 1 else pltpu.with_memory_space_constraint(a, pltpu.VMEM) for a in args))


def on_device(embeddings, labels):
    rows = embeddings.shape[0]
    is_even = lax.axis_index("blk") % 2 == 0
    even = is_even.astype(jnp.int32)[None]
    zero = jnp.zeros((CLUSTERS, rows), jnp.float32)
    own = pack(embeddings, labels)

    b2 = pull(own)
    bm2 = push(own[: TOP + rows])
    (score,) = call(self_body, 1, own, zero)
    b2, score = lax.optimization_barrier((b2, score))
    b4 = pull(b2)

    score, for_2 = call(pair_body, 2, own, b2, score, zero)
    b2, score, for_2 = lax.optimization_barrier((b2, score, for_2))
    even_y = give(b2[: TOP + rows], 0)
    bm2, score, for_2 = lax.optimization_barrier((bm2, score, for_2))
    odd_y = give(bm2, 1)
    for_m2, for_2 = call(pair_body, 2, bm2, b2, zero, for_2)

    even_y, odd_y, for_2, for_m2 = lax.optimization_barrier((even_y, odd_y, for_2, for_m2))
    score, for_m2, for_2, for_y = call(
        visitor_body, 4, even, own, bm2, b2, even_y, odd_y, score, for_m2, for_2
    )
    back_m2 = give(for_y, 0)

    b4, score, for_2, for_m2, for_y = lax.optimization_barrier((b4, score, for_2, for_m2, for_y))
    for_m2, for_4, for_y = call(
        late_body, 3, even, bm2, b4, even_y, odd_y, for_m2, for_y, flops=12 * rows * rows * 768
    )
    back_4 = push(for_4)
    home_m2 = pull(for_m2 + back_m2)
    back_2 = give(for_y, 1)
    home_2 = push(for_2 + back_2 + back_4)
    return (score + home_m2 + home_2).T


def solution(mesh):
    placed = (P("blk", None), P("blk"))
    return jax.shard_map(
        on_device, mesh=mesh, in_specs=placed, out_specs=P("blk", None), check_vma=False
    )
```

time: 138 us -> 130 us (0.942)
  other arithmetic: 7.26 us -> 0.37 us
  Pallas kernels: 34.7 us -> 30.3 us
  waiting for transfers between devices: 48.6 us -> 51.8 us
    ppermute x3, waiting for transfers between devices: 25 us -> 29.8 us  [pull(): return lax.ppermute(value, 'blk', even_odd(n, -2, 2))]
    select_n x2 -> x0, other arithmetic: 4.66 us -> none  [the longest x1 2.51 us: on_device(): first = swap(jnp.where(is_even, b2[:cut], bm2[:cut]))]
    pallas_call x5 -> x6, Pallas kernels: 34.7 us -> 30.3 us  [the longest x5 28.8 us: call(): pl.pallas_call(body, out_shape=[pltpu.VMEM((CLUSTERS, rows), jnp.float32)...]
    ppermute x3, waiting for transfers between devices: 23.6 us -> 22 us  [push(): return lax.ppermute(value, 'blk', even_odd(n, 2, -2))]
    unnamed x16 -> x12, local copies, waits for them, and re-layouts: 3.92 us -> 2.27 us
    concatenate x1 -> x0, other arithmetic: 1.51 us -> none  [on_device(): own = jnp.concatenate([top, embeddings], axis=0)]
    slice x0 -> x2, local copies, waits for them, and re-layouts: none -> 1.47 us  [the longest x1 1.37 us: on_device(): even_y = give(b2[:TOP + rows], 0)]
    ppermute x3 -> x4, starting transfers between devices: 6.41 us -> 6.77 us  [give(): return lax.ppermute(value, 'blk', [(i, i ^ 1) for i in range(core, n, 2)])]
  transfers between devices with their start and end apart: 9 -> 10, of which waited for: 3 -> 3; matrix products, arithmetic and copies ran while one was open for 4% -> 1% of each run, Pallas kernels for 17% -> 22%
where the time goes in v2:
time: 130 us
  waiting for transfers between devices  51.8 us (40%)
  starting transfers between devices  42.4 us (33%)
  Pallas kernels  30.3 us (23%)
  local copies, waits for them, and re-layouts  4.79 us (4%)
    ppermute x3, starting transfers between devices, pull(): return lax.ppermute(value, 'blk', even_odd(n, -2, 2))  29.8 us
    ppermute x3, waiting for transfers between devices, pull(): return lax.ppermute(value, 'blk', even_odd(n, -2, 2))  29.8 us
    pallas_call x5, Pallas kernels, call(): pl.pallas_call(body, out_shape=[pltpu.VMEM((CLUSTERS, rows), jnp.float32)...  28.8 us
    ppermute x3, waiting for transfers between devices, push(): return lax.ppermute(value, 'blk', even_odd(n, 2, -2))  22 us
    ppermute x4, starting transfers between devices, give(): return lax.ppermute(value, 'blk', [(i, i ^ 1) for i in range(core, n, 2)])  6.77 us
    ppermute x3, starting transfers between devices, push(): return lax.ppermute(value, 'blk', even_odd(n, 2, -2))  5.76 us
  transfers between devices with their start and end apart: 10, of which 3 were waited for; matrix products, arithmetic and copies ran while one was open for 1% of the time, Pallas kernels for 22%

profile of v2, /device:TPU:0, one launch (start us, length us, event | category | flops | bytes accessed | tf_op | source)
XLA Modules:
  0.0 129.8 jit_solution(10187094156472353062)
XLA Ops:
  0.0 1.4 %shard_map.28.own_ref.left_ref = f32[528,768]{1,0:T(8,128)S(1)} custom-call(f32[512,768]{1,0:T(8,128)} %embeddings_ref.1, s32[1,512]{1,0:T(1,128)} %bitcast.4), custom_call_target="tpu_custom_call" | custom-call | tf_op jit(solution)/shard_map/pallas_call | solution.py:62
  1.4 10.7 %collective-permute-start = (f32[528,768]{1,0:T(8,128)S(1)}, f32[528,768]{1,0:T(8,128)S(1)}, u32[]{:S(2)}, u32[]{:S(2)}) collective-permute-start(f32[528,768]{1,0:T(8,128)S(1)} %shard_map.28.own_ref.left_ref), channel_id=1, source_target_pairs={{0,510},{1,3},{2,0},{3,5},{4,2},{5,7},{6,4},{7,9},{8,6},{9,11},{10... | collective-permute-start | bytes 4866056 | tf_op jit(solution)/shard_map/ppermute | solution.py:19
  12.2 1.9 %collective-permute-start.2 = (f32[520,768]{1,0:T(8,128)S(1)}, f32[520,768]{1,0:T(8,128)}, u32[]{:S(2)}, u32[]{:S(2)}) collective-permute-start(f32[520,768]{1,0:T(8,128)S(1)} %slice.8), channel_id=1, source_target_pairs={{0,2},{1,511},{2,4},{3,1},{4,6},{5,3},{6,8},{7,5},{8,10},{9,7},{10... | collective-permute-start | bytes 4792328 | tf_op jit(solution)/shard_map/ppermute | solution.py:24
  14.2 3.0 %shard_map.29.left_in = f32[256,512]{1,0:T(8,128)S(1)} custom-call(f32[528,768]{1,0:T(8,128)S(1)} %shard_map.28.own_ref.left_ref, f32[256,512]{1,0:T(8,128)S(1)} %broadcast_in_dim.12.own_in.right_in.left_in), custom_call_target="tpu_custom_call" | custom-call | flops 1000 | bytes 1000 | tf_op jit(solution)/shard_map/pallas_call | solution.py:162
  17.2 29.8 %collective-permute-done.right_ref.b2_ref = f32[528,768]{1,0:T(8,128)S(1)} collective-permute-done((f32[528,768]{1,0:T(8,128)S(1)}, f32[528,768]{1,0:T(8,128)S(1)}, u32[]{:S(2)}, u32[]{:S(2)}) %collective-permute-start) | collective-permute-done | bytes 1622048 | tf_op jit(solution)/shard_map/ppermute | solution.py:19
  47.0 9.8 %collective-permute-start.1 = (f32[528,768]{1,0:T(8,128)S(1)}, f32[528,768]{1,0:T(8,128)}, u32[]{:S(2)}, u32[]{:S(2)}) collective-permute-start(f32[528,768]{1,0:T(8,128)S(1)} %collective-permute-done.right_ref.b2_ref), channel_id=1, source_target_pairs={{0,510},{1,3},{2,0},{3,5},{4,2},{5,7},{6,4},{7,9},{8,6},{9,11},{10... | collective-permute-start | bytes 4866056 | tf_op jit(solution)/shard_map/ppermute | solution.py:19
  56.9 3.2 %shard_map.30 = (f32[256,512]{1,0:T(8,128)S(1)}, f32[256,512]{1,0:T(8,128)S(1)}) custom-call(f32[528,768]{1,0:T(8,128)S(1)} %shard_map.28.own_ref.left_ref, f32[528,768]{1,0:T(8,128)S(1)} %collective-permute-done.right_ref.b2_ref, f32[256,512]{1,0:T(8,128)S(1)} %shard_map.29.left_in, f32[256,512]{1,0:T(8,128)S(1)} %broadcast_in_dim.12.own_in.right_in.left_in), custom_call_target="tpu_custom_call" | custom-call | flops 1000 | bytes 1000 | tf_op jit(solution)/shard_map/pallas_call | solution.py:162
  60.1 1.4 %slice.7 = f32[520,768]{1,0:T(8,128)} slice(f32[528,768]{1,0:T(8,128)S(1)} %collective-permute-done.right_ref.b2_ref), slice={[0:520], [0:768]} | slice | bytes 3194880 | tf_op jit(solution)/shard_map/slice | solution.py:187
  61.5 0.2 copy-done.4
  61.7 2.5 %collective-permute-start.3 = (f32[520,768]{1,0:T(8,128)}, f32[520,768]{1,0:T(8,128)}, u32[]{:S(2)}, u32[]{:S(2)}) collective-permute-start(f32[520,768]{1,0:T(8,128)} %slice.7), channel_id=1, source_target_pairs={{0,1},{2,3},{4,5},{6,7},{8,9},{10,11},{12,13},{14,15},{16,17},{18,... | collective-permute-start | bytes 4792328 | tf_op jit(solution)/shard_map/ppermute | solution.py:34
  64.2 1.5 %collective-permute-start.4 = (f32[520,768]{1,0:T(8,128)}, f32[520,768]{1,0:T(8,128)}, u32[]{:S(2)}, u32[]{:S(2)}) collective-permute-start(f32[520,768]{1,0:T(8,128)} %collective-permute-done.2.left_ref.bm2_ref), channel_id=1, source_target_pairs={{1,0},{3,2},{5,4},{7,6},{9,8},{11,10},{13,12},{15,14},{17,16},{19,... | collective-permute-start | bytes 4792328 | tf_op jit(solution)/shard_map/ppermute | solution.py:34
  65.6 1.0 copy-done.1
  66.7 1.0 copy-done.5
  67.7 4.7 %shard_map.31 = (f32[256,512]{1,0:T(8,128)S(1)}, f32[256,512]{1,0:T(8,128)S(1)}) custom-call(f32[520,768]{1,0:T(8,128)} %collective-permute-done.2.left_ref.bm2_ref, f32[528,768]{1,0:T(8,128)S(1)} %collective-permute-done.right_ref.b2_ref, f32[256,512]{1,0:T(8,128)S(1)} %copy-done.1, f32[256,512]{1,0:T(8,128)S(1)} %copy-done.5), custom_call_target="tpu_custom_call" | custom-call | flops 1000 | bytes 1000 | tf_op jit(solution)/shard_map/pallas_call | solution.py:162
  72.5 11.7 %shard_map.32 = (f32[256,512]{1,0:T(8,128)S(1)}, f32[256,512]{1,0:T(8,128)S(1)}, f32[256,512]{1,0:T(8,128)S(1)}, f32[256,512]{1,0:T(8,128)S(1)}) custom-call(s32[1]{0:T(128)} %bitcast.1.even_ref, f32[528,768]{1,0:T(8,128)S(1)} %shard_map.28.own_ref.left_ref, f32[520,768]{1,0:T(8,128)} %collective-permute-done.2.left_ref.bm2_ref, ...), custom_call_target="tpu_custom_call" | custom-call | flops 1000 | bytes 1000 | tf_op jit(solution)/shard_map/pallas_call | solution.py:162
  84.2 1.5 %collective-permute-start.5 = (f32[256,512]{1,0:T(8,128)S(1)}, f32[256,512]{1,0:T(8,128)S(1)}, u32[]{:S(2)}, u32[]{:S(2)}) collective-permute-start(f32[256,512]{1,0:T(8,128)S(1)} %get-tuple-element.56.for_y_in), channel_id=1, source_target_pairs={{0,1},{2,3},{4,5},{6,7},{8,9},{10,11},{12,13},{14,15},{16,17},{18,... | collective-permute-start | bytes 1572872 | tf_op jit(solution)/shard_map/ppermute | solution.py:34
  85.7 6.2 %shard_map.33 = (f32[256,512]{1,0:T(8,128)S(1)}, f32[256,512]{1,0:T(8,128)S(1)}, f32[256,512]{1,0:T(8,128)S(1)}) custom-call(s32[1]{0:T(128)} %bitcast.1.even_ref, f32[520,768]{1,0:T(8,128)} %collective-permute-done.2.left_ref.bm2_ref, f32[528,768]{1,0:T(8,128)} %collective-permute-done.1.b4_ref, f32[520,768]{1,0:T(8,128)} %collective-permute-done.3.even_y_ref, ...), custom_call_target="tpu_custom_call" | custom-call | flops 2415919104 | bytes 1000 | tf_op jit(solution)/shard_map/pallas_call | solution.py:162
  91.9 1.3 collective-permute-start.7
  93.2 1.9 %collective-permute-start.8 = (f32[256,512]{1,0:T(8,128)S(1)}, f32[256,512]{1,0:T(8,128)S(1)}, u32[]{:S(2)}, u32[]{:S(2)}) collective-permute-start(f32[256,512]{1,0:T(8,128)S(1)} %get-tuple-element.60), channel_id=1, source_target_pairs={{0,2},{1,511},{2,4},{3,1},{4,6},{5,3},{6,8},{7,5},{8,10},{9,7},{10... | collective-permute-start | bytes 1572872 | tf_op jit(solution)/shard_map/ppermute | solution.py:24
  95.3 9.4 %collective-permute-start.6 = (f32[256,512]{1,0:T(8,128)S(1)}, f32[256,512]{1,0:T(8,128)S(1)}, u32[]{:S(2)}, u32[]{:S(2)}) collective-permute-start(f32[256,512]{1,0:T(8,128)S(1)} %add.20), channel_id=1, source_target_pairs={{0,510},{1,3},{2,0},{3,5},{4,2},{5,7},{6,4},{7,9},{8,6},{9,11},{10... | collective-permute-start | bytes 1572872 | tf_op jit(solution)/shard_map/ppermute | solution.py:19
  104.6 7.4 %collective-permute-done.8 = f32[256,512]{1,0:T(8,128)S(1)} collective-permute-done((f32[256,512]{1,0:T(8,128)S(1)}, f32[256,512]{1,0:T(8,128)S(1)}, u32[]{:S(2)}, u32[]{:S(2)}) %collective-permute-start.8) | collective-permute-done | bytes 524320 | tf_op jit(solution)/shard_map/ppermute | solution.py:24
  112.2 1.9 %collective-permute-start.9 = (f32[256,512]{1,0:T(8,128)S(1)}, f32[256,512]{1,0:T(8,128)S(1)}, u32[]{:S(2)}, u32[]{:S(2)}) collective-permute-start(f32[256,512]{1,0:T(8,128)S(1)} %add_add_fusion), channel_id=1, source_target_pairs={{0,2},{1,511},{2,4},{3,1},{4,6},{5,3},{6,8},{7,5},{8,10},{9,7},{10... | collective-permute-start | bytes 1572872 | tf_op jit(solution)/shard_map/ppermute | solution.py:24
  114.1 14.6 %collective-permute-done.9 = f32[256,512]{1,0:T(8,128)S(1)} collective-permute-done((f32[256,512]{1,0:T(8,128)S(1)}, f32[256,512]{1,0:T(8,128)S(1)}, u32[]{:S(2)}, u32[]{:S(2)}) %collective-permute-start.9) | collective-permute-done | bytes 524320 | tf_op jit(solution)/shard_map/ppermute | solution.py:24
  128.8 1.0 copy.3
  (21 shorter events, 0.6 us)
Async XLA Ops:
  1.4 45.6 %collective-permute-start = (f32[528,768]{1,0:T(8,128)S(1)}, f32[528,768]{1,0:T(8,128)S(1)}, u32[]{:S(2)}, u32[]{:S(2)}) collective-permute-start(f32[528,768]{1,0:T(8,128)S(1)} %shard_map.28.own_ref.left_ref), channel_id=1, source_target_pairs={{0,510},{1,3},{2,0},{3,5},{4,2},{5,7},{6,4},{7,9},{8,6},{9,11},{10... | collective-permute-start | bytes 4866056 | tf_op jit(solution)/shard_map/ppermute | solution.py:19
  12.2 47.9 %collective-permute-start.2 = (f32[520,768]{1,0:T(8,128)S(1)}, f32[520,768]{1,0:T(8,128)}, u32[]{:S(2)}, u32[]{:S(2)}) collective-permute-start(f32[520,768]{1,0:T(8,128)S(1)} %slice.8), channel_id=1, source_target_pairs={{0,2},{1,511},{2,4},{3,1},{4,6},{5,3},{6,8},{7,5},{8,10},{9,7},{10... | collective-permute-start | bytes 4792328 | tf_op jit(solution)/shard_map/ppermute | solution.py:24
  14.2 45.9 %copy-start = (f32[256,512]{1,0:T(8,128)}, f32[256,512]{1,0:T(8,128)S(1)}, u32[]{:S(2)}) copy-start(f32[256,512]{1,0:T(8,128)S(1)} %broadcast_in_dim.12.own_in.right_in.left_in) | copy-start | bytes 1572868
  47.0 38.7 %collective-permute-start.1 = (f32[528,768]{1,0:T(8,128)S(1)}, f32[528,768]{1,0:T(8,128)}, u32[]{:S(2)}, u32[]{:S(2)}) collective-permute-start(f32[528,768]{1,0:T(8,128)S(1)} %collective-permute-done.right_ref.b2_ref), channel_id=1, source_target_pairs={{0,510},{1,3},{2,0},{3,5},{4,2},{5,7},{6,4},{7,9},{8,6},{9,11},{10... | collective-permute-start | bytes 4866056 | tf_op jit(solution)/shard_map/ppermute | solution.py:19
  60.1 1.4 %copy-start.2 = (f32[256,512]{1,0:T(8,128)}, f32[256,512]{1,0:T(8,128)S(1)}, u32[]{:S(2)}) copy-start(f32[256,512]{1,0:T(8,128)S(1)} %get-tuple-element.46.own_in) | copy-start | bytes 1572868
  60.1 1.6 %copy-start.4 = (f32[256,512]{1,0:T(8,128)}, f32[256,512]{1,0:T(8,128)S(1)}, u32[]{:S(2)}) copy-start(f32[256,512]{1,0:T(8,128)S(1)} %get-tuple-element.41.right_in) | copy-start | bytes 1572868
  61.7 10.8 %collective-permute-start.3 = (f32[520,768]{1,0:T(8,128)}, f32[520,768]{1,0:T(8,128)}, u32[]{:S(2)}, u32[]{:S(2)}) collective-permute-start(f32[520,768]{1,0:T(8,128)} %slice.7), channel_id=1, source_target_pairs={{0,1},{2,3},{4,5},{6,7},{8,9},{10,11},{12,13},{14,15},{16,17},{18,... | collective-permute-start | bytes 4792328 | tf_op jit(solution)/shard_map/ppermute | solution.py:34
  64.2 8.3 %collective-permute-start.4 = (f32[520,768]{1,0:T(8,128)}, f32[520,768]{1,0:T(8,128)}, u32[]{:S(2)}, u32[]{:S(2)}) collective-permute-start(f32[520,768]{1,0:T(8,128)} %collective-permute-done.2.left_ref.bm2_ref), channel_id=1, source_target_pairs={{1,0},{3,2},{5,4},{7,6},{9,8},{11,10},{13,12},{15,14},{17,16},{19,... | collective-permute-start | bytes 4792328 | tf_op jit(solution)/shard_map/ppermute | solution.py:34
  65.6 1.0 copy-start.1
  66.7 1.0 copy-start.5
  67.7 4.8 %copy-start.3 = (f32[256,512]{1,0:T(8,128)S(1)}, f32[256,512]{1,0:T(8,128)}, u32[]{:S(2)}) copy-start(f32[256,512]{1,0:T(8,128)} %copy-done.2) | copy-start | bytes 1572868
  84.2 11.0 %collective-permute-start.5 = (f32[256,512]{1,0:T(8,128)S(1)}, f32[256,512]{1,0:T(8,128)S(1)}, u32[]{:S(2)}, u32[]{:S(2)}) collective-permute-start(f32[256,512]{1,0:T(8,128)S(1)} %get-tuple-element.56.for_y_in), channel_id=1, source_target_pairs={{0,1},{2,3},{4,5},{6,7},{8,9},{10,11},{12,13},{14,15},{16,17},{18,... | collective-permute-start | bytes 1572872 | tf_op jit(solution)/shard_map/ppermute | solution.py:34
  91.9 12.7 %collective-permute-start.7 = (f32[256,512]{1,0:T(8,128)S(1)}, f32[256,512]{1,0:T(8,128)S(1)}, u32[]{:S(2)}, u32[]{:S(2)}) collective-permute-start(f32[256,512]{1,0:T(8,128)S(1)} %get-tuple-element.59), channel_id=1, source_target_pairs={{1,0},{3,2},{5,4},{7,6},{9,8},{11,10},{13,12},{15,14},{17,16},{19,... | collective-permute-start | bytes 1572872 | tf_op jit(solution)/shard_map/ppermute | solution.py:34
  93.2 18.8 %collective-permute-start.8 = (f32[256,512]{1,0:T(8,128)S(1)}, f32[256,512]{1,0:T(8,128)S(1)}, u32[]{:S(2)}, u32[]{:S(2)}) collective-permute-start(f32[256,512]{1,0:T(8,128)S(1)} %get-tuple-element.60), channel_id=1, source_target_pairs={{0,2},{1,511},{2,4},{3,1},{4,6},{5,3},{6,8},{7,5},{8,10},{9,7},{10... | collective-permute-start | bytes 1572872 | tf_op jit(solution)/shard_map/ppermute | solution.py:24
  95.3 18.9 %collective-permute-start.6 = (f32[256,512]{1,0:T(8,128)S(1)}, f32[256,512]{1,0:T(8,128)S(1)}, u32[]{:S(2)}, u32[]{:S(2)}) collective-permute-start(f32[256,512]{1,0:T(8,128)S(1)} %add.20), channel_id=1, source_target_pairs={{0,510},{1,3},{2,0},{3,5},{4,2},{5,7},{6,4},{7,9},{8,6},{9,11},{10... | collective-permute-start | bytes 1572872 | tf_op jit(solution)/shard_map/ppermute | solution.py:19
  112.2 16.5 %collective-permute-start.9 = (f32[256,512]{1,0:T(8,128)S(1)}, f32[256,512]{1,0:T(8,128)S(1)}, u32[]{:S(2)}, u32[]{:S(2)}) collective-permute-start(f32[256,512]{1,0:T(8,128)S(1)} %add_add_fusion), channel_id=1, source_target_pairs={{0,2},{1,511},{2,4},{3,1},{4,6},{5,3},{6,8},{7,5},{8,10},{9,7},{10... | collective-permute-start | bytes 1572872 | tf_op jit(solution)/shard_map/ppermute | solution.py:24

commit v3 on v2

v3 whole, which is shorter than its diff:
```python
import jax
import jax.numpy as jnp
from jax import lax
from jax.experimental import pallas as pl
from jax.experimental.pallas import tpu as pltpu
from jax.sharding import PartitionSpec as P

CLUSTERS = 256
TOP = 8


def even_odd(n, even, odd):
    return [(i, (i + (even if i % 2 == 0 else odd)) % n) for i in range(n)]


def pull(value):
    n = lax.axis_size("blk")
    return lax.ppermute(value, "blk", even_odd(n, -2, 2))


def push(value):
    n = lax.axis_size("blk")
    return lax.ppermute(value, "blk", even_odd(n, 2, -2))


def swap(value):
    n = lax.axis_size("blk")
    return lax.ppermute(value, "blk", even_odd(n, 1, -1))


def give(value, core):
    n = lax.axis_size("blk")
    return lax.ppermute(value, "blk", [(i, i ^ 1) for i in range(core, n, 2)])


def one_hot(labels):
    cluster = lax.broadcasted_iota(jnp.int32, (CLUSTERS, labels.shape[1]), 0)
    return jnp.where(cluster == labels.astype(jnp.int32), 1.0, 0.0).astype(jnp.bfloat16)


def unpack(message):
    rows = message.shape[0] - TOP
    return message[TOP:, :], one_hot(message[0:1, :rows])


def pack_body(embeddings_ref, labels_ref, message_ref, held, done):
    rows = embeddings_ref.shape[0]
    copy = pltpu.make_async_copy(embeddings_ref, message_ref.at[pl.ds(TOP, rows)], done.at[0])
    copy.start()
    labels = pltpu.make_async_copy(labels_ref, held, done.at[1])
    labels.start()
    message_ref[:TOP, :] = jnp.zeros((TOP, message_ref.shape[1]), jnp.float32)
    labels.wait()
    message_ref[0:1, :rows] = held[...].astype(jnp.float32)
    copy.wait()


def pack(embeddings, labels):
    rows, dim = embeddings.shape
    return pl.pallas_call(
        pack_body,
        out_shape=pltpu.VMEM((TOP + rows, dim), jnp.float32),
        in_specs=[pl.BlockSpec(memory_space=pltpu.HBM)] * 2,
        out_specs=pl.BlockSpec(memory_space=pltpu.VMEM),
        scratch_shapes=[pltpu.VMEM((1, rows), jnp.int32), pltpu.SemaphoreType.DMA((2,))],
        compiler_params=pltpu.CompilerParams(vmem_limit_bytes=16 * 2**20),
    )(
        pltpu.with_memory_space_constraint(embeddings, pltpu.HBM),
        pltpu.with_memory_space_constraint(labels[None, :], pltpu.HBM),
    )


def kernel_tile(left, right):
    left_norms = jnp.sum(left * left, axis=1, keepdims=True)
    right_norms = jnp.sum(right * right, axis=1, keepdims=True)
    right_norms = jnp.transpose(jnp.broadcast_to(right_norms, (right.shape[0], 128)))[0:1, :]
    inner = lax.dot_general(
        left,
        right,
        (((1,), (1,)), ((), ())),
        precision=lax.Precision.HIGHEST,
        preferred_element_type=jnp.float32,
    )
    return jnp.exp(-(left_norms + right_norms - 2.0 * inner)).astype(jnp.bfloat16)


def left_sums(right_hot, kernel):
    return lax.dot_general(
        right_hot, kernel, (((1,), (1,)), ((), ())), preferred_element_type=jnp.float32
    )


def right_sums(left_hot, kernel):
    return jnp.dot(left_hot, kernel, preferred_element_type=jnp.float32)


def self_body(own_ref, own_out):
    own, own_hot = unpack(own_ref)
    own_out[...] = left_sums(own_hot, kernel_tile(own, own))


def pair_body(left_ref, right_ref, left_out, right_out):
    left, left_hot = unpack(left_ref)
    right, right_hot = unpack(right_ref)
    kernel = kernel_tile(left, right)
    left_out[...] = left_sums(right_hot, kernel)
    right_out[...] = right_sums(left_hot, kernel)


def visitor_body(
    even_ref, own_ref, bm2_ref, b2_ref, y_top_ref, y_end_ref,
    own_out, for_m2_out, for_2_out, for_y_out,
):
    y, y_hot = unpack(jnp.concatenate([y_top_ref[...], y_end_ref[...]], axis=0))
    own, own_hot = unpack(own_ref)
    kernel = kernel_tile(own, y)
    own_out[...] = left_sums(y_hot, kernel)
    for_y_out[...] = right_sums(own_hot, kernel)
    b2, b2_hot = unpack(b2_ref)
    kernel = kernel_tile(b2, y)
    for_2_out[...] = left_sums(y_hot, kernel)
    for_y_out[...] += right_sums(b2_hot, kernel)
    for_m2_out[...] = jnp.zeros_like(for_m2_out)

    @pl.when(even_ref[0] == 1)
    def _():
        bm2, bm2_hot = unpack(bm2_ref)
        kernel = kernel_tile(bm2, y)
        for_m2_out[...] = left_sums(y_hot, kernel)
        for_y_out[...] += right_sums(bm2_hot, kernel)


def late_body(
    even_ref, bm2_ref, b4_ref, y_top_ref, y_end_ref, for_y_in, for_m2_out, for_4_out, for_y_out
):
    b4, b4_hot = unpack(b4_ref)
    bm2, bm2_hot = unpack(bm2_ref)
    kernel = kernel_tile(bm2, b4)
    for_m2_out[...] = left_sums(b4_hot, kernel)
    for_4_out[...] = right_sums(bm2_hot, kernel)
    for_y_out[...] = for_y_in[...]

    @pl.when(even_ref[0] == 0)
    def _():
        y, y_hot = unpack(jnp.concatenate([y_top_ref[...], y_end_ref[...]], axis=0))
        kernel = kernel_tile(b4, y)
        for_4_out[...] += left_sums(y_hot, kernel)
        for_y_out[...] += right_sums(b4_hot, kernel)


def call(body, outs, rows, *args, moved=1000):
    vmem = pl.BlockSpec(memory_space=pltpu.VMEM)
    smem = pl.BlockSpec(memory_space=pltpu.SMEM)
    return pl.pallas_call(
        body,
        out_shape=[pltpu.VMEM((CLUSTERS, rows), jnp.float32)] * outs,
        in_specs=[smem if a.ndim == 1 else vmem for a in args],
        out_specs=[vmem] * outs,
        compiler_params=pltpu.CompilerParams(vmem_limit_bytes=16 * 2**20),
        cost_estimate=pl.CostEstimate(flops=1000, bytes_accessed=moved, transcendentals=0),
    )(*(a if a.ndim == 1 else pltpu.with_memory_space_constraint(a, pltpu.VMEM) for a in args))


def on_device(embeddings, labels):
    rows = embeddings.shape[0]
    is_even = lax.axis_index("blk") % 2 == 0
    even = is_even.astype(jnp.int32)[None]
    own = pack(embeddings, labels)

    b2 = pull(own)
    bm2 = push(own)
    (own_0,) = call(self_body, 1, rows, own, moved=4 * own.size)
    b2, own_0 = lax.optimization_barrier((b2, own_0))
    b4 = pull(b2)

    b2, bm2 = lax.optimization_barrier((b2, bm2))
    own_2, for_2 = call(pair_body, 2, rows, own, b2, moved=1000)
    cut = TOP + rows // 2
    y = (
        swap(jnp.where(is_even, b2[:cut], bm2[:cut])),
        swap(jnp.where(is_even, b2[cut:], bm2[cut:])),
    )
    for_m2, for_2_m2 = call(pair_body, 2, rows, bm2, b2)

    y, own_2, for_2, for_m2, for_2_m2 = lax.optimization_barrier(
        (y, own_2, for_2, for_m2, for_2_m2)
    )
    own_y, for_m2_y, for_2_y, for_y = call(visitor_body, 4, rows, even, own, bm2, b2, *y)
    back_m2 = give(for_y, 0)

    b4, own_y, for_m2_y, for_2_y, for_y = lax.optimization_barrier(
        (b4, own_y, for_m2_y, for_2_y, for_y)
    )
    for_m2_4, for_4, for_y = call(
        late_body, 3, rows, even, bm2, b4, *y, for_y, moved=16 * own.size
    )
    back_4 = push(for_4)
    home_m2 = pull(for_m2 + for_m2_y + for_m2_4 + back_m2)
    back_2 = give(for_y, 1)
    back_4, back_2, for_2 = lax.optimization_barrier((back_4, back_2, for_2 + for_2_m2 + for_2_y))
    home_2 = push(for_2 + back_2 + back_4)
    return (own_0 + own_2 + own_y + home_m2 + home_2).T


def solution(mesh):
    placed = (P("blk", None), P("blk"))
    return jax.shard_map(
        on_device, mesh=mesh, in_specs=placed, out_specs=P("blk", None), check_vma=False
    )
```

time: 130 us -> 127 us (0.977)
  waiting for transfers between devices: 51.8 us -> 47.1 us
  local copies, waits for them, and re-layouts: 4.79 us -> 1.79 us
  other arithmetic: 0.37 us -> 2.78 us
  Pallas kernels: 30.3 us -> 31.6 us
    ppermute x0 -> x2, starting transfers between devices: none -> 4.49 us  [swap(): return lax.ppermute(value, 'blk', even_odd(n, 1, -1))]
    ppermute x4 -> x2, starting transfers between devices: 6.77 us -> 2.61 us  [give(): return lax.ppermute(value, 'blk', [(i, i ^ 1) for i in range(core, n, 2)])]
    ppermute x3, waiting for transfers between devices: 22 us -> 18.1 us  [push(): return lax.ppermute(value, 'blk', even_odd(n, 2, -2))]
    select_n x0 -> x2, other arithmetic: none -> 1.98 us  [the longest x1 0.99 us: on_device(): jnp.where(is_even, b2[cut:], bm2[cut:])]
    unnamed x12 -> x4, local copies, waits for them, and re-layouts: 2.27 us -> 0.79 us
    slice x2 -> x0, local copies, waits for them, and re-layouts: 1.47 us -> none  [the longest x1 1.37 us: on_device(): even_y = give(b2[:TOP + rows], 0)]
  transfers between devices with their start and end apart: 10 -> 10, of which waited for: 3 -> 4; matrix products, arithmetic and copies ran while one was open for 1% -> 2% of each run, Pallas kernels for 22% -> 23%
where the time goes in v3:
time: 127 us; the launch traced here: 126 us
  waiting for transfers between devices  47.1 us (37%)
  starting transfers between devices  42.7 us (34%)
  Pallas kernels  31.6 us (25%)
  other arithmetic  2.78 us (2%)
  local copies, waits for them, and re-layouts  1.79 us (1%)
    ppermute x3, starting transfers between devices, pull(): return lax.ppermute(value, 'blk', even_odd(n, -2, 2))  29.9 us
    ppermute x3, waiting for transfers between devices, pull(): return lax.ppermute(value, 'blk', even_odd(n, -2, 2))  29 us
    pallas_call x5, Pallas kernels, call(): pl.pallas_call(body, out_shape=[pltpu.VMEM((CLUSTERS, rows), jnp.float32)...  29 us
    ppermute x3, waiting for transfers between devices, push(): return lax.ppermute(value, 'blk', even_odd(n, 2, -2))  18.1 us
    ppermute x3, starting transfers between devices, push(): return lax.ppermute(value, 'blk', even_odd(n, 2, -2))  5.76 us
    ppermute x2, starting transfers between devices, swap(): return lax.ppermute(value, 'blk', even_odd(n, 1, -1))  4.49 us
    ppermute x2, starting transfers between devices, give(): return lax.ppermute(value, 'blk', [(i, i ^ 1) for i in range(core, n, 2)])  2.61 us
    pallas_call x1, Pallas kernels, pack(): pl.pallas_call(pack_body, out_shape=pltpu.VMEM((TOP + rows, dim), jnp.flo...  2.61 us
  transfers between devices with their start and end apart: 10, of which 4 were waited for; matrix products, arithmetic and copies ran while one was open for 2% of the time, Pallas kernels for 23%

profile of v3, /device:TPU:0, one launch (start us, length us, event | category | flops | bytes accessed | tf_op | source)
XLA Modules:
  0.0 126.2 jit_solution(1595039063108018917)
XLA Ops:
  0.0 2.6 %shard_map.28.own_ref.left_ref = f32[520,768]{1,0:T(8,128)} custom-call(f32[512,768]{1,0:T(8,128)} %embeddings_ref.1, s32[1,512]{1,0:T(1,128)} %bitcast.4), custom_call_target="tpu_custom_call" | custom-call | tf_op jit(solution)/shard_map/pallas_call | solution.py:60
  2.6 10.7 %collective-permute-start = (f32[520,768]{1,0:T(8,128)}, f32[520,768]{1,0:T(8,128)S(1)}, u32[]{:S(2)}, u32[]{:S(2)}) collective-permute-start(f32[520,768]{1,0:T(8,128)} %shard_map.28.own_ref.left_ref), channel_id=1, source_target_pairs={{0,510},{1,3},{2,0},{3,5},{4,2},{5,7},{6,4},{7,9},{8,6},{9,11},{10... | collective-permute-start | bytes 4792328 | tf_op jit(solution)/shard_map/ppermute | solution.py:18
  13.3 1.9 %collective-permute-start.1 = (f32[520,768]{1,0:T(8,128)}, f32[520,768]{1,0:T(8,128)S(1)}, u32[]{:S(2)}, u32[]{:S(2)}) collective-permute-start(f32[520,768]{1,0:T(8,128)} %shard_map.28.own_ref.left_ref), channel_id=1, source_target_pairs={{0,2},{1,511},{2,4},{3,1},{4,6},{5,3},{6,8},{7,5},{8,10},{9,7},{10... | collective-permute-start | bytes 4792328 | tf_op jit(solution)/shard_map/ppermute | solution.py:23
  15.2 4.4 %shard_map.29 = f32[256,512]{1,0:T(8,128)S(1)} custom-call(f32[520,768]{1,0:T(8,128)} %shard_map.28.own_ref.left_ref), custom_call_target="tpu_custom_call" | custom-call | flops 1000 | bytes 1597440 | tf_op jit(solution)/shard_map/pallas_call | solution.py:154
  19.7 0.8 copy-done
  20.4 27.7 %collective-permute-done.right_ref.b2_ref = f32[520,768]{1,0:T(8,128)S(1)} collective-permute-done((f32[520,768]{1,0:T(8,128)}, f32[520,768]{1,0:T(8,128)S(1)}, u32[]{:S(2)}, u32[]{:S(2)}) %collective-permute-start) | collective-permute-done | bytes 1597472 | tf_op jit(solution)/shard_map/ppermute | solution.py:18
  48.1 9.7 %collective-permute-start.4 = (f32[520,768]{1,0:T(8,128)S(1)}, f32[520,768]{1,0:T(8,128)}, u32[]{:S(2)}, u32[]{:S(2)}) collective-permute-start(f32[520,768]{1,0:T(8,128)S(1)} %collective-permute-done.right_ref.b2_ref), channel_id=1, source_target_pairs={{0,510},{1,3},{2,0},{3,5},{4,2},{5,7},{6,4},{7,9},{8,6},{9,11},{10... | collective-permute-start | bytes 4792328 | tf_op jit(solution)/shard_map/ppermute | solution.py:18
  57.9 1.0 slice_select_fusion
  58.9 1.9 %collective-permute-start.2 = (f32[264,768]{1,0:T(8,128)}, f32[264,768]{1,0:T(8,128)}, u32[]{:S(2)}, u32[]{:S(2)}) collective-permute-start(f32[264,768]{1,0:T(8,128)} %slice_select_fusion), channel_id=1, source_target_pairs={{0,1},{1,0},{2,3},{3,2},{4,5},{5,4},{6,7},{7,6},{8,9},{9,8},{10,11... | collective-permute-start | bytes 2433032 | tf_op jit(solution)/shard_map/ppermute | solution.py:28
  60.8 1.0 slice_select_fusion.1
  61.8 2.6 %collective-permute-start.3 = (f32[256,768]{1,0:T(8,128)}, f32[256,768]{1,0:T(8,128)}, u32[]{:S(2)}, u32[]{:S(2)}) collective-permute-start(f32[256,768]{1,0:T(8,128)} %slice_select_fusion.1), channel_id=1, source_target_pairs={{0,1},{1,0},{2,3},{3,2},{4,5},{5,4},{6,7},{7,6},{8,9},{9,8},{10,11... | collective-permute-start | bytes 2359304 | tf_op jit(solution)/shard_map/ppermute | solution.py:28
  64.3 3.3 %shard_map.31 = (f32[256,512]{1,0:T(8,128)S(1)}, f32[256,512]{1,0:T(8,128)S(1)}) custom-call(f32[520,768]{1,0:T(8,128)S(1)} %collective-permute-done.1.left_ref.bm2_ref, f32[520,768]{1,0:T(8,128)S(1)} %collective-permute-done.right_ref.b2_ref), custom_call_target="tpu_custom_call" | custom-call | flops 1000 | bytes 1000 | tf_op jit(solution)/shard_map/pallas_call | solution.py:154
  67.6 4.7 %shard_map.30 = (f32[256,512]{1,0:T(8,128)S(1)}, f32[256,512]{1,0:T(8,128)S(1)}) custom-call(f32[520,768]{1,0:T(8,128)} %shard_map.28.own_ref.left_ref, f32[520,768]{1,0:T(8,128)S(1)} %collective-permute-done.right_ref.b2_ref), custom_call_target="tpu_custom_call" | custom-call | flops 1000 | bytes 1000 | tf_op jit(solution)/shard_map/pallas_call | solution.py:154
  72.3 11.4 %shard_map.32 = (f32[256,512]{1,0:T(8,128)S(1)}, f32[256,512]{1,0:T(8,128)S(1)}, f32[256,512]{1,0:T(8,128)S(1)}, f32[256,512]{1,0:T(8,128)S(1)}) custom-call(s32[1]{0:T(128)} %bitcast.1.even_ref, f32[520,768]{1,0:T(8,128)} %shard_map.28.own_ref.left_ref, f32[520,768]{1,0:T(8,128)S(1)} %collective-permute-done.1.left_ref.bm2_ref, ...), custom_call_target="tpu_custom_call" | custom-call | flops 1000 | bytes 1000 | tf_op jit(solution)/shard_map/pallas_call | solution.py:154
  83.7 1.3 %collective-permute-start.5 = (f32[256,512]{1,0:T(8,128)S(1)}, f32[256,512]{1,0:T(8,128)S(1)}, u32[]{:S(2)}, u32[]{:S(2)}) collective-permute-start(f32[256,512]{1,0:T(8,128)S(1)} %get-tuple-element.53.for_y_in), channel_id=1, source_target_pairs={{0,1},{2,3},{4,5},{6,7},{8,9},{10,11},{12,13},{14,15},{16,17},{18,... | collective-permute-start | bytes 1572872 | tf_op jit(solution)/shard_map/ppermute | solution.py:33
  85.1 5.2 %shard_map.33 = (f32[256,512]{1,0:T(8,128)S(1)}, f32[256,512]{1,0:T(8,128)S(1)}, f32[256,512]{1,0:T(8,128)S(1)}) custom-call(s32[1]{0:T(128)} %bitcast.1.even_ref, f32[520,768]{1,0:T(8,128)S(1)} %collective-permute-done.1.left_ref.bm2_ref, f32[520,768]{1,0:T(8,128)} %collective-permute-done.4.b4_ref, f32[264,768]{1,0:T(8,128)} %collective-permute-done.2.y_top_ref, ...), custom_call_target="tpu_custom_call" | custom-call | flops 1000 | bytes 6389760 | tf_op jit(solution)/shard_map/pallas_call | solution.py:154
  90.3 1.9 %collective-permute-start.7 = (f32[256,512]{1,0:T(8,128)S(1)}, f32[256,512]{1,0:T(8,128)S(1)}, u32[]{:S(2)}, u32[]{:S(2)}) collective-permute-start(f32[256,512]{1,0:T(8,128)S(1)} %get-tuple-element.55), channel_id=1, source_target_pairs={{0,2},{1,511},{2,4},{3,1},{4,6},{5,3},{6,8},{7,5},{8,10},{9,7},{10... | collective-permute-start | bytes 1572872 | tf_op jit(solution)/shard_map/ppermute | solution.py:23
  92.2 1.3 %collective-permute-start.8 = (f32[256,512]{1,0:T(8,128)S(1)}, f32[256,512]{1,0:T(8,128)S(1)}, u32[]{:S(2)}, u32[]{:S(2)}) collective-permute-start(f32[256,512]{1,0:T(8,128)S(1)} %get-tuple-element.56), channel_id=1, source_target_pairs={{1,0},{3,2},{5,4},{7,6},{9,8},{11,10},{13,12},{15,14},{17,16},{19,... | collective-permute-start | bytes 1572872 | tf_op jit(solution)/shard_map/ppermute | solution.py:33
  93.7 9.5 %collective-permute-start.6 = (f32[256,512]{1,0:T(8,128)S(1)}, f32[256,512]{1,0:T(8,128)S(1)}, u32[]{:S(2)}, u32[]{:S(2)}) collective-permute-start(f32[256,512]{1,0:T(8,128)S(1)} %add_add_fusion.2), channel_id=1, source_target_pairs={{0,510},{1,3},{2,0},{3,5},{4,2},{5,7},{6,4},{7,9},{8,6},{9,11},{10... | collective-permute-start | bytes 1572872 | tf_op jit(solution)/shard_map/ppermute | solution.py:18
  103.4 4.9 %collective-permute-done.7 = f32[256,512]{1,0:T(8,128)S(1)} collective-permute-done((f32[256,512]{1,0:T(8,128)S(1)}, f32[256,512]{1,0:T(8,128)S(1)}, u32[]{:S(2)}, u32[]{:S(2)}) %collective-permute-start.7) | collective-permute-done | bytes 524320 | tf_op jit(solution)/shard_map/ppermute | solution.py:23
  108.4 1.9 %collective-permute-start.9 = (f32[256,512]{1,0:T(8,128)S(1)}, f32[256,512]{1,0:T(8,128)S(1)}, u32[]{:S(2)}, u32[]{:S(2)}) collective-permute-start(f32[256,512]{1,0:T(8,128)S(1)} %add_add_fusion), channel_id=1, source_target_pairs={{0,2},{1,511},{2,4},{3,1},{4,6},{5,3},{6,8},{7,5},{8,10},{9,7},{10... | collective-permute-start | bytes 1572872 | tf_op jit(solution)/shard_map/ppermute | solution.py:23
  110.3 1.3 %collective-permute-done.6 = f32[256,512]{1,0:T(8,128)S(1)} collective-permute-done((f32[256,512]{1,0:T(8,128)S(1)}, f32[256,512]{1,0:T(8,128)S(1)}, u32[]{:S(2)}, u32[]{:S(2)}) %collective-permute-start.6) | collective-permute-done | bytes 524320 | tf_op jit(solution)/shard_map/ppermute | solution.py:18
  111.6 13.3 %collective-permute-done.9 = f32[256,512]{1,0:T(8,128)S(1)} collective-permute-done((f32[256,512]{1,0:T(8,128)S(1)}, f32[256,512]{1,0:T(8,128)S(1)}, u32[]{:S(2)}, u32[]{:S(2)}) %collective-permute-start.9) | collective-permute-done | bytes 524320 | tf_op jit(solution)/shard_map/ppermute | solution.py:23
  125.2 1.0 copy.3
  (13 shorter events, 0.8 us)
Async XLA Ops:
  2.6 45.5 %collective-permute-start = (f32[520,768]{1,0:T(8,128)}, f32[520,768]{1,0:T(8,128)S(1)}, u32[]{:S(2)}, u32[]{:S(2)}) collective-permute-start(f32[520,768]{1,0:T(8,128)} %shard_map.28.own_ref.left_ref), channel_id=1, source_target_pairs={{0,510},{1,3},{2,0},{3,5},{4,2},{5,7},{6,4},{7,9},{8,6},{9,11},{10... | collective-permute-start | bytes 4792328 | tf_op jit(solution)/shard_map/ppermute | solution.py:18
  13.3 44.6 %collective-permute-start.1 = (f32[520,768]{1,0:T(8,128)}, f32[520,768]{1,0:T(8,128)S(1)}, u32[]{:S(2)}, u32[]{:S(2)}) collective-permute-start(f32[520,768]{1,0:T(8,128)} %shard_map.28.own_ref.left_ref), channel_id=1, source_target_pairs={{0,2},{1,511},{2,4},{3,1},{4,6},{5,3},{6,8},{7,5},{8,10},{9,7},{10... | collective-permute-start | bytes 4792328 | tf_op jit(solution)/shard_map/ppermute | solution.py:23
  19.6 0.8 copy-start
  48.1 36.9 %collective-permute-start.4 = (f32[520,768]{1,0:T(8,128)S(1)}, f32[520,768]{1,0:T(8,128)}, u32[]{:S(2)}, u32[]{:S(2)}) collective-permute-start(f32[520,768]{1,0:T(8,128)S(1)} %collective-permute-done.right_ref.b2_ref), channel_id=1, source_target_pairs={{0,510},{1,3},{2,0},{3,5},{4,2},{5,7},{6,4},{7,9},{8,6},{9,11},{10... | collective-permute-start | bytes 4792328 | tf_op jit(solution)/shard_map/ppermute | solution.py:18
  58.9 13.5 %collective-permute-start.2 = (f32[264,768]{1,0:T(8,128)}, f32[264,768]{1,0:T(8,128)}, u32[]{:S(2)}, u32[]{:S(2)}) collective-permute-start(f32[264,768]{1,0:T(8,128)} %slice_select_fusion), channel_id=1, source_target_pairs={{0,1},{1,0},{2,3},{3,2},{4,5},{5,4},{6,7},{7,6},{8,9},{9,8},{10,11... | collective-permute-start | bytes 2433032 | tf_op jit(solution)/shard_map/ppermute | solution.py:28
  61.8 10.6 %collective-permute-start.3 = (f32[256,768]{1,0:T(8,128)}, f32[256,768]{1,0:T(8,128)}, u32[]{:S(2)}, u32[]{:S(2)}) collective-permute-start(f32[256,768]{1,0:T(8,128)} %slice_select_fusion.1), channel_id=1, source_target_pairs={{0,1},{1,0},{2,3},{3,2},{4,5},{5,4},{6,7},{7,6},{8,9},{9,8},{10,11... | collective-permute-start | bytes 2359304 | tf_op jit(solution)/shard_map/ppermute | solution.py:28
  83.7 9.8 %collective-permute-start.5 = (f32[256,512]{1,0:T(8,128)S(1)}, f32[256,512]{1,0:T(8,128)S(1)}, u32[]{:S(2)}, u32[]{:S(2)}) collective-permute-start(f32[256,512]{1,0:T(8,128)S(1)} %get-tuple-element.53.for_y_in), channel_id=1, source_target_pairs={{0,1},{2,3},{4,5},{6,7},{8,9},{10,11},{12,13},{14,15},{16,17},{18,... | collective-permute-start | bytes 1572872 | tf_op jit(solution)/shard_map/ppermute | solution.py:33
  90.3 18.0 %collective-permute-start.7 = (f32[256,512]{1,0:T(8,128)S(1)}, f32[256,512]{1,0:T(8,128)S(1)}, u32[]{:S(2)}, u32[]{:S(2)}) collective-permute-start(f32[256,512]{1,0:T(8,128)S(1)} %get-tuple-element.55), channel_id=1, source_target_pairs={{0,2},{1,511},{2,4},{3,1},{4,6},{5,3},{6,8},{7,5},{8,10},{9,7},{10... | collective-permute-start | bytes 1572872 | tf_op jit(solution)/shard_map/ppermute | solution.py:23
  92.2 16.1 %collective-permute-start.8 = (f32[256,512]{1,0:T(8,128)S(1)}, f32[256,512]{1,0:T(8,128)S(1)}, u32[]{:S(2)}, u32[]{:S(2)}) collective-permute-start(f32[256,512]{1,0:T(8,128)S(1)} %get-tuple-element.56), channel_id=1, source_target_pairs={{1,0},{3,2},{5,4},{7,6},{9,8},{11,10},{13,12},{15,14},{17,16},{19,... | collective-permute-start | bytes 1572872 | tf_op jit(solution)/shard_map/ppermute | solution.py:33
  93.7 31.2 %copy-start.1 = (f32[256,512]{1,0:T(8,128)S(1)}, f32[256,512]{1,0:T(8,128)}, u32[]{:S(2)}) copy-start(f32[256,512]{1,0:T(8,128)} %copy-done) | copy-start | bytes 1572868
  93.7 17.9 %collective-permute-start.6 = (f32[256,512]{1,0:T(8,128)S(1)}, f32[256,512]{1,0:T(8,128)S(1)}, u32[]{:S(2)}, u32[]{:S(2)}) collective-permute-start(f32[256,512]{1,0:T(8,128)S(1)} %add_add_fusion.2), channel_id=1, source_target_pairs={{0,510},{1,3},{2,0},{3,5},{4,2},{5,7},{6,4},{7,9},{8,6},{9,11},{10... | collective-permute-start | bytes 1572872 | tf_op jit(solution)/shard_map/ppermute | solution.py:18
  108.4 16.5 %collective-permute-start.9 = (f32[256,512]{1,0:T(8,128)S(1)}, f32[256,512]{1,0:T(8,128)S(1)}, u32[]{:S(2)}, u32[]{:S(2)}) collective-permute-start(f32[256,512]{1,0:T(8,128)S(1)} %add_add_fusion), channel_id=1, source_target_pairs={{0,2},{1,511},{2,4},{3,1},{4,6},{5,3},{6,8},{7,5},{8,10},{9,7},{10... | collective-permute-start | bytes 1572872 | tf_op jit(solution)/shard_map/ppermute | solution.py:23

commit v4 on v3

--- a/solution.py
+++ b/solution.py
@@ -148,51 +148,68 @@
         for_y_out[...] += right_sums(b4_hot, kernel)
 
 
-def call(body, outs, rows, *args, moved=1000):
+def choose_body(even_ref, b2_ref, bm2_ref, top_out, end_out):
+    cut = top_out.shape[0]
+
+    @pl.when(even_ref[0] == 1)
+    def _():
+        top_out[...] = b2_ref[:cut, :]
+        end_out[...] = b2_ref[cut:, :]
+
+    @pl.when(even_ref[0] == 0)
+    def _():
+        top_out[...] = bm2_ref[:cut, :]
+        end_out[...] = bm2_ref[cut:, :]
+
+
+def call(body, shapes, *args, moved=1000):
     vmem = pl.BlockSpec(memory_space=pltpu.VMEM)
     smem = pl.BlockSpec(memory_space=pltpu.SMEM)
     return pl.pallas_call(
         body,
-        out_shape=[pltpu.VMEM((CLUSTERS, rows), jnp.float32)] * outs,
+        out_shape=[pltpu.VMEM(shape, jnp.float32) for shape in shapes],
         in_specs=[smem if a.ndim == 1 else vmem for a in args],
-        out_specs=[vmem] * outs,
+        out_specs=[vmem] * len(shapes),
         compiler_params=pltpu.CompilerParams(vmem_limit_bytes=16 * 2**20),
         cost_estimate=pl.CostEstimate(flops=1000, bytes_accessed=moved, transcendentals=0),
     )(*(a if a.ndim == 1 else pltpu.with_memory_space_constraint(a, pltpu.VMEM) for a in args))
 
 
 def on_device(embeddings, labels):
-    rows = embeddings.shape[0]
-    is_even = lax.axis_index("blk") % 2 == 0
-    even = is_even.astype(jnp.int32)[None]
+    rows, dim = embeddings.shape
+    cut = TOP + rows // 2
+    sums = (CLUSTERS, rows)
+    even = swap((lax.axis_index("blk") % 2).astype(jnp.int32)[None])
     own = pack(embeddings, labels)
+    own, even = lax.optimization_barrier((own, even))
 
     b2 = pull(own)
     bm2 = push(own)
-    (own_0,) = call(self_body, 1, rows, own, moved=4 * own.size)
+    (own_0,) = call(self_body, [sums], own, moved=4 * own.size)
     b2, own_0 = lax.optimization_barrier((b2, own_0))
     b4 = pull(b2)
 
     b2, bm2 = lax.optimization_barrier((b2, bm2))
-    own_2, for_2 = call(pair_body, 2, rows, own, b2, moved=1000)
-    cut = TOP + rows // 2
-    y = (
-        swap(jnp.where(is_even, b2[:cut], bm2[:cut])),
-        swap(jnp.where(is_even, b2[cut:], bm2[cut:])),
-    )
-    for_m2, for_2_m2 = call(pair_body, 2, rows, bm2, b2)
+    y_top, y_end = call(
+        choose_body, [(cut, dim), (rows + TOP - cut, dim)], even, b2, bm2, moved=8 * own.size
+    )
+    y = swap(y_top), swap(y_end)
+    own_2, for_2 = call(pair_body, [sums] * 2, own, b2, moved=8 * own.size)
+    for_m2, for_2_m2 = call(pair_body, [sums] * 2, bm2, b2, moved=8 * own.size)
 
     y, own_2, for_2, for_m2, for_2_m2 = lax.optimization_barrier(
         (y, own_2, for_2, for_m2, for_2_m2)
     )
-    own_y, for_m2_y, for_2_y, for_y = call(visitor_body, 4, rows, even, own, bm2, b2, *y)
+    own_y, for_m2_y, for_2_y, for_y = call(
+        visitor_body, [sums] * 4, even, own, bm2, b2, *y, moved=8 * own.size
+    )
     back_m2 = give(for_y, 0)
 
     b4, own_y, for_m2_y, for_2_y, for_y = lax.optimization_barrier(
         (b4, own_y, for_m2_y, for_2_y, for_y)
     )
     for_m2_4, for_4, for_y = call(
-        late_body, 3, rows, even, bm2, b4, *y, for_y, moved=16 * own.size
+        late_body, [sums] * 3, even, bm2, b4, *y, for_y, moved=16 * own.size
     )
     back_4 = push(for_4)
     home_m2 = pull(for_m2 + for_m2_y + for_m2_4 + back_m2)

time: 127 us -> 123 us (0.969)
  Pallas kernels: 31.6 us -> 26.2 us
  starting transfers between devices: 42.7 us -> 45.4 us
  other arithmetic: 2.78 us -> 0.81 us
  waiting for transfers between devices: 47.1 us -> 48.5 us
    pallas_call x5 -> x6, Pallas kernels: 29 us -> 24.8 us  [call(): pl.pallas_call(body, out_shape=[pltpu.VMEM(shape, jnp.float32) for shape...]
    ppermute x2 -> x3, starting transfers between devices: 4.49 us -> 7.22 us  [swap(): return lax.ppermute(value, 'blk', even_odd(n, 1, -1))]
    select_n x2 -> x0, other arithmetic: 1.98 us -> none  [the longest x1 0.99 us: on_device(): jnp.where(is_even, b2[cut:], bm2[cut:])]
  transfers between devices with their start and end apart: 10 -> 11, of which waited for: 4 -> 4; matrix products, arithmetic and copies ran while one was open for 2% -> 0% of each run, Pallas kernels for 23% -> 21%
where the time goes in v4:
time: 123 us; the launch traced here: 122 us
  waiting for transfers between devices  48.5 us (39%)
  starting transfers between devices  45.4 us (37%)
  Pallas kernels  26.2 us (21%)
    ppermute x3, starting transfers between devices, pull(): return lax.ppermute(value, 'blk', even_odd(n, -2, 2))  29.8 us
    ppermute x3, waiting for transfers between devices, pull(): return lax.ppermute(value, 'blk', even_odd(n, -2, 2))  29.6 us
    pallas_call x6, Pallas kernels, call(): pl.pallas_call(body, out_shape=[pltpu.VMEM(shape, jnp.float32) for shape...  24.8 us
    ppermute x3, waiting for transfers between devices, push(): return lax.ppermute(value, 'blk', even_odd(n, 2, -2))  18.9 us
    ppermute x3, starting transfers between devices, swap(): return lax.ppermute(value, 'blk', even_odd(n, 1, -1))  7.22 us
    ppermute x3, starting transfers between devices, push(): return lax.ppermute(value, 'blk', even_odd(n, 2, -2))  5.76 us
    ppermute x2, starting transfers between devices, give(): return lax.ppermute(value, 'blk', [(i, i ^ 1) for i in range(core, n, 2)])  2.61 us
  transfers between devices with their start and end apart: 11, of which 4 were waited for; matrix products, arithmetic and copies ran while one was open for 0% of the time, Pallas kernels for 21%

profile of v4, /device:TPU:0, one launch (start us, length us, event | category | flops | bytes accessed | tf_op | source)
XLA Modules:
  0.0 122.1 jit_solution(10256047630147973602)
XLA Ops:
  0.0 2.7 %collective-permute-start = (s32[1]{0:T(128)}, s32[1]{0:T(128)}, u32[]{:S(2)}, u32[]{:S(2)}) collective-permute-start(s32[1]{0:T(128)} %bitcast.1), channel_id=1, source_target_pairs={{0,1},{1,0},{2,3},{3,2},{4,5},{5,4},{6,7},{7,6},{8,9},{9,8},{10,11... | collective-permute-start | bytes 20 | tf_op jit(solution)/shard_map/ppermute | solution.py:28
  2.7 1.4 %shard_map.28.own_ref.left_ref = f32[520,768]{1,0:T(8,128)S(1)} custom-call(f32[512,768]{1,0:T(8,128)} %embeddings_ref.1, s32[1,512]{1,0:T(1,128)} %bitcast.4), custom_call_target="tpu_custom_call" | custom-call | tf_op jit(solution)/shard_map/pallas_call | solution.py:60
  4.2 10.7 %collective-permute-start.1 = (f32[520,768]{1,0:T(8,128)S(1)}, f32[520,768]{1,0:T(8,128)S(1)}, u32[]{:S(2)}, u32[]{:S(2)}) collective-permute-start(f32[520,768]{1,0:T(8,128)S(1)} %shard_map.28.own_ref.left_ref), channel_id=1, source_target_pairs={{0,510},{1,3},{2,0},{3,5},{4,2},{5,7},{6,4},{7,9},{8,6},{9,11},{10... | collective-permute-start | bytes 4792328 | tf_op jit(solution)/shard_map/ppermute | solution.py:18
  14.8 1.9 %collective-permute-start.2 = (f32[520,768]{1,0:T(8,128)S(1)}, f32[520,768]{1,0:T(8,128)S(1)}, u32[]{:S(2)}, u32[]{:S(2)}) collective-permute-start(f32[520,768]{1,0:T(8,128)S(1)} %shard_map.28.own_ref.left_ref), channel_id=1, source_target_pairs={{0,2},{1,511},{2,4},{3,1},{4,6},{5,3},{6,8},{7,5},{8,10},{9,7},{10... | collective-permute-start | bytes 4792328 | tf_op jit(solution)/shard_map/ppermute | solution.py:23
  16.8 3.1 %shard_map.29 = f32[256,512]{1,0:T(8,128)S(1)} custom-call(f32[520,768]{1,0:T(8,128)S(1)} %shard_map.28.own_ref.left_ref), custom_call_target="tpu_custom_call" | custom-call | flops 1000 | bytes 1597440 | tf_op jit(solution)/shard_map/pallas_call | solution.py:168
  19.8 28.8 %collective-permute-done.1.b2_ref.right_ref = f32[520,768]{1,0:T(8,128)S(1)} collective-permute-done((f32[520,768]{1,0:T(8,128)S(1)}, f32[520,768]{1,0:T(8,128)S(1)}, u32[]{:S(2)}, u32[]{:S(2)}) %collective-permute-start.1) | collective-permute-done | bytes 1597472 | tf_op jit(solution)/shard_map/ppermute | solution.py:18
  48.6 9.8 %collective-permute-start.5 = (f32[520,768]{1,0:T(8,128)S(1)}, f32[520,768]{1,0:T(8,128)S(1)}, u32[]{:S(2)}, u32[]{:S(2)}) collective-permute-start(f32[520,768]{1,0:T(8,128)S(1)} %collective-permute-done.1.b2_ref.right_ref), channel_id=1, source_target_pairs={{0,510},{1,3},{2,0},{3,5},{4,2},{5,7},{6,4},{7,9},{8,6},{9,11},{10... | collective-permute-start | bytes 4792328 | tf_op jit(solution)/shard_map/ppermute | solution.py:18
  58.4 0.7 shard_map.30
  59.2 1.9 %collective-permute-start.3 = (f32[264,768]{1,0:T(8,128)S(1)}, f32[264,768]{1,0:T(8,128)S(1)}, u32[]{:S(2)}, u32[]{:S(2)}) collective-permute-start(f32[264,768]{1,0:T(8,128)S(1)} %get-tuple-element.44), channel_id=1, source_target_pairs={{0,1},{1,0},{2,3},{3,2},{4,5},{5,4},{6,7},{7,6},{8,9},{9,8},{10,11... | collective-permute-start | bytes 2433032 | tf_op jit(solution)/shard_map/ppermute | solution.py:28
  61.1 2.6 %collective-permute-start.4 = (f32[256,768]{1,0:T(8,128)S(1)}, f32[256,768]{1,0:T(8,128)S(1)}, u32[]{:S(2)}, u32[]{:S(2)}) collective-permute-start(f32[256,768]{1,0:T(8,128)S(1)} %get-tuple-element.45), channel_id=1, source_target_pairs={{0,1},{1,0},{2,3},{3,2},{4,5},{5,4},{6,7},{7,6},{8,9},{9,8},{10,11... | collective-permute-start | bytes 2359304 | tf_op jit(solution)/shard_map/ppermute | solution.py:28
  63.7 3.3 %shard_map.32 = (f32[256,512]{1,0:T(8,128)S(1)}, f32[256,512]{1,0:T(8,128)S(1)}) custom-call(f32[520,768]{1,0:T(8,128)S(1)} %collective-permute-done.2.bm2_ref.left_ref, f32[520,768]{1,0:T(8,128)S(1)} %collective-permute-done.1.b2_ref.right_ref), custom_call_target="tpu_custom_call" | custom-call | flops 1000 | bytes 3194880 | tf_op jit(solution)/shard_map/pallas_call | solution.py:168
  67.0 3.3 %shard_map.31 = (f32[256,512]{1,0:T(8,128)S(1)}, f32[256,512]{1,0:T(8,128)S(1)}) custom-call(f32[520,768]{1,0:T(8,128)S(1)} %shard_map.28.own_ref.left_ref, f32[520,768]{1,0:T(8,128)S(1)} %collective-permute-done.1.b2_ref.right_ref), custom_call_target="tpu_custom_call" | custom-call | flops 1000 | bytes 3194880 | tf_op jit(solution)/shard_map/pallas_call | solution.py:168
  70.3 10.3 %shard_map.33 = (f32[256,512]{1,0:T(8,128)S(1)}, f32[256,512]{1,0:T(8,128)S(1)}, f32[256,512]{1,0:T(8,128)S(1)}, f32[256,512]{1,0:T(8,128)S(1)}) custom-call(s32[1]{0:T(128)} %collective-permute-done.even_ref, f32[520,768]{1,0:T(8,128)S(1)} %shard_map.28.own_ref.left_ref, f32[520,768]{1,0:T(8,128)S(1)} %collective-permute-done.2.bm2_ref.left_ref, ...), custom_call_target="tpu_custom_call" | custom-call | flops 1000 | bytes 3194880 | tf_op jit(solution)/shard_map/pallas_call | solution.py:168
  80.7 1.3 %collective-permute-start.6 = (f32[256,512]{1,0:T(8,128)S(1)}, f32[256,512]{1,0:T(8,128)S(1)}, u32[]{:S(2)}, u32[]{:S(2)}) collective-permute-start(f32[256,512]{1,0:T(8,128)S(1)} %get-tuple-element.61.for_y_in), channel_id=1, source_target_pairs={{0,1},{2,3},{4,5},{6,7},{8,9},{10,11},{12,13},{14,15},{16,17},{18,... | collective-permute-start | bytes 1572872 | tf_op jit(solution)/shard_map/ppermute | solution.py:33
  82.0 4.1 %shard_map.34 = (f32[256,512]{1,0:T(8,128)S(1)}, f32[256,512]{1,0:T(8,128)S(1)}, f32[256,512]{1,0:T(8,128)S(1)}) custom-call(s32[1]{0:T(128)} %collective-permute-done.even_ref, f32[520,768]{1,0:T(8,128)S(1)} %collective-permute-done.2.bm2_ref.left_ref, f32[520,768]{1,0:T(8,128)S(1)} %collective-permute-done.5.b4_ref, ...), custom_call_target="tpu_custom_call" | custom-call | flops 1000 | bytes 6389760 | tf_op jit(solution)/shard_map/pallas_call | solution.py:168
  86.1 1.9 %collective-permute-start.8 = (f32[256,512]{1,0:T(8,128)S(1)}, f32[256,512]{1,0:T(8,128)S(1)}, u32[]{:S(2)}, u32[]{:S(2)}) collective-permute-start(f32[256,512]{1,0:T(8,128)S(1)} %get-tuple-element.63), channel_id=1, source_target_pairs={{0,2},{1,511},{2,4},{3,1},{4,6},{5,3},{6,8},{7,5},{8,10},{9,7},{10... | collective-permute-start | bytes 1572872 | tf_op jit(solution)/shard_map/ppermute | solution.py:23
  88.0 1.3 %collective-permute-start.9 = (f32[256,512]{1,0:T(8,128)S(1)}, f32[256,512]{1,0:T(8,128)S(1)}, u32[]{:S(2)}, u32[]{:S(2)}) collective-permute-start(f32[256,512]{1,0:T(8,128)S(1)} %get-tuple-element.64), channel_id=1, source_target_pairs={{1,0},{3,2},{5,4},{7,6},{9,8},{11,10},{13,12},{15,14},{17,16},{19,... | collective-permute-start | bytes 1572872 | tf_op jit(solution)/shard_map/ppermute | solution.py:33
  89.5 9.4 %collective-permute-start.7 = (f32[256,512]{1,0:T(8,128)S(1)}, f32[256,512]{1,0:T(8,128)S(1)}, u32[]{:S(2)}, u32[]{:S(2)}) collective-permute-start(f32[256,512]{1,0:T(8,128)S(1)} %add_add_fusion.2), channel_id=1, source_target_pairs={{0,510},{1,3},{2,0},{3,5},{4,2},{5,7},{6,4},{7,9},{8,6},{9,11},{10... | collective-permute-start | bytes 1572872 | tf_op jit(solution)/shard_map/ppermute | solution.py:18
  99.0 5.2 %collective-permute-done.8 = f32[256,512]{1,0:T(8,128)S(1)} collective-permute-done((f32[256,512]{1,0:T(8,128)S(1)}, f32[256,512]{1,0:T(8,128)S(1)}, u32[]{:S(2)}, u32[]{:S(2)}) %collective-permute-start.8) | collective-permute-done | bytes 524320 | tf_op jit(solution)/shard_map/ppermute | solution.py:23
  104.3 1.9 %collective-permute-start.10 = (f32[256,512]{1,0:T(8,128)S(1)}, f32[256,512]{1,0:T(8,128)S(1)}, u32[]{:S(2)}, u32[]{:S(2)}) collective-permute-start(f32[256,512]{1,0:T(8,128)S(1)} %add_add_fusion), channel_id=1, source_target_pairs={{0,2},{1,511},{2,4},{3,1},{4,6},{5,3},{6,8},{7,5},{8,10},{9,7},{10... | collective-permute-start | bytes 1572872 | tf_op jit(solution)/shard_map/ppermute | solution.py:23
  106.3 0.8 collective-permute-done.7
  107.1 13.8 %collective-permute-done.10 = f32[256,512]{1,0:T(8,128)S(1)} collective-permute-done((f32[256,512]{1,0:T(8,128)S(1)}, f32[256,512]{1,0:T(8,128)S(1)}, u32[]{:S(2)}, u32[]{:S(2)}) %collective-permute-start.10) | collective-permute-done | bytes 524320 | tf_op jit(solution)/shard_map/ppermute | solution.py:23
  120.8 0.3 add_bitcast_fusion
  121.1 1.0 copy.3
  (10 shorter events, 0.5 us)
Async XLA Ops:
  0.0 4.2 %collective-permute-start = (s32[1]{0:T(128)}, s32[1]{0:T(128)}, u32[]{:S(2)}, u32[]{:S(2)}) collective-permute-start(s32[1]{0:T(128)} %bitcast.1), channel_id=1, source_target_pairs={{0,1},{1,0},{2,3},{3,2},{4,5},{5,4},{6,7},{7,6},{8,9},{9,8},{10,11... | collective-permute-start | bytes 20 | tf_op jit(solution)/shard_map/ppermute | solution.py:28
  4.2 44.5 %collective-permute-start.1 = (f32[520,768]{1,0:T(8,128)S(1)}, f32[520,768]{1,0:T(8,128)S(1)}, u32[]{:S(2)}, u32[]{:S(2)}) collective-permute-start(f32[520,768]{1,0:T(8,128)S(1)} %shard_map.28.own_ref.left_ref), channel_id=1, source_target_pairs={{0,510},{1,3},{2,0},{3,5},{4,2},{5,7},{6,4},{7,9},{8,6},{9,11},{10... | collective-permute-start | bytes 4792328 | tf_op jit(solution)/shard_map/ppermute | solution.py:18
  14.8 43.6 %collective-permute-start.2 = (f32[520,768]{1,0:T(8,128)S(1)}, f32[520,768]{1,0:T(8,128)S(1)}, u32[]{:S(2)}, u32[]{:S(2)}) collective-permute-start(f32[520,768]{1,0:T(8,128)S(1)} %shard_map.28.own_ref.left_ref), channel_id=1, source_target_pairs={{0,2},{1,511},{2,4},{3,1},{4,6},{5,3},{6,8},{7,5},{8,10},{9,7},{10... | collective-permute-start | bytes 4792328 | tf_op jit(solution)/shard_map/ppermute | solution.py:23
  48.6 33.4 %collective-permute-start.5 = (f32[520,768]{1,0:T(8,128)S(1)}, f32[520,768]{1,0:T(8,128)S(1)}, u32[]{:S(2)}, u32[]{:S(2)}) collective-permute-start(f32[520,768]{1,0:T(8,128)S(1)} %collective-permute-done.1.b2_ref.right_ref), channel_id=1, source_target_pairs={{0,510},{1,3},{2,0},{3,5},{4,2},{5,7},{6,4},{7,9},{8,6},{9,11},{10... | collective-permute-start | bytes 4792328 | tf_op jit(solution)/shard_map/ppermute | solution.py:18
  59.2 11.2 %collective-permute-start.3 = (f32[264,768]{1,0:T(8,128)S(1)}, f32[264,768]{1,0:T(8,128)S(1)}, u32[]{:S(2)}, u32[]{:S(2)}) collective-permute-start(f32[264,768]{1,0:T(8,128)S(1)} %get-tuple-element.44), channel_id=1, source_target_pairs={{0,1},{1,0},{2,3},{3,2},{4,5},{5,4},{6,7},{7,6},{8,9},{9,8},{10,11... | collective-permute-start | bytes 2433032 | tf_op jit(solution)/shard_map/ppermute | solution.py:28
  61.1 9.2 %collective-permute-start.4 = (f32[256,768]{1,0:T(8,128)S(1)}, f32[256,768]{1,0:T(8,128)S(1)}, u32[]{:S(2)}, u32[]{:S(2)}) collective-permute-start(f32[256,768]{1,0:T(8,128)S(1)} %get-tuple-element.45), channel_id=1, source_target_pairs={{0,1},{1,0},{2,3},{3,2},{4,5},{5,4},{6,7},{7,6},{8,9},{9,8},{10,11... | collective-permute-start | bytes 2359304 | tf_op jit(solution)/shard_map/ppermute | solution.py:28
  80.7 8.6 %collective-permute-start.6 = (f32[256,512]{1,0:T(8,128)S(1)}, f32[256,512]{1,0:T(8,128)S(1)}, u32[]{:S(2)}, u32[]{:S(2)}) collective-permute-start(f32[256,512]{1,0:T(8,128)S(1)} %get-tuple-element.61.for_y_in), channel_id=1, source_target_pairs={{0,1},{2,3},{4,5},{6,7},{8,9},{10,11},{12,13},{14,15},{16,17},{18,... | collective-permute-start | bytes 1572872 | tf_op jit(solution)/shard_map/ppermute | solution.py:33
  86.1 18.1 %collective-permute-start.8 = (f32[256,512]{1,0:T(8,128)S(1)}, f32[256,512]{1,0:T(8,128)S(1)}, u32[]{:S(2)}, u32[]{:S(2)}) collective-permute-start(f32[256,512]{1,0:T(8,128)S(1)} %get-tuple-element.63), channel_id=1, source_target_pairs={{0,2},{1,511},{2,4},{3,1},{4,6},{5,3},{6,8},{7,5},{8,10},{9,7},{10... | collective-permute-start | bytes 1572872 | tf_op jit(solution)/shard_map/ppermute | solution.py:23
  88.0 16.2 %collective-permute-start.9 = (f32[256,512]{1,0:T(8,128)S(1)}, f32[256,512]{1,0:T(8,128)S(1)}, u32[]{:S(2)}, u32[]{:S(2)}) collective-permute-start(f32[256,512]{1,0:T(8,128)S(1)} %get-tuple-element.64), channel_id=1, source_target_pairs={{1,0},{3,2},{5,4},{7,6},{9,8},{11,10},{13,12},{15,14},{17,16},{19,... | collective-permute-start | bytes 1572872 | tf_op jit(solution)/shard_map/ppermute | solution.py:33
  89.5 17.6 %collective-permute-start.7 = (f32[256,512]{1,0:T(8,128)S(1)}, f32[256,512]{1,0:T(8,128)S(1)}, u32[]{:S(2)}, u32[]{:S(2)}) collective-permute-start(f32[256,512]{1,0:T(8,128)S(1)} %add_add_fusion.2), channel_id=1, source_target_pairs={{0,510},{1,3},{2,0},{3,5},{4,2},{5,7},{6,4},{7,9},{8,6},{9,11},{10... | collective-permute-start | bytes 1572872 | tf_op jit(solution)/shard_map/ppermute | solution.py:18
  104.3 16.5 %collective-permute-start.10 = (f32[256,512]{1,0:T(8,128)S(1)}, f32[256,512]{1,0:T(8,128)S(1)}, u32[]{:S(2)}, u32[]{:S(2)}) collective-permute-start(f32[256,512]{1,0:T(8,128)S(1)} %add_add_fusion), channel_id=1, source_target_pairs={{0,2},{1,511},{2,4},{3,1},{4,6},{5,3},{6,8},{7,5},{8,10},{9,7},{10... | collective-permute-start | bytes 1572872 | tf_op jit(solution)/shard_map/ppermute | solution.py:23

commit v5 on v4

--- a/solution.py
+++ b/solution.py
@@ -18,9 +18,9 @@
     return lax.ppermute(value, "blk", even_odd(n, -2, 2))
 
 
-def push(value):
-    n = lax.axis_size("blk")
-    return lax.ppermute(value, "blk", even_odd(n, 2, -2))
+def push(value, chips=1):
+    n = lax.axis_size("blk")
+    return lax.ppermute(value, "blk", even_odd(n, 2 * chips, -2 * chips))
 
 
 def swap(value):
@@ -179,14 +179,15 @@
     rows, dim = embeddings.shape
     cut = TOP + rows // 2
     sums = (CLUSTERS, rows)
-    even = swap((lax.axis_index("blk") % 2).astype(jnp.int32)[None])
+    even = (1 - lax.axis_index("blk") % 2).astype(jnp.int32)[None]
     own = pack(embeddings, labels)
-    own, even = lax.optimization_barrier((own, even))
 
     b2 = pull(own)
     bm2 = push(own)
     (own_0,) = call(self_body, [sums], own, moved=4 * own.size)
     b2, own_0 = lax.optimization_barrier((b2, own_0))
+    own_2, for_2 = call(pair_body, [sums] * 2, own, b2, moved=8 * own.size)
+    b2, own_2, for_2 = lax.optimization_barrier((b2, own_2, for_2))
     b4 = pull(b2)
 
     b2, bm2 = lax.optimization_barrier((b2, bm2))
@@ -194,12 +195,9 @@
         choose_body, [(cut, dim), (rows + TOP - cut, dim)], even, b2, bm2, moved=8 * own.size
     )
     y = swap(y_top), swap(y_end)
-    own_2, for_2 = call(pair_body, [sums] * 2, own, b2, moved=8 * own.size)
     for_m2, for_2_m2 = call(pair_body, [sums] * 2, bm2, b2, moved=8 * own.size)
 
-    y, own_2, for_2, for_m2, for_2_m2 = lax.optimization_barrier(
-        (y, own_2, for_2, for_m2, for_2_m2)
-    )
+    y, for_m2, for_2_m2 = lax.optimization_barrier((y, for_m2, for_2_m2))
     own_y, for_m2_y, for_2_y, for_y = call(
         visitor_body, [sums] * 4, even, own, bm2, b2, *y, moved=8 * own.size
     )
@@ -211,12 +209,14 @@
     for_m2_4, for_4, for_y = call(
         late_body, [sums] * 3, even, bm2, b4, *y, for_y, moved=16 * own.size
     )
-    back_4 = push(for_4)
+    home_4 = push(for_4, chips=2)
     home_m2 = pull(for_m2 + for_m2_y + for_m2_4 + back_m2)
     back_2 = give(for_y, 1)
-    back_4, back_2, for_2 = lax.optimization_barrier((back_4, back_2, for_2 + for_2_m2 + for_2_y))
-    home_2 = push(for_2 + back_2 + back_4)
-    return (own_0 + own_2 + own_y + home_m2 + home_2).T
+    home_2 = push(for_2 + for_2_m2 + for_2_y + back_2)
+    own, home_m2, home_2 = lax.optimization_barrier(
+        (own_0 + own_2 + own_y + home_4, home_m2, home_2)
+    )
+    return (own + home_m2 + home_2).T
 
 
 def solution(mesh):

time: 123 us -> 131 us (1.065)
  the two profiles are of different devices: /device:TPU:0 before, /device:TPU:1 now
where the time goes in v5:
time: 131 us; the launch traced here: 130 us
  starting transfers between devices  56.8 us (43%)
  waiting for transfers between devices  38.7 us (30%)
  Pallas kernels  30.8 us (24%)
  local copies, waits for them, and re-layouts  2.59 us (2%)
    pallas_call x6, Pallas kernels, call(): pl.pallas_call(body, out_shape=[pltpu.VMEM(shape, jnp.float32) for shape...  28.2 us
    ppermute x3, starting transfers between devices, push(): return lax.ppermute(value, 'blk', even_odd(n, 2 * chips, -2 * chips))  24.9 us
    ppermute x2, starting transfers between devices, swap(): return lax.ppermute(value, 'blk', even_odd(n, 1, -1))  19.7 us
    ppermute x3, waiting for transfers between devices, push(): return lax.ppermute(value, 'blk', even_odd(n, 2 * chips, -2 * chips))  19.6 us
    ppermute x3, waiting for transfers between devices, pull(): return lax.ppermute(value, 'blk', even_odd(n, -2, 2))  19 us
    ppermute x3, starting transfers between devices, pull(): return lax.ppermute(value, 'blk', even_odd(n, -2, 2))  8.34 us
    ppermute x2, starting transfers between devices, give(): return lax.ppermute(value, 'blk', [(i, i ^ 1) for i in range(core, n, 2)])  3.96 us
  transfers between devices with their start and end apart: 10, of which 4 were waited for; matrix products, arithmetic and copies ran while one was open for 1% of the time, Pallas kernels for 22%

profile of v5, /device:TPU:1, one launch (start us, length us, event | category | flops | bytes accessed | tf_op | source)
XLA Modules:
  0.0 130.0 jit_solution(2627350862138472148)
XLA Ops:
  0.0 2.6 %shard_map.28.own_ref.left_ref = f32[520,768]{1,0:T(8,128)} custom-call(f32[512,768]{1,0:T(8,128)} %embeddings_ref.1, s32[1,512]{1,0:T(1,128)} %bitcast.4), custom_call_target="tpu_custom_call" | custom-call | tf_op jit(solution)/shard_map/pallas_call | solution.py:60
  2.6 4.4 %collective-permute-start = (f32[520,768]{1,0:T(8,128)}, f32[520,768]{1,0:T(8,128)S(1)}, u32[]{:S(2)}, u32[]{:S(2)}) collective-permute-start(f32[520,768]{1,0:T(8,128)} %shard_map.28.own_ref.left_ref), channel_id=1, source_target_pairs={{0,510},{1,3},{2,0},{3,5},{4,2},{5,7},{6,4},{7,9},{8,6},{9,11},{10... | collective-permute-start | bytes 4792328 | tf_op jit(solution)/shard_map/ppermute | solution.py:18
  7.0 14.1 %collective-permute-start.2 = (f32[520,768]{1,0:T(8,128)}, f32[520,768]{1,0:T(8,128)S(1)}, u32[]{:S(2)}, u32[]{:S(2)}) collective-permute-start(f32[520,768]{1,0:T(8,128)} %shard_map.28.own_ref.left_ref), channel_id=1, source_target_pairs={{0,2},{1,511},{2,4},{3,1},{4,6},{5,3},{6,8},{7,5},{8,10},{9,7},{10... | collective-permute-start | bytes 4792328 | tf_op jit(solution)/shard_map/ppermute | solution.py:23
  21.1 4.4 %shard_map.29 = f32[256,512]{1,0:T(8,128)S(1)} custom-call(f32[520,768]{1,0:T(8,128)} %shard_map.28.own_ref.left_ref), custom_call_target="tpu_custom_call" | custom-call | flops 1000 | bytes 1597440 | tf_op jit(solution)/shard_map/pallas_call | solution.py:168
  25.6 19.0 %collective-permute-done.right_ref.b2_ref = f32[520,768]{1,0:T(8,128)S(1)} collective-permute-done((f32[520,768]{1,0:T(8,128)}, f32[520,768]{1,0:T(8,128)S(1)}, u32[]{:S(2)}, u32[]{:S(2)}) %collective-permute-start) | collective-permute-done | bytes 1597472 | tf_op jit(solution)/shard_map/ppermute | solution.py:18
  44.6 4.7 %shard_map.30 = (f32[256,512]{1,0:T(8,128)S(1)}, f32[256,512]{1,0:T(8,128)S(1)}) custom-call(f32[520,768]{1,0:T(8,128)} %shard_map.28.own_ref.left_ref, f32[520,768]{1,0:T(8,128)S(1)} %collective-permute-done.right_ref.b2_ref), custom_call_target="tpu_custom_call" | custom-call | flops 1000 | bytes 3194880 | tf_op jit(solution)/shard_map/pallas_call | solution.py:168
  49.3 0.8 copy-done.2
  50.1 0.8 copy-done.4
  50.9 1.9 %collective-permute-start.1 = (f32[520,768]{1,0:T(8,128)S(1)}, f32[520,768]{1,0:T(8,128)}, u32[]{:S(2)}, u32[]{:S(2)}) collective-permute-start(f32[520,768]{1,0:T(8,128)S(1)} %collective-permute-done.right_ref.b2_ref), channel_id=1, source_target_pairs={{0,510},{1,3},{2,0},{3,5},{4,2},{5,7},{6,4},{7,9},{8,6},{9,11},{10... | collective-permute-start | bytes 4792328 | tf_op jit(solution)/shard_map/ppermute | solution.py:18
  52.8 2.5 %collective-permute-done.2.bm2_ref.left_ref = f32[520,768]{1,0:T(8,128)S(1)} collective-permute-done((f32[520,768]{1,0:T(8,128)}, f32[520,768]{1,0:T(8,128)S(1)}, u32[]{:S(2)}, u32[]{:S(2)}) %collective-permute-start.2) | collective-permute-done | bytes 1597472 | tf_op jit(solution)/shard_map/ppermute | solution.py:23
  55.5 17.6 %collective-permute-start.3 = (f32[264,768]{1,0:T(8,128)S(1)}, f32[264,768]{1,0:T(8,128)S(1)}, u32[]{:S(2)}, u32[]{:S(2)}) collective-permute-start(f32[264,768]{1,0:T(8,128)S(1)} %get-tuple-element.45), channel_id=1, source_target_pairs={{0,1},{1,0},{2,3},{3,2},{4,5},{5,4},{6,7},{7,6},{8,9},{9,8},{10,11... | collective-permute-start | bytes 2433032 | tf_op jit(solution)/shard_map/ppermute | solution.py:28
  73.1 2.1 %collective-permute-start.4 = (f32[256,768]{1,0:T(8,128)S(1)}, f32[256,768]{1,0:T(8,128)S(1)}, u32[]{:S(2)}, u32[]{:S(2)}) collective-permute-start(f32[256,768]{1,0:T(8,128)S(1)} %get-tuple-element.46), channel_id=1, source_target_pairs={{0,1},{1,0},{2,3},{3,2},{4,5},{5,4},{6,7},{7,6},{8,9},{9,8},{10,11... | collective-permute-start | bytes 2359304 | tf_op jit(solution)/shard_map/ppermute | solution.py:28
  75.2 3.3 %shard_map.32 = (f32[256,512]{1,0:T(8,128)S(1)}, f32[256,512]{1,0:T(8,128)S(1)}) custom-call(f32[520,768]{1,0:T(8,128)S(1)} %collective-permute-done.2.bm2_ref.left_ref, f32[520,768]{1,0:T(8,128)S(1)} %collective-permute-done.right_ref.b2_ref), custom_call_target="tpu_custom_call" | custom-call | flops 1000 | bytes 3194880 | tf_op jit(solution)/shard_map/pallas_call | solution.py:168
  78.5 7.7 %shard_map.33 = (f32[256,512]{1,0:T(8,128)S(1)}, f32[256,512]{1,0:T(8,128)S(1)}, f32[256,512]{1,0:T(8,128)S(1)}, f32[256,512]{1,0:T(8,128)S(1)}) custom-call(s32[1]{0:T(128)} %bitcast.1.even_ref, f32[520,768]{1,0:T(8,128)} %shard_map.28.own_ref.left_ref, f32[520,768]{1,0:T(8,128)S(1)} %collective-permute-done.2.bm2_ref.left_ref, ...), custom_call_target="tpu_custom_call" | custom-call | flops 1000 | bytes 3194880 | tf_op jit(solution)/shard_map/pallas_call | solution.py:168
  86.2 1.5 %collective-permute-start.6 = (f32[256,512]{1,0:T(8,128)S(1)}, f32[256,512]{1,0:T(8,128)S(1)}, u32[]{:S(2)}, u32[]{:S(2)}) collective-permute-start(f32[256,512]{1,0:T(8,128)S(1)} %get-tuple-element.57.for_y_in), channel_id=1, source_target_pairs={{0,1},{2,3},{4,5},{6,7},{8,9},{10,11},{12,13},{14,15},{16,17},{18,... | collective-permute-start | bytes 1572872 | tf_op jit(solution)/shard_map/ppermute | solution.py:33
  87.7 8.0 %shard_map.34 = (f32[256,512]{1,0:T(8,128)S(1)}, f32[256,512]{1,0:T(8,128)S(1)}, f32[256,512]{1,0:T(8,128)S(1)}) custom-call(s32[1]{0:T(128)} %bitcast.1.even_ref, f32[520,768]{1,0:T(8,128)S(1)} %collective-permute-done.2.bm2_ref.left_ref, f32[520,768]{1,0:T(8,128)} %collective-permute-done.1.b4_ref, f32[264,768]{1,0:T(8,128)S(1)} %collective-permute-done.3.y_top_ref, ...), custom_call_target="tpu_custom_call" | custom-call | flops 1000 | bytes 6389760 | tf_op jit(solution)/shard_map/pallas_call | solution.py:168
  95.8 2.4 %collective-permute-start.8 = (f32[256,512]{1,0:T(8,128)S(1)}, f32[256,512]{1,0:T(8,128)S(1)}, u32[]{:S(2)}, u32[]{:S(2)}) collective-permute-start(f32[256,512]{1,0:T(8,128)S(1)} %get-tuple-element.65), channel_id=1, source_target_pairs={{1,0},{3,2},{5,4},{7,6},{9,8},{11,10},{13,12},{15,14},{17,16},{19,... | collective-permute-start | bytes 1572872 | tf_op jit(solution)/shard_map/ppermute | solution.py:33
  98.5 2.1 %collective-permute-start.7 = (f32[256,512]{1,0:T(8,128)S(1)}, f32[256,512]{1,0:T(8,128)S(1)}, u32[]{:S(2)}, u32[]{:S(2)}) collective-permute-start(f32[256,512]{1,0:T(8,128)S(1)} %add_add_fusion.1), channel_id=1, source_target_pairs={{0,510},{1,3},{2,0},{3,5},{4,2},{5,7},{6,4},{7,9},{8,6},{9,11},{10... | collective-permute-start | bytes 1572872 | tf_op jit(solution)/shard_map/ppermute | solution.py:18
  100.5 8.6 %collective-permute-start.5 = (f32[256,512]{1,0:T(8,128)S(1)}, f32[256,512]{1,0:T(8,128)S(1)}, u32[]{:S(2)}, u32[]{:S(2)}) collective-permute-start(f32[256,512]{1,0:T(8,128)S(1)} %get-tuple-element.58), channel_id=1, source_target_pairs={{0,4},{1,509},{2,6},{3,511},{4,8},{5,1},{6,10},{7,3},{8,12},{9,5},... | collective-permute-start | bytes 1572872 | tf_op jit(solution)/shard_map/ppermute | solution.py:23
  109.4 2.1 %collective-permute-start.9 = (f32[256,512]{1,0:T(8,128)S(1)}, f32[256,512]{1,0:T(8,128)S(1)}, u32[]{:S(2)}, u32[]{:S(2)}) collective-permute-start(f32[256,512]{1,0:T(8,128)S(1)} %add_add_fusion), channel_id=1, source_target_pairs={{0,2},{1,511},{2,4},{3,1},{4,6},{5,3},{6,8},{7,5},{8,10},{9,7},{10... | collective-permute-start | bytes 1572872 | tf_op jit(solution)/shard_map/ppermute | solution.py:23
  111.5 11.7 %collective-permute-done.5 = f32[256,512]{1,0:T(8,128)S(1)} collective-permute-done((f32[256,512]{1,0:T(8,128)S(1)}, f32[256,512]{1,0:T(8,128)S(1)}, u32[]{:S(2)}, u32[]{:S(2)}) %collective-permute-start.5) | collective-permute-done | bytes 524320 | tf_op jit(solution)/shard_map/ppermute | solution.py:23
  123.2 0.2 add_add_fusion.2
  123.5 5.4 %collective-permute-done.9 = f32[256,512]{1,0:T(8,128)S(1)} collective-permute-done((f32[256,512]{1,0:T(8,128)S(1)}, f32[256,512]{1,0:T(8,128)S(1)}, u32[]{:S(2)}, u32[]{:S(2)}) %collective-permute-start.9) | collective-permute-done | bytes 524320 | tf_op jit(solution)/shard_map/ppermute | solution.py:23
  129.0 1.0 copy.3
  (20 shorter events, 0.7 us)
Async XLA Ops:
  2.6 42.0 %collective-permute-start = (f32[520,768]{1,0:T(8,128)}, f32[520,768]{1,0:T(8,128)S(1)}, u32[]{:S(2)}, u32[]{:S(2)}) collective-permute-start(f32[520,768]{1,0:T(8,128)} %shard_map.28.own_ref.left_ref), channel_id=1, source_target_pairs={{0,510},{1,3},{2,0},{3,5},{4,2},{5,7},{6,4},{7,9},{8,6},{9,11},{10... | collective-permute-start | bytes 4792328 | tf_op jit(solution)/shard_map/ppermute | solution.py:18
  7.0 48.4 %collective-permute-start.2 = (f32[520,768]{1,0:T(8,128)}, f32[520,768]{1,0:T(8,128)S(1)}, u32[]{:S(2)}, u32[]{:S(2)}) collective-permute-start(f32[520,768]{1,0:T(8,128)} %shard_map.28.own_ref.left_ref), channel_id=1, source_target_pairs={{0,2},{1,511},{2,4},{3,1},{4,6},{5,3},{6,8},{7,5},{8,10},{9,7},{10... | collective-permute-start | bytes 4792328 | tf_op jit(solution)/shard_map/ppermute | solution.py:23
  25.6 25.4 %copy-start = (f32[256,512]{1,0:T(8,128)}, f32[256,512]{1,0:T(8,128)S(1)}, u32[]{:S(2)}) copy-start(f32[256,512]{1,0:T(8,128)S(1)} %shard_map.29) | copy-start | bytes 1572868
  49.3 0.8 copy-start.2
  50.1 0.8 copy-start.4
  50.9 36.8 %collective-permute-start.1 = (f32[520,768]{1,0:T(8,128)S(1)}, f32[520,768]{1,0:T(8,128)}, u32[]{:S(2)}, u32[]{:S(2)}) collective-permute-start(f32[520,768]{1,0:T(8,128)S(1)} %collective-permute-done.right_ref.b2_ref), channel_id=1, source_target_pairs={{0,510},{1,3},{2,0},{3,5},{4,2},{5,7},{6,4},{7,9},{8,6},{9,11},{10... | collective-permute-start | bytes 4792328 | tf_op jit(solution)/shard_map/ppermute | solution.py:18
  55.5 23.0 %collective-permute-start.3 = (f32[264,768]{1,0:T(8,128)S(1)}, f32[264,768]{1,0:T(8,128)S(1)}, u32[]{:S(2)}, u32[]{:S(2)}) collective-permute-start(f32[264,768]{1,0:T(8,128)S(1)} %get-tuple-element.45), channel_id=1, source_target_pairs={{0,1},{1,0},{2,3},{3,2},{4,5},{5,4},{6,7},{7,6},{8,9},{9,8},{10,11... | collective-permute-start | bytes 2433032 | tf_op jit(solution)/shard_map/ppermute | solution.py:28
  73.1 5.4 %collective-permute-start.4 = (f32[256,768]{1,0:T(8,128)S(1)}, f32[256,768]{1,0:T(8,128)S(1)}, u32[]{:S(2)}, u32[]{:S(2)}) collective-permute-start(f32[256,768]{1,0:T(8,128)S(1)} %get-tuple-element.46), channel_id=1, source_target_pairs={{0,1},{1,0},{2,3},{3,2},{4,5},{5,4},{6,7},{7,6},{8,9},{9,8},{10,11... | collective-permute-start | bytes 2359304 | tf_op jit(solution)/shard_map/ppermute | solution.py:28
  86.2 12.0 %collective-permute-start.6 = (f32[256,512]{1,0:T(8,128)S(1)}, f32[256,512]{1,0:T(8,128)S(1)}, u32[]{:S(2)}, u32[]{:S(2)}) collective-permute-start(f32[256,512]{1,0:T(8,128)S(1)} %get-tuple-element.57.for_y_in), channel_id=1, source_target_pairs={{0,1},{2,3},{4,5},{6,7},{8,9},{10,11},{12,13},{14,15},{16,17},{18,... | collective-permute-start | bytes 1572872 | tf_op jit(solution)/shard_map/ppermute | solution.py:33
  95.8 13.4 %copy-start.5 = (f32[256,512]{1,0:T(8,128)S(1)}, f32[256,512]{1,0:T(8,128)}, u32[]{:S(2)}) copy-start(f32[256,512]{1,0:T(8,128)} %copy-done.4) | copy-start | bytes 1572868
  95.8 13.4 %collective-permute-start.8 = (f32[256,512]{1,0:T(8,128)S(1)}, f32[256,512]{1,0:T(8,128)S(1)}, u32[]{:S(2)}, u32[]{:S(2)}) collective-permute-start(f32[256,512]{1,0:T(8,128)S(1)} %get-tuple-element.65), channel_id=1, source_target_pairs={{1,0},{3,2},{5,4},{7,6},{9,8},{11,10},{13,12},{15,14},{17,16},{19,... | collective-permute-start | bytes 1572872 | tf_op jit(solution)/shard_map/ppermute | solution.py:33
  98.5 24.8 %copy-start.1 = (f32[256,512]{1,0:T(8,128)S(1)}, f32[256,512]{1,0:T(8,128)}, u32[]{:S(2)}) copy-start(f32[256,512]{1,0:T(8,128)} %copy-done) | copy-start | bytes 1572868
  98.5 24.8 %copy-start.3 = (f32[256,512]{1,0:T(8,128)S(1)}, f32[256,512]{1,0:T(8,128)}, u32[]{:S(2)}) copy-start(f32[256,512]{1,0:T(8,128)} %copy-done.2) | copy-start | bytes 1572868
  98.5 25.0 %collective-permute-start.7 = (f32[256,512]{1,0:T(8,128)S(1)}, f32[256,512]{1,0:T(8,128)S(1)}, u32[]{:S(2)}, u32[]{:S(2)}) collective-permute-start(f32[256,512]{1,0:T(8,128)S(1)} %add_add_fusion.1), channel_id=1, source_target_pairs={{0,510},{1,3},{2,0},{3,5},{4,2},{5,7},{6,4},{7,9},{8,6},{9,11},{10... | collective-permute-start | bytes 1572872 | tf_op jit(solution)/shard_map/ppermute | solution.py:18
  100.5 22.7 %collective-permute-start.5 = (f32[256,512]{1,0:T(8,128)S(1)}, f32[256,512]{1,0:T(8,128)S(1)}, u32[]{:S(2)}, u32[]{:S(2)}) collective-permute-start(f32[256,512]{1,0:T(8,128)S(1)} %get-tuple-element.58), channel_id=1, source_target_pairs={{0,4},{1,509},{2,6},{3,511},{4,8},{5,1},{6,10},{7,3},{8,12},{9,5},... | collective-permute-start | bytes 1572872 | tf_op jit(solution)/shard_map/ppermute | solution.py:23
  109.4 19.4 %collective-permute-start.9 = (f32[256,512]{1,0:T(8,128)S(1)}, f32[256,512]{1,0:T(8,128)S(1)}, u32[]{:S(2)}, u32[]{:S(2)}) collective-permute-start(f32[256,512]{1,0:T(8,128)S(1)} %add_add_fusion), channel_id=1, source_target_pairs={{0,2},{1,511},{2,4},{3,1},{4,6},{5,3},{6,8},{7,5},{8,10},{9,7},{10... | collective-permute-start | bytes 1572872 | tf_op jit(solution)/shard_map/ppermute | solution.py:23

commit v6 on v4

--- a/solution.py
+++ b/solution.py
@@ -39,8 +39,12 @@
 
 
 def unpack(message):
-    rows = message.shape[0] - TOP
-    return message[TOP:, :], one_hot(message[0:1, :rows])
+    rows = message[TOP:, :]
+    high = rows.astype(jnp.bfloat16)
+    low = (rows - high.astype(jnp.float32)).astype(jnp.bfloat16)
+    kept = high.astype(jnp.float32) + low.astype(jnp.float32)
+    norms = jnp.sum(kept * kept, axis=1, keepdims=True)
+    return (high, low, norms), one_hot(message[0:1, : rows.shape[0]])
 
 
 def pack_body(embeddings_ref, labels_ref, message_ref, held, done):
@@ -71,15 +75,18 @@
 
 
 def kernel_tile(left, right):
-    left_norms = jnp.sum(left * left, axis=1, keepdims=True)
-    right_norms = jnp.sum(right * right, axis=1, keepdims=True)
-    right_norms = jnp.transpose(jnp.broadcast_to(right_norms, (right.shape[0], 128)))[0:1, :]
-    inner = lax.dot_general(
-        left,
-        right,
-        (((1,), (1,)), ((), ())),
-        precision=lax.Precision.HIGHEST,
-        preferred_element_type=jnp.float32,
+    high, low, left_norms = left
+    left = jnp.concatenate([high, low], axis=1)
+    high, low, right_norms = right
+    right_norms = jnp.transpose(jnp.broadcast_to(right_norms, (high.shape[0], 128)))[0:1, :]
+    inner = sum(
+        lax.dot_general(
+            left,
+            jnp.concatenate(parts, axis=1),
+            (((1,), (1,)), ((), ())),
+            preferred_element_type=jnp.float32,
+        )
+        for parts in ((low, high), (high, low))
     )
     return jnp.exp(-(left_norms + right_norms - 2.0 * inner)).astype(jnp.bfloat16)
 
@@ -99,12 +106,16 @@
     own_out[...] = left_sums(own_hot, kernel_tile(own, own))
 
 
-def pair_body(left_ref, right_ref, left_out, right_out):
-    left, left_hot = unpack(left_ref)
-    right, right_hot = unpack(right_ref)
-    kernel = kernel_tile(left, right)
-    left_out[...] = left_sums(right_hot, kernel)
-    right_out[...] = right_sums(left_hot, kernel)
+def pair_body(own_ref, bm2_ref, b2_ref, own_out, for_m2_out, for_2_out):
+    b2, b2_hot = unpack(b2_ref)
+    bm2, bm2_hot = unpack(bm2_ref)
+    kernel = kernel_tile(bm2, b2)
+    for_m2_out[...] = left_sums(b2_hot, kernel)
+    for_2_out[...] = right_sums(bm2_hot, kernel)
+    own, own_hot = unpack(own_ref)
+    kernel = kernel_tile(own, b2)
+    own_out[...] = left_sums(b2_hot, kernel)
+    for_2_out[...] += right_sums(own_hot, kernel)
 
 
 def visitor_body(
@@ -179,9 +190,8 @@
     rows, dim = embeddings.shape
     cut = TOP + rows // 2
     sums = (CLUSTERS, rows)
-    even = swap((lax.axis_index("blk") % 2).astype(jnp.int32)[None])
-    own = pack(embeddings, labels)
-    own, even = lax.optimization_barrier((own, even))
+    even = (1 - lax.axis_index("blk") % 2).astype(jnp.int32)[None]
+    own, even = lax.optimization_barrier((pack(embeddings, labels), even))
 
     b2 = pull(own)
     bm2 = push(own)
@@ -194,12 +204,9 @@
         choose_body, [(cut, dim), (rows + TOP - cut, dim)], even, b2, bm2, moved=8 * own.size
     )
     y = swap(y_top), swap(y_end)
-    own_2, for_2 = call(pair_body, [sums] * 2, own, b2, moved=8 * own.size)
-    for_m2, for_2_m2 = call(pair_body, [sums] * 2, bm2, b2, moved=8 * own.size)
-
-    y, own_2, for_2, for_m2, for_2_m2 = lax.optimization_barrier(
-        (y, own_2, for_2, for_m2, for_2_m2)
-    )
+    own_2, for_m2, for_2 = call(pair_body, [sums] * 3, own, bm2, b2, moved=16 * own.size)
+
+    y, own_2, for_m2, for_2 = lax.optimization_barrier((y, own_2, for_m2, for_2))
     own_y, for_m2_y, for_2_y, for_y = call(
         visitor_body, [sums] * 4, even, own, bm2, b2, *y, moved=8 * own.size
     )
@@ -214,7 +221,7 @@
     back_4 = push(for_4)
     home_m2 = pull(for_m2 + for_m2_y + for_m2_4 + back_m2)
     back_2 = give(for_y, 1)
-    back_4, back_2, for_2 = lax.optimization_barrier((back_4, back_2, for_2 + for_2_m2 + for_2_y))
+    back_4, back_2, for_2 = lax.optimization_barrier((back_4, back_2, for_2 + for_2_y))
     home_2 = push(for_2 + back_2 + back_4)
     return (own_0 + own_2 + own_y + home_m2 + home_2).T
 

time: 123 us -> 114 us (0.927)
  Pallas kernels: 26.2 us -> 18.4 us
  starting transfers between devices: 45.4 us -> 43 us
  waiting for transfers between devices: 48.5 us -> 50.4 us
    pallas_call x6 -> x5, Pallas kernels: 24.8 us -> 17 us  [call(): pl.pallas_call(body, out_shape=[pltpu.VMEM(shape, jnp.float32) for shape...]
    ppermute x3 -> x2, starting transfers between devices: 7.22 us -> 4.33 us  [swap(): return lax.ppermute(value, 'blk', even_odd(n, 1, -1))]
    ppermute x3, waiting for transfers between devices: 29.6 us -> 32.2 us  [pull(): return lax.ppermute(value, 'blk', even_odd(n, -2, 2))]
  transfers between devices with their start and end apart: 11 -> 10, of which waited for: 4 -> 5; matrix products, arithmetic and copies ran while one was open for 0% -> 0% of each run, Pallas kernels for 21% -> 15%
where the time goes in v6:
time: 114 us
  waiting for transfers between devices  50.4 us (44%)
  starting transfers between devices  43 us (38%)
  Pallas kernels  18.4 us (16%)
    ppermute x3, waiting for transfers between devices, pull(): return lax.ppermute(value, 'blk', even_odd(n, -2, 2))  32.2 us
    ppermute x3, starting transfers between devices, pull(): return lax.ppermute(value, 'blk', even_odd(n, -2, 2))  30.3 us
    ppermute x3, waiting for transfers between devices, push(): return lax.ppermute(value, 'blk', even_odd(n, 2, -2))  18.2 us
    pallas_call x5, Pallas kernels, call(): pl.pallas_call(body, out_shape=[pltpu.VMEM(shape, jnp.float32) for shape...  17 us
    ppermute x3, starting transfers between devices, push(): return lax.ppermute(value, 'blk', even_odd(n, 2, -2))  5.76 us
    ppermute x2, starting transfers between devices, swap(): return lax.ppermute(value, 'blk', even_odd(n, 1, -1))  4.33 us
    ppermute x2, starting transfers between devices, give(): return lax.ppermute(value, 'blk', [(i, i ^ 1) for i in range(core, n, 2)])  2.61 us
  transfers between devices with their start and end apart: 10, of which 5 were waited for; matrix products, arithmetic and copies ran while one was open for 0% of the time, Pallas kernels for 15%

profile of v6, /device:TPU:0, one launch (start us, length us, event | category | flops | bytes accessed | tf_op | source)
XLA Modules:
  0.0 113.7 jit_solution(335041461542759717)
XLA Ops:
  0.0 1.4 %shard_map.28.own_ref = f32[520,768]{1,0:T(8,128)S(1)} custom-call(f32[512,768]{1,0:T(8,128)} %embeddings_ref.1, s32[1,512]{1,0:T(1,128)} %bitcast.4), custom_call_target="tpu_custom_call" | custom-call | tf_op jit(solution)/shard_map/pallas_call | solution.py:64
  1.4 10.7 %collective-permute-start = (f32[520,768]{1,0:T(8,128)S(1)}, f32[520,768]{1,0:T(8,128)S(1)}, u32[]{:S(2)}, u32[]{:S(2)}) collective-permute-start(f32[520,768]{1,0:T(8,128)S(1)} %shard_map.28.own_ref), channel_id=1, source_target_pairs={{0,510},{1,3},{2,0},{3,5},{4,2},{5,7},{6,4},{7,9},{8,6},{9,11},{10... | collective-permute-start | bytes 4792328 | tf_op jit(solution)/shard_map/ppermute | solution.py:18
  12.1 1.9 %collective-permute-start.1 = (f32[520,768]{1,0:T(8,128)S(1)}, f32[520,768]{1,0:T(8,128)S(1)}, u32[]{:S(2)}, u32[]{:S(2)}) collective-permute-start(f32[520,768]{1,0:T(8,128)S(1)} %shard_map.28.own_ref), channel_id=1, source_target_pairs={{0,2},{1,511},{2,4},{3,1},{4,6},{5,3},{6,8},{7,5},{8,10},{9,7},{10... | collective-permute-start | bytes 4792328 | tf_op jit(solution)/shard_map/ppermute | solution.py:23
  14.0 2.2 %shard_map.29 = f32[256,512]{1,0:T(8,128)S(1)} custom-call(f32[520,768]{1,0:T(8,128)S(1)} %shard_map.28.own_ref), custom_call_target="tpu_custom_call" | custom-call | flops 1000 | bytes 1597440 | tf_op jit(solution)/shard_map/pallas_call | solution.py:179
  16.3 30.3 %collective-permute-done.b2_ref = f32[520,768]{1,0:T(8,128)S(1)} collective-permute-done((f32[520,768]{1,0:T(8,128)S(1)}, f32[520,768]{1,0:T(8,128)S(1)}, u32[]{:S(2)}, u32[]{:S(2)}) %collective-permute-start) | collective-permute-done | bytes 1597472 | tf_op jit(solution)/shard_map/ppermute | solution.py:18
  46.6 9.8 %collective-permute-start.4 = (f32[520,768]{1,0:T(8,128)S(1)}, f32[520,768]{1,0:T(8,128)S(1)}, u32[]{:S(2)}, u32[]{:S(2)}) collective-permute-start(f32[520,768]{1,0:T(8,128)S(1)} %collective-permute-done.b2_ref), channel_id=1, source_target_pairs={{0,510},{1,3},{2,0},{3,5},{4,2},{5,7},{6,4},{7,9},{8,6},{9,11},{10... | collective-permute-start | bytes 4792328 | tf_op jit(solution)/shard_map/ppermute | solution.py:18
  56.6 1.9 %collective-permute-start.2 = (f32[264,768]{1,0:T(8,128)S(1)}, f32[264,768]{1,0:T(8,128)S(1)}, u32[]{:S(2)}, u32[]{:S(2)}) collective-permute-start(f32[264,768]{1,0:T(8,128)S(1)} %get-tuple-element.42), channel_id=1, source_target_pairs={{0,1},{1,0},{2,3},{3,2},{4,5},{5,4},{6,7},{7,6},{8,9},{9,8},{10,11... | collective-permute-start | bytes 2433032 | tf_op jit(solution)/shard_map/ppermute | solution.py:28
  58.5 2.4 %collective-permute-start.3 = (f32[256,768]{1,0:T(8,128)S(1)}, f32[256,768]{1,0:T(8,128)S(1)}, u32[]{:S(2)}, u32[]{:S(2)}) collective-permute-start(f32[256,768]{1,0:T(8,128)S(1)} %get-tuple-element.43), channel_id=1, source_target_pairs={{0,1},{1,0},{2,3},{3,2},{4,5},{5,4},{6,7},{7,6},{8,9},{9,8},{10,11... | collective-permute-start | bytes 2359304 | tf_op jit(solution)/shard_map/ppermute | solution.py:28
  60.9 4.7 %shard_map.31 = (f32[256,512]{1,0:T(8,128)S(1)}, f32[256,512]{1,0:T(8,128)S(1)}, f32[256,512]{1,0:T(8,128)S(1)}) custom-call(f32[520,768]{1,0:T(8,128)S(1)} %shard_map.28.own_ref, f32[520,768]{1,0:T(8,128)S(1)} %collective-permute-done.1.bm2_ref, f32[520,768]{1,0:T(8,128)S(1)} %collective-permute-done.b2_ref), custom_call_target="tpu_custom_call" | custom-call | flops 1000 | bytes 6389760 | tf_op jit(solution)/shard_map/pallas_call | solution.py:179
  65.7 7.4 %shard_map.32 = (f32[256,512]{1,0:T(8,128)S(1)}, f32[256,512]{1,0:T(8,128)S(1)}, f32[256,512]{1,0:T(8,128)S(1)}, f32[256,512]{1,0:T(8,128)S(1)}) custom-call(s32[1]{0:T(128)} %bitcast.1.even_ref, f32[520,768]{1,0:T(8,128)S(1)} %shard_map.28.own_ref, f32[520,768]{1,0:T(8,128)S(1)} %collective-permute-done.1.bm2_ref, ...), custom_call_target="tpu_custom_call" | custom-call | flops 1000 | bytes 3194880 | tf_op jit(solution)/shard_map/pallas_call | solution.py:179
  73.1 1.3 %collective-permute-start.5 = (f32[256,512]{1,0:T(8,128)S(1)}, f32[256,512]{1,0:T(8,128)S(1)}, u32[]{:S(2)}, u32[]{:S(2)}) collective-permute-start(f32[256,512]{1,0:T(8,128)S(1)} %get-tuple-element.58.for_y_in), channel_id=1, source_target_pairs={{0,1},{2,3},{4,5},{6,7},{8,9},{10,11},{12,13},{14,15},{16,17},{18,... | collective-permute-start | bytes 1572872 | tf_op jit(solution)/shard_map/ppermute | solution.py:33
  74.4 0.2 collective-permute-done.4.b4_ref
  74.6 2.5 %shard_map.33 = (f32[256,512]{1,0:T(8,128)S(1)}, f32[256,512]{1,0:T(8,128)S(1)}, f32[256,512]{1,0:T(8,128)S(1)}) custom-call(s32[1]{0:T(128)} %bitcast.1.even_ref, f32[520,768]{1,0:T(8,128)S(1)} %collective-permute-done.1.bm2_ref, f32[520,768]{1,0:T(8,128)S(1)} %collective-permute-done.4.b4_ref, f32[264,768]{1,0:T(8,128)S(1)} %collective-permute-done.2.y_top_ref, ...), custom_call_target="tpu_custom_call" | custom-call | flops 1000 | bytes 6389760 | tf_op jit(solution)/shard_map/pallas_call | solution.py:179
  77.2 1.9 %collective-permute-start.7 = (f32[256,512]{1,0:T(8,128)S(1)}, f32[256,512]{1,0:T(8,128)S(1)}, u32[]{:S(2)}, u32[]{:S(2)}) collective-permute-start(f32[256,512]{1,0:T(8,128)S(1)} %get-tuple-element.60), channel_id=1, source_target_pairs={{0,2},{1,511},{2,4},{3,1},{4,6},{5,3},{6,8},{7,5},{8,10},{9,7},{10... | collective-permute-start | bytes 1572872 | tf_op jit(solution)/shard_map/ppermute | solution.py:23
  79.1 1.3 %collective-permute-start.8 = (f32[256,512]{1,0:T(8,128)S(1)}, f32[256,512]{1,0:T(8,128)S(1)}, u32[]{:S(2)}, u32[]{:S(2)}) collective-permute-start(f32[256,512]{1,0:T(8,128)S(1)} %get-tuple-element.61), channel_id=1, source_target_pairs={{1,0},{3,2},{5,4},{7,6},{9,8},{11,10},{13,12},{15,14},{17,16},{19,... | collective-permute-start | bytes 1572872 | tf_op jit(solution)/shard_map/ppermute | solution.py:33
  80.4 0.2 add_add_fusion.1
  80.6 9.8 %collective-permute-start.6 = (f32[256,512]{1,0:T(8,128)S(1)}, f32[256,512]{1,0:T(8,128)S(1)}, u32[]{:S(2)}, u32[]{:S(2)}) collective-permute-start(f32[256,512]{1,0:T(8,128)S(1)} %add_add_fusion.1), channel_id=1, source_target_pairs={{0,510},{1,3},{2,0},{3,5},{4,2},{5,7},{6,4},{7,9},{8,6},{9,11},{10... | collective-permute-start | bytes 1572872 | tf_op jit(solution)/shard_map/ppermute | solution.py:18
  90.5 5.2 %collective-permute-done.7 = f32[256,512]{1,0:T(8,128)S(1)} collective-permute-done((f32[256,512]{1,0:T(8,128)S(1)}, f32[256,512]{1,0:T(8,128)S(1)}, u32[]{:S(2)}, u32[]{:S(2)}) %collective-permute-start.7) | collective-permute-done | bytes 524320 | tf_op jit(solution)/shard_map/ppermute | solution.py:23
  95.8 0.2 add_add_fusion
  95.9 1.9 %collective-permute-start.9 = (f32[256,512]{1,0:T(8,128)S(1)}, f32[256,512]{1,0:T(8,128)S(1)}, u32[]{:S(2)}, u32[]{:S(2)}) collective-permute-start(f32[256,512]{1,0:T(8,128)S(1)} %add_add_fusion), channel_id=1, source_target_pairs={{0,2},{1,511},{2,4},{3,1},{4,6},{5,3},{6,8},{7,5},{8,10},{9,7},{10... | collective-permute-start | bytes 1572872 | tf_op jit(solution)/shard_map/ppermute | solution.py:23
  97.8 1.6 %collective-permute-done.6 = f32[256,512]{1,0:T(8,128)S(1)} collective-permute-done((f32[256,512]{1,0:T(8,128)S(1)}, f32[256,512]{1,0:T(8,128)S(1)}, u32[]{:S(2)}, u32[]{:S(2)}) %collective-permute-start.6) | collective-permute-done | bytes 524320 | tf_op jit(solution)/shard_map/ppermute | solution.py:18
  99.4 13.0 %collective-permute-done.9 = f32[256,512]{1,0:T(8,128)S(1)} collective-permute-done((f32[256,512]{1,0:T(8,128)S(1)}, f32[256,512]{1,0:T(8,128)S(1)}, u32[]{:S(2)}, u32[]{:S(2)}) %collective-permute-start.9) | collective-permute-done | bytes 524320 | tf_op jit(solution)/shard_map/ppermute | solution.py:23
  112.4 0.3 add_bitcast_fusion
  112.7 1.0 copy.3
  (7 shorter events, 0.2 us)
Async XLA Ops:
  1.4 45.2 %collective-permute-start = (f32[520,768]{1,0:T(8,128)S(1)}, f32[520,768]{1,0:T(8,128)S(1)}, u32[]{:S(2)}, u32[]{:S(2)}) collective-permute-start(f32[520,768]{1,0:T(8,128)S(1)} %shard_map.28.own_ref), channel_id=1, source_target_pairs={{0,510},{1,3},{2,0},{3,5},{4,2},{5,7},{6,4},{7,9},{8,6},{9,11},{10... | collective-permute-start | bytes 4792328 | tf_op jit(solution)/shard_map/ppermute | solution.py:18
  12.1 44.3 %collective-permute-start.1 = (f32[520,768]{1,0:T(8,128)S(1)}, f32[520,768]{1,0:T(8,128)S(1)}, u32[]{:S(2)}, u32[]{:S(2)}) collective-permute-start(f32[520,768]{1,0:T(8,128)S(1)} %shard_map.28.own_ref), channel_id=1, source_target_pairs={{0,2},{1,511},{2,4},{3,1},{4,6},{5,3},{6,8},{7,5},{8,10},{9,7},{10... | collective-permute-start | bytes 4792328 | tf_op jit(solution)/shard_map/ppermute | solution.py:23
  46.6 28.0 %collective-permute-start.4 = (f32[520,768]{1,0:T(8,128)S(1)}, f32[520,768]{1,0:T(8,128)S(1)}, u32[]{:S(2)}, u32[]{:S(2)}) collective-permute-start(f32[520,768]{1,0:T(8,128)S(1)} %collective-permute-done.b2_ref), channel_id=1, source_target_pairs={{0,510},{1,3},{2,0},{3,5},{4,2},{5,7},{6,4},{7,9},{8,6},{9,11},{10... | collective-permute-start | bytes 4792328 | tf_op jit(solution)/shard_map/ppermute | solution.py:18
  56.6 9.1 %collective-permute-start.2 = (f32[264,768]{1,0:T(8,128)S(1)}, f32[264,768]{1,0:T(8,128)S(1)}, u32[]{:S(2)}, u32[]{:S(2)}) collective-permute-start(f32[264,768]{1,0:T(8,128)S(1)} %get-tuple-element.42), channel_id=1, source_target_pairs={{0,1},{1,0},{2,3},{3,2},{4,5},{5,4},{6,7},{7,6},{8,9},{9,8},{10,11... | collective-permute-start | bytes 2433032 | tf_op jit(solution)/shard_map/ppermute | solution.py:28
  58.5 7.2 %collective-permute-start.3 = (f32[256,768]{1,0:T(8,128)S(1)}, f32[256,768]{1,0:T(8,128)S(1)}, u32[]{:S(2)}, u32[]{:S(2)}) collective-permute-start(f32[256,768]{1,0:T(8,128)S(1)} %get-tuple-element.43), channel_id=1, source_target_pairs={{0,1},{1,0},{2,3},{3,2},{4,5},{5,4},{6,7},{7,6},{8,9},{9,8},{10,11... | collective-permute-start | bytes 2359304 | tf_op jit(solution)/shard_map/ppermute | solution.py:28
  73.1 7.3 %collective-permute-start.5 = (f32[256,512]{1,0:T(8,128)S(1)}, f32[256,512]{1,0:T(8,128)S(1)}, u32[]{:S(2)}, u32[]{:S(2)}) collective-permute-start(f32[256,512]{1,0:T(8,128)S(1)} %get-tuple-element.58.for_y_in), channel_id=1, source_target_pairs={{0,1},{2,3},{4,5},{6,7},{8,9},{10,11},{12,13},{14,15},{16,17},{18,... | collective-permute-start | bytes 1572872 | tf_op jit(solution)/shard_map/ppermute | solution.py:33
  77.2 18.6 %collective-permute-start.7 = (f32[256,512]{1,0:T(8,128)S(1)}, f32[256,512]{1,0:T(8,128)S(1)}, u32[]{:S(2)}, u32[]{:S(2)}) collective-permute-start(f32[256,512]{1,0:T(8,128)S(1)} %get-tuple-element.60), channel_id=1, source_target_pairs={{0,2},{1,511},{2,4},{3,1},{4,6},{5,3},{6,8},{7,5},{8,10},{9,7},{10... | collective-permute-start | bytes 1572872 | tf_op jit(solution)/shard_map/ppermute | solution.py:23
  79.1 16.7 %collective-permute-start.8 = (f32[256,512]{1,0:T(8,128)S(1)}, f32[256,512]{1,0:T(8,128)S(1)}, u32[]{:S(2)}, u32[]{:S(2)}) collective-permute-start(f32[256,512]{1,0:T(8,128)S(1)} %get-tuple-element.61), channel_id=1, source_target_pairs={{1,0},{3,2},{5,4},{7,6},{9,8},{11,10},{13,12},{15,14},{17,16},{19,... | collective-permute-start | bytes 1572872 | tf_op jit(solution)/shard_map/ppermute | solution.py:33
  80.6 18.8 %collective-permute-start.6 = (f32[256,512]{1,0:T(8,128)S(1)}, f32[256,512]{1,0:T(8,128)S(1)}, u32[]{:S(2)}, u32[]{:S(2)}) collective-permute-start(f32[256,512]{1,0:T(8,128)S(1)} %add_add_fusion.1), channel_id=1, source_target_pairs={{0,510},{1,3},{2,0},{3,5},{4,2},{5,7},{6,4},{7,9},{8,6},{9,11},{10... | collective-permute-start | bytes 1572872 | tf_op jit(solution)/shard_map/ppermute | solution.py:18
  95.9 16.5 %collective-permute-start.9 = (f32[256,512]{1,0:T(8,128)S(1)}, f32[256,512]{1,0:T(8,128)S(1)}, u32[]{:S(2)}, u32[]{:S(2)}) collective-permute-start(f32[256,512]{1,0:T(8,128)S(1)} %add_add_fusion), channel_id=1, source_target_pairs={{0,2},{1,511},{2,4},{3,1},{4,6},{5,3},{6,8},{7,5},{8,10},{9,7},{10... | collective-permute-start | bytes 1572872 | tf_op jit(solution)/shard_map/ppermute | solution.py:23

commit v7 on v6

v7 whole, which is shorter than its diff:
```python
import jax
import jax.numpy as jnp
from jax import lax
from jax.experimental import pallas as pl
from jax.experimental.pallas import tpu as pltpu
from jax.sharding import PartitionSpec as P

CLUSTERS = 256
ROWS = 512
DIM = 768
SUMS = ((CLUSTERS, ROWS), jnp.float32)
SPLIT = ((ROWS, 2 * DIM), jnp.bfloat16), ((ROWS, 128), jnp.float32)
TOP = 8


def even_odd(n, even, odd):
    return [(i, (i + (even if i % 2 == 0 else odd)) % n) for i in range(n)]


def pull(value):
    n = lax.axis_size("blk")
    return lax.ppermute(value, "blk", even_odd(n, -2, 2))


def push(value):
    n = lax.axis_size("blk")
    return lax.ppermute(value, "blk", even_odd(n, 2, -2))


def swap(value):
    n = lax.axis_size("blk")
    return lax.ppermute(value, "blk", even_odd(n, 1, -1))


def give(value, core):
    n = lax.axis_size("blk")
    return lax.ppermute(value, "blk", [(i, i ^ 1) for i in range(core, n, 2)])


def one_hot(labels):
    cluster = lax.broadcasted_iota(jnp.int32, (CLUSTERS, labels.shape[1]), 0)
    return jnp.where(cluster == labels.astype(jnp.int32), 1.0, 0.0).astype(jnp.bfloat16)


def labels_of(message_ref):
    return one_hot(message_ref[0:1, :ROWS])


def split(message, parts_out, norms_out):
    rows = message[TOP:, :]
    dim = rows.shape[1]
    high = rows.astype(jnp.bfloat16)
    low = (rows - high.astype(jnp.float32)).astype(jnp.bfloat16)
    kept = high.astype(jnp.float32) + low.astype(jnp.float32)
    parts_out[:, :dim] = high
    parts_out[:, dim:] = low
    norms_out[...] = jnp.broadcast_to(jnp.sum(kept * kept, axis=1, keepdims=True), norms_out.shape)


def pack_body(embeddings_ref, labels_ref, message_ref, held, done):
    rows = embeddings_ref.shape[0]
    copy = pltpu.make_async_copy(embeddings_ref, message_ref.at[pl.ds(TOP, rows)], done.at[0])
    copy.start()
    labels = pltpu.make_async_copy(labels_ref, held, done.at[1])
    labels.start()
    message_ref[:TOP, :] = jnp.zeros((TOP, message_ref.shape[1]), jnp.float32)
    labels.wait()
    message_ref[0:1, :rows] = held[...].astype(jnp.float32)
    copy.wait()


def pack(embeddings, labels):
    rows, dim = embeddings.shape
    return pl.pallas_call(
        pack_body,
        out_shape=pltpu.VMEM((TOP + rows, dim), jnp.float32),
        in_specs=[pl.BlockSpec(memory_space=pltpu.HBM)] * 2,
        out_specs=pl.BlockSpec(memory_space=pltpu.VMEM),
        scratch_shapes=[pltpu.VMEM((1, rows), jnp.int32), pltpu.SemaphoreType.DMA((2,))],
        compiler_params=pltpu.CompilerParams(vmem_limit_bytes=16 * 2**20),
    )(
        pltpu.with_memory_space_constraint(embeddings, pltpu.HBM),
        pltpu.with_memory_space_constraint(labels[None, :], pltpu.HBM),
    )


def kernel_tile(left, left_norms, right, right_norms):
    dim = right.shape[1] // 2
    swapped = jnp.concatenate([right[:, dim:], right[:, :dim]], axis=1)
    inner = sum(
        lax.dot_general(
            left[...], parts, (((1,), (1,)), ((), ())), preferred_element_type=jnp.float32
        )
        for parts in (swapped, right[...])
    )
    right_norms = jnp.transpose(right_norms[...])[0:1, :]
    return jnp.exp(-(left_norms[:, 0:1] + right_norms - 2.0 * inner)).astype(jnp.bfloat16)


def left_sums(right_hot, kernel):
    return lax.dot_general(
        right_hot, kernel, (((1,), (1,)), ((), ())), preferred_element_type=jnp.float32
    )


def right_sums(left_hot, kernel):
    return jnp.dot(left_hot, kernel, preferred_element_type=jnp.float32)


def self_body(own_ref, own_out, parts, norms):
    split(own_ref, parts, norms)
    own_out[...] = left_sums(labels_of(own_ref), kernel_tile(parts, norms, parts, norms))


def pair_body(
    own_ref, own_parts, own_norms, bm2_ref, b2_ref,
    own_out, for_m2_out, for_2_out, bm2_parts, bm2_norms, b2_parts, b2_norms,
):
    split(b2_ref, b2_parts, b2_norms)
    split(bm2_ref, bm2_parts, bm2_norms)
    b2_hot = labels_of(b2_ref)
    kernel = kernel_tile(bm2_parts, bm2_norms, b2_parts, b2_norms)
    for_m2_out[...] = left_sums(b2_hot, kernel)
    for_2_out[...] = right_sums(labels_of(bm2_ref), kernel)
    kernel = kernel_tile(own_parts, own_norms, b2_parts, b2_norms)
    own_out[...] = left_sums(b2_hot, kernel)
    for_2_out[...] += right_sums(labels_of(own_ref), kernel)


def visitor_body(
    even_ref, own_ref, own_parts, own_norms, bm2_ref, bm2_parts, bm2_norms,
    b2_ref, b2_parts, b2_norms, y_top_ref, y_end_ref,
    own_out, for_m2_out, for_2_out, for_y_out, y_parts, y_norms,
):
    split(jnp.concatenate([y_top_ref[...], y_end_ref[...]], axis=0), y_parts, y_norms)
    y_hot = labels_of(y_top_ref)
    kernel = kernel_tile(own_parts, own_norms, y_parts, y_norms)
    own_out[...] = left_sums(y_hot, kernel)
    for_y_out[...] = right_sums(labels_of(own_ref), kernel)
    kernel = kernel_tile(b2_parts, b2_norms, y_parts, y_norms)
    for_2_out[...] = left_sums(y_hot, kernel)
    for_y_out[...] += right_sums(labels_of(b2_ref), kernel)
    for_m2_out[...] = jnp.zeros_like(for_m2_out)

    @pl.when(even_ref[0] == 1)
    def _():
        kernel = kernel_tile(bm2_parts, bm2_norms, y_parts, y_norms)
        for_m2_out[...] = left_sums(y_hot, kernel)
        for_y_out[...] += right_sums(labels_of(bm2_ref), kernel)


def late_body(
    even_ref, bm2_ref, bm2_parts, bm2_norms, b4_ref, y_top_ref, y_parts, y_norms, for_y_in,
    for_m2_out, for_4_out, for_y_out, b4_parts, b4_norms,
):
    split(b4_ref, b4_parts, b4_norms)
    b4_hot = labels_of(b4_ref)
    kernel = kernel_tile(bm2_parts, bm2_norms, b4_parts, b4_norms)
    for_m2_out[...] = left_sums(b4_hot, kernel)
    for_4_out[...] = right_sums(labels_of(bm2_ref), kernel)
    for_y_out[...] = for_y_in[...]

    @pl.when(even_ref[0] == 0)
    def _():
        kernel = kernel_tile(b4_parts, b4_norms, y_parts, y_norms)
        for_4_out[...] += left_sums(labels_of(y_top_ref), kernel)
        for_y_out[...] += right_sums(b4_hot, kernel)


def choose_body(even_ref, b2_ref, bm2_ref, top_out, end_out):
    cut = top_out.shape[0]

    @pl.when(even_ref[0] == 1)
    def _():
        top_out[...] = b2_ref[:cut, :]
        end_out[...] = b2_ref[cut:, :]

    @pl.when(even_ref[0] == 0)
    def _():
        top_out[...] = bm2_ref[:cut, :]
        end_out[...] = bm2_ref[cut:, :]


def call(body, outs, *args, scratch=(), moved=1000):
    vmem = pl.BlockSpec(memory_space=pltpu.VMEM)
    smem = pl.BlockSpec(memory_space=pltpu.SMEM)
    return pl.pallas_call(
        body,
        out_shape=[pltpu.VMEM(*out) for out in outs],
        in_specs=[smem if a.ndim == 1 else vmem for a in args],
        out_specs=[vmem] * len(outs),
        scratch_shapes=[pltpu.VMEM(*shape) for shape in scratch],
        compiler_params=pltpu.CompilerParams(vmem_limit_bytes=16 * 2**20),
        cost_estimate=pl.CostEstimate(flops=1000, bytes_accessed=moved, transcendentals=0),
    )(*(a if a.ndim == 1 else pltpu.with_memory_space_constraint(a, pltpu.VMEM) for a in args))


def on_device(embeddings, labels):
    cut = TOP + ROWS // 2
    even = (1 - lax.axis_index("blk") % 2).astype(jnp.int32)[None]
    own, even = lax.optimization_barrier((pack(embeddings, labels), even))

    b2 = pull(own)
    bm2 = push(own)
    own_0, *own_split = call(self_body, [SUMS, *SPLIT], own, moved=4 * own.size)
    b2, own_0 = lax.optimization_barrier((b2, own_0))
    b4 = pull(b2)

    b2, bm2 = lax.optimization_barrier((b2, bm2))
    pieces = [((rows, DIM), jnp.float32) for rows in (cut, TOP + ROWS - cut)]
    y_top, y_end = call(choose_body, pieces, even, b2, bm2, moved=8 * own.size)
    y = swap(y_top), swap(y_end)
    own_2, for_m2, for_2, *splits = call(
        pair_body, [SUMS] * 3 + [*SPLIT] * 2, own, *own_split, bm2, b2, moved=16 * own.size
    )
    bm2_split, b2_split = splits[:2], splits[2:]

    y, own_2, for_m2, for_2 = lax.optimization_barrier((y, own_2, for_m2, for_2))
    own_y, for_m2_y, for_2_y, for_y, *y_split = call(
        visitor_body, [SUMS] * 4 + [*SPLIT],
        even, own, *own_split, bm2, *bm2_split, b2, *b2_split, *y, moved=8 * own.size,
    )
    back_m2 = give(for_y, 0)

    b4, own_y, for_m2_y, for_2_y, for_y = lax.optimization_barrier(
        (b4, own_y, for_m2_y, for_2_y, for_y)
    )
    for_m2_4, for_4, for_y = call(
        late_body, [SUMS] * 3, even, bm2, *bm2_split, b4, y[0], *y_split, for_y,
        scratch=SPLIT, moved=16 * own.size,
    )
    back_4 = push(for_4)
    home_m2 = pull(for_m2 + for_m2_y + for_m2_4 + back_m2)
    back_2 = give(for_y, 1)
    back_4, back_2, for_2 = lax.optimization_barrier((back_4, back_2, for_2 + for_2_y))
    home_2 = push(for_2 + back_2 + back_4)
    return (own_0 + own_2 + own_y + home_m2 + home_2).T


def solution(mesh):
    placed = (P("blk", None), P("blk"))
    return jax.shard_map(
        on_device, mesh=mesh, in_specs=placed, out_specs=P("blk", None), check_vma=False
    )
```

time: 114 us -> 114 us (level)
  transfers between devices with their start and end apart: 10 -> 10, of which waited for: 5 -> 5; matrix products, arithmetic and copies ran while one was open for 0% -> 0% of each run, Pallas kernels for 15% -> 14%
where the time goes in v7:
time: 114 us
  waiting for transfers between devices  50.7 us (44%)
  starting transfers between devices  43.2 us (38%)
  Pallas kernels  17.8 us (16%)
    ppermute x3, waiting for transfers between devices, pull(): return lax.ppermute(value, 'blk', even_odd(n, -2, 2))  32.9 us
    ppermute x3, starting transfers between devices, pull(): return lax.ppermute(value, 'blk', even_odd(n, -2, 2))  30.3 us
    ppermute x3, waiting for transfers between devices, push(): return lax.ppermute(value, 'blk', even_odd(n, 2, -2))  17.8 us
    pallas_call x5, Pallas kernels, call(): pl.pallas_call(body, out_shape=[pltpu.VMEM(*out) for out in outs], in_spe...  16.4 us
    ppermute x3, starting transfers between devices, push(): return lax.ppermute(value, 'blk', even_odd(n, 2, -2))  5.76 us
    ppermute x2, starting transfers between devices, swap(): return lax.ppermute(value, 'blk', even_odd(n, 1, -1))  4.33 us
    ppermute x2, starting transfers between devices, give(): return lax.ppermute(value, 'blk', [(i, i ^ 1) for i in range(core, n, 2)])  2.8 us
  transfers between devices with their start and end apart: 10, of which 5 were waited for; matrix products, arithmetic and copies ran while one was open for 0% of the time, Pallas kernels for 14%

profile of v7, /device:TPU:0, one launch (start us, length us, event | category | flops | bytes accessed | tf_op | source)
XLA Modules:
  0.0 113.6 jit_solution(8472918495840858050)
XLA Ops:
  0.0 1.4 %shard_map.28.own_ref = f32[520,768]{1,0:T(8,128)S(1)} custom-call(f32[512,768]{1,0:T(8,128)} %embeddings_ref.1, s32[1,512]{1,0:T(1,128)} %bitcast.4), custom_call_target="tpu_custom_call" | custom-call | tf_op jit(solution)/shard_map/pallas_call | solution.py:74
  1.4 10.7 %collective-permute-start = (f32[520,768]{1,0:T(8,128)S(1)}, f32[520,768]{1,0:T(8,128)S(1)}, u32[]{:S(2)}, u32[]{:S(2)}) collective-permute-start(f32[520,768]{1,0:T(8,128)S(1)} %shard_map.28.own_ref), channel_id=1, source_target_pairs={{0,510},{1,3},{2,0},{3,5},{4,2},{5,7},{6,4},{7,9},{8,6},{9,11},{10... | collective-permute-start | bytes 4792328 | tf_op jit(solution)/shard_map/ppermute | solution.py:22
  12.1 1.9 %collective-permute-start.1 = (f32[520,768]{1,0:T(8,128)S(1)}, f32[520,768]{1,0:T(8,128)S(1)}, u32[]{:S(2)}, u32[]{:S(2)}) collective-permute-start(f32[520,768]{1,0:T(8,128)S(1)} %shard_map.28.own_ref), channel_id=1, source_target_pairs={{0,2},{1,511},{2,4},{3,1},{4,6},{5,3},{6,8},{7,5},{8,10},{9,7},{10... | collective-permute-start | bytes 4792328 | tf_op jit(solution)/shard_map/ppermute | solution.py:27
  14.0 2.3 %shard_map.29 = (f32[256,512]{1,0:T(8,128)S(1)}, bf16[512,1536]{1,0:T(8,128)(2,1)S(1)}, f32[512,128]{1,0:T(8,128)S(1)}) custom-call(f32[520,768]{1,0:T(8,128)S(1)} %shard_map.28.own_ref), custom_call_target="tpu_custom_call" | custom-call | flops 1000 | bytes 1597440 | tf_op jit(solution)/shard_map/pallas_call | solution.py:187
  16.4 30.3 %collective-permute-done.b2_ref = f32[520,768]{1,0:T(8,128)S(1)} collective-permute-done((f32[520,768]{1,0:T(8,128)S(1)}, f32[520,768]{1,0:T(8,128)S(1)}, u32[]{:S(2)}, u32[]{:S(2)}) %collective-permute-start) | collective-permute-done | bytes 1597472 | tf_op jit(solution)/shard_map/ppermute | solution.py:22
  46.6 9.8 %collective-permute-start.4 = (f32[520,768]{1,0:T(8,128)S(1)}, f32[520,768]{1,0:T(8,128)S(1)}, u32[]{:S(2)}, u32[]{:S(2)}) collective-permute-start(f32[520,768]{1,0:T(8,128)S(1)} %collective-permute-done.b2_ref), channel_id=1, source_target_pairs={{0,510},{1,3},{2,0},{3,5},{4,2},{5,7},{6,4},{7,9},{8,6},{9,11},{10... | collective-permute-start | bytes 4792328 | tf_op jit(solution)/shard_map/ppermute | solution.py:22
  56.6 1.9 %collective-permute-start.2 = (f32[264,768]{1,0:T(8,128)S(1)}, f32[264,768]{1,0:T(8,128)S(1)}, u32[]{:S(2)}, u32[]{:S(2)}) collective-permute-start(f32[264,768]{1,0:T(8,128)S(1)} %get-tuple-element.52), channel_id=1, source_target_pairs={{0,1},{1,0},{2,3},{3,2},{4,5},{5,4},{6,7},{7,6},{8,9},{9,8},{10,11... | collective-permute-start | bytes 2433032 | tf_op jit(solution)/shard_map/ppermute | solution.py:32
  58.5 2.4 %collective-permute-start.3 = (f32[256,768]{1,0:T(8,128)S(1)}, f32[256,768]{1,0:T(8,128)S(1)}, u32[]{:S(2)}, u32[]{:S(2)}) collective-permute-start(f32[256,768]{1,0:T(8,128)S(1)} %get-tuple-element.53), channel_id=1, source_target_pairs={{0,1},{1,0},{2,3},{3,2},{4,5},{5,4},{6,7},{7,6},{8,9},{9,8},{10,11... | collective-permute-start | bytes 2359304 | tf_op jit(solution)/shard_map/ppermute | solution.py:32
  60.9 4.7 %shard_map.31 = (f32[256,512]{1,0:T(8,128)S(1)}, f32[256,512]{1,0:T(8,128)S(1)}, f32[256,512]{1,0:T(8,128)S(1)}, bf16[512,1536]{1,0:T(8,128)(2,1)S(1)}, f32[512,...) custom-call(f32[520,768]{1,0:T(8,128)S(1)} %shard_map.28.own_ref, ...), custom_call_target="tpu_custom_call" | custom-call | flops 1000 | bytes 6389760 | tf_op jit(solution)/shard_map/pallas_call | solution.py:187
  65.7 6.8 %shard_map.32 = (f32[256,512]{1,0:T(8,128)S(1)}, f32[256,512]{1,0:T(8,128)S(1)}, f32[256,512]{1,0:T(8,128)S(1)}, f32[256,512]{1,0:T(8,128)S(1)}, bf16[512,1536]{1,0:T(8,128)(2,1)S(1)}, /*index=5*/f32[512,128]{1,0:T(8,128)S(1)}) custom-call(s32[1]{0:T(128)} %bitcast.1.even_ref, f32[520,768]{1,0:T(8,128)S(1)} %shard_map.28.own_ref, ...), custom_call_target="tpu_custom_call" | custom-call | flops 1000 | bytes 3194880 | tf_op jit(solution)/shard_map/pallas_call | solution.py:187
  72.5 1.5 %collective-permute-start.5 = (f32[256,512]{1,0:T(8,128)S(1)}, f32[256,512]{1,0:T(8,128)S(1)}, u32[]{:S(2)}, u32[]{:S(2)}) collective-permute-start(f32[256,512]{1,0:T(8,128)S(1)} %get-tuple-element.76.for_y_in), channel_id=1, source_target_pairs={{0,1},{2,3},{4,5},{6,7},{8,9},{10,11},{12,13},{14,15},{16,17},{18,... | collective-permute-start | bytes 1572872 | tf_op jit(solution)/shard_map/ppermute | solution.py:37
  74.0 0.6 collective-permute-done.4.b4_ref
  74.6 2.4 %shard_map.33 = (f32[256,512]{1,0:T(8,128)S(1)}, f32[256,512]{1,0:T(8,128)S(1)}, f32[256,512]{1,0:T(8,128)S(1)}) custom-call(s32[1]{0:T(128)} %bitcast.1.even_ref, f32[520,768]{1,0:T(8,128)S(1)} %collective-permute-done.1.bm2_ref, bf16[512,1536]{1,0:T(8,128)(2,1)S(1)} %get-tuple-element.60.bm2_parts, f32[512,128]{1,0:T(8,128)S(1)} %get-tuple-element.61.bm2_norms, ...), custom_call_target="tpu_custom_call" | custom-call | flops 1000 | bytes 6389760 | tf_op jit(solution)/shard_map/pallas_call | solution.py:187
  77.1 1.9 %collective-permute-start.7 = (f32[256,512]{1,0:T(8,128)S(1)}, f32[256,512]{1,0:T(8,128)S(1)}, u32[]{:S(2)}, u32[]{:S(2)}) collective-permute-start(f32[256,512]{1,0:T(8,128)S(1)} %get-tuple-element.78), channel_id=1, source_target_pairs={{0,2},{1,511},{2,4},{3,1},{4,6},{5,3},{6,8},{7,5},{8,10},{9,7},{10... | collective-permute-start | bytes 1572872 | tf_op jit(solution)/shard_map/ppermute | solution.py:27
  79.0 1.3 %collective-permute-start.8 = (f32[256,512]{1,0:T(8,128)S(1)}, f32[256,512]{1,0:T(8,128)S(1)}, u32[]{:S(2)}, u32[]{:S(2)}) collective-permute-start(f32[256,512]{1,0:T(8,128)S(1)} %get-tuple-element.79), channel_id=1, source_target_pairs={{1,0},{3,2},{5,4},{7,6},{9,8},{11,10},{13,12},{15,14},{17,16},{19,... | collective-permute-start | bytes 1572872 | tf_op jit(solution)/shard_map/ppermute | solution.py:37
  80.3 0.2 add_add_fusion.1
  80.5 9.8 %collective-permute-start.6 = (f32[256,512]{1,0:T(8,128)S(1)}, f32[256,512]{1,0:T(8,128)S(1)}, u32[]{:S(2)}, u32[]{:S(2)}) collective-permute-start(f32[256,512]{1,0:T(8,128)S(1)} %add_add_fusion.1), channel_id=1, source_target_pairs={{0,510},{1,3},{2,0},{3,5},{4,2},{5,7},{6,4},{7,9},{8,6},{9,11},{10... | collective-permute-start | bytes 1572872 | tf_op jit(solution)/shard_map/ppermute | solution.py:22
  90.5 5.2 %collective-permute-done.7 = f32[256,512]{1,0:T(8,128)S(1)} collective-permute-done((f32[256,512]{1,0:T(8,128)S(1)}, f32[256,512]{1,0:T(8,128)S(1)}, u32[]{:S(2)}, u32[]{:S(2)}) %collective-permute-start.7) | collective-permute-done | bytes 524320 | tf_op jit(solution)/shard_map/ppermute | solution.py:27
  95.7 0.2 add_add_fusion
  95.8 1.9 %collective-permute-start.9 = (f32[256,512]{1,0:T(8,128)S(1)}, f32[256,512]{1,0:T(8,128)S(1)}, u32[]{:S(2)}, u32[]{:S(2)}) collective-permute-start(f32[256,512]{1,0:T(8,128)S(1)} %add_add_fusion), channel_id=1, source_target_pairs={{0,2},{1,511},{2,4},{3,1},{4,6},{5,3},{6,8},{7,5},{8,10},{9,7},{10... | collective-permute-start | bytes 1572872 | tf_op jit(solution)/shard_map/ppermute | solution.py:27
  97.8 2.0 %collective-permute-done.6 = f32[256,512]{1,0:T(8,128)S(1)} collective-permute-done((f32[256,512]{1,0:T(8,128)S(1)}, f32[256,512]{1,0:T(8,128)S(1)}, u32[]{:S(2)}, u32[]{:S(2)}) %collective-permute-start.6) | collective-permute-done | bytes 524320 | tf_op jit(solution)/shard_map/ppermute | solution.py:22
  99.8 12.6 %collective-permute-done.9 = f32[256,512]{1,0:T(8,128)S(1)} collective-permute-done((f32[256,512]{1,0:T(8,128)S(1)}, f32[256,512]{1,0:T(8,128)S(1)}, u32[]{:S(2)}, u32[]{:S(2)}) %collective-permute-start.9) | collective-permute-done | bytes 524320 | tf_op jit(solution)/shard_map/ppermute | solution.py:27
  112.3 0.3 add_bitcast_fusion
  112.6 1.0 copy.3
  (7 shorter events, 0.2 us)
Async XLA Ops:
  1.4 45.2 %collective-permute-start = (f32[520,768]{1,0:T(8,128)S(1)}, f32[520,768]{1,0:T(8,128)S(1)}, u32[]{:S(2)}, u32[]{:S(2)}) collective-permute-start(f32[520,768]{1,0:T(8,128)S(1)} %shard_map.28.own_ref), channel_id=1, source_target_pairs={{0,510},{1,3},{2,0},{3,5},{4,2},{5,7},{6,4},{7,9},{8,6},{9,11},{10... | collective-permute-start | bytes 4792328 | tf_op jit(solution)/shard_map/ppermute | solution.py:22
  12.1 44.3 %collective-permute-start.1 = (f32[520,768]{1,0:T(8,128)S(1)}, f32[520,768]{1,0:T(8,128)S(1)}, u32[]{:S(2)}, u32[]{:S(2)}) collective-permute-start(f32[520,768]{1,0:T(8,128)S(1)} %shard_map.28.own_ref), channel_id=1, source_target_pairs={{0,2},{1,511},{2,4},{3,1},{4,6},{5,3},{6,8},{7,5},{8,10},{9,7},{10... | collective-permute-start | bytes 4792328 | tf_op jit(solution)/shard_map/ppermute | solution.py:27
  46.6 28.0 %collective-permute-start.4 = (f32[520,768]{1,0:T(8,128)S(1)}, f32[520,768]{1,0:T(8,128)S(1)}, u32[]{:S(2)}, u32[]{:S(2)}) collective-permute-start(f32[520,768]{1,0:T(8,128)S(1)} %collective-permute-done.b2_ref), channel_id=1, source_target_pairs={{0,510},{1,3},{2,0},{3,5},{4,2},{5,7},{6,4},{7,9},{8,6},{9,11},{10... | collective-permute-start | bytes 4792328 | tf_op jit(solution)/shard_map/ppermute | solution.py:22
  56.6 9.1 %collective-permute-start.2 = (f32[264,768]{1,0:T(8,128)S(1)}, f32[264,768]{1,0:T(8,128)S(1)}, u32[]{:S(2)}, u32[]{:S(2)}) collective-permute-start(f32[264,768]{1,0:T(8,128)S(1)} %get-tuple-element.52), channel_id=1, source_target_pairs={{0,1},{1,0},{2,3},{3,2},{4,5},{5,4},{6,7},{7,6},{8,9},{9,8},{10,11... | collective-permute-start | bytes 2433032 | tf_op jit(solution)/shard_map/ppermute | solution.py:32
  58.5 7.1 %collective-permute-start.3 = (f32[256,768]{1,0:T(8,128)S(1)}, f32[256,768]{1,0:T(8,128)S(1)}, u32[]{:S(2)}, u32[]{:S(2)}) collective-permute-start(f32[256,768]{1,0:T(8,128)S(1)} %get-tuple-element.53), channel_id=1, source_target_pairs={{0,1},{1,0},{2,3},{3,2},{4,5},{5,4},{6,7},{7,6},{8,9},{9,8},{10,11... | collective-permute-start | bytes 2359304 | tf_op jit(solution)/shard_map/ppermute | solution.py:32
  72.5 7.8 %collective-permute-start.5 = (f32[256,512]{1,0:T(8,128)S(1)}, f32[256,512]{1,0:T(8,128)S(1)}, u32[]{:S(2)}, u32[]{:S(2)}) collective-permute-start(f32[256,512]{1,0:T(8,128)S(1)} %get-tuple-element.76.for_y_in), channel_id=1, source_target_pairs={{0,1},{2,3},{4,5},{6,7},{8,9},{10,11},{12,13},{14,15},{16,17},{18,... | collective-permute-start | bytes 1572872 | tf_op jit(solution)/shard_map/ppermute | solution.py:37
  77.1 18.6 %collective-permute-start.7 = (f32[256,512]{1,0:T(8,128)S(1)}, f32[256,512]{1,0:T(8,128)S(1)}, u32[]{:S(2)}, u32[]{:S(2)}) collective-permute-start(f32[256,512]{1,0:T(8,128)S(1)} %get-tuple-element.78), channel_id=1, source_target_pairs={{0,2},{1,511},{2,4},{3,1},{4,6},{5,3},{6,8},{7,5},{8,10},{9,7},{10... | collective-permute-start | bytes 1572872 | tf_op jit(solution)/shard_map/ppermute | solution.py:27
  79.0 16.7 %collective-permute-start.8 = (f32[256,512]{1,0:T(8,128)S(1)}, f32[256,512]{1,0:T(8,128)S(1)}, u32[]{:S(2)}, u32[]{:S(2)}) collective-permute-start(f32[256,512]{1,0:T(8,128)S(1)} %get-tuple-element.79), channel_id=1, source_target_pairs={{1,0},{3,2},{5,4},{7,6},{9,8},{11,10},{13,12},{15,14},{17,16},{19,... | collective-permute-start | bytes 1572872 | tf_op jit(solution)/shard_map/ppermute | solution.py:37
  80.5 19.2 %collective-permute-start.6 = (f32[256,512]{1,0:T(8,128)S(1)}, f32[256,512]{1,0:T(8,128)S(1)}, u32[]{:S(2)}, u32[]{:S(2)}) collective-permute-start(f32[256,512]{1,0:T(8,128)S(1)} %add_add_fusion.1), channel_id=1, source_target_pairs={{0,510},{1,3},{2,0},{3,5},{4,2},{5,7},{6,4},{7,9},{8,6},{9,11},{10... | collective-permute-start | bytes 1572872 | tf_op jit(solution)/shard_map/ppermute | solution.py:22
  95.8 16.5 %collective-permute-start.9 = (f32[256,512]{1,0:T(8,128)S(1)}, f32[256,512]{1,0:T(8,128)S(1)}, u32[]{:S(2)}, u32[]{:S(2)}) collective-permute-start(f32[256,512]{1,0:T(8,128)S(1)} %add_add_fusion), channel_id=1, source_target_pairs={{0,2},{1,511},{2,4},{3,1},{4,6},{5,3},{6,8},{7,5},{8,10},{9,7},{10... | collective-permute-start | bytes 1572872 | tf_op jit(solution)/shard_map/ppermute | solution.py:27

commit v8 on v7

--- a/solution.py
+++ b/solution.py
@@ -8,9 +8,10 @@
 CLUSTERS = 256
 ROWS = 512
 DIM = 768
+TOP = 8
 SUMS = ((CLUSTERS, ROWS), jnp.float32)
 SPLIT = ((ROWS, 2 * DIM), jnp.bfloat16), ((ROWS, 128), jnp.float32)
-TOP = 8
+PIECES = ((TOP + ROWS // 2, DIM), jnp.float32), ((ROWS // 2, DIM), jnp.float32)
 
 
 def even_odd(n, even, odd):
@@ -57,26 +58,42 @@
     norms_out[...] = jnp.broadcast_to(jnp.sum(kept * kept, axis=1, keepdims=True), norms_out.shape)
 
 
-def pack_body(embeddings_ref, labels_ref, message_ref, held, done):
-    rows = embeddings_ref.shape[0]
-    copy = pltpu.make_async_copy(embeddings_ref, message_ref.at[pl.ds(TOP, rows)], done.at[0])
-    copy.start()
-    labels = pltpu.make_async_copy(labels_ref, held, done.at[1])
+def pack_body(embeddings_ref, labels_ref, message_ref, top_ref, end_ref, held, done):
+    rows = top_ref.shape[0] - TOP
+    whole = pltpu.make_async_copy(
+        embeddings_ref, message_ref.at[pl.ds(TOP, ROWS)], done.at[0]
+    )
+    first = pltpu.make_async_copy(
+        embeddings_ref.at[pl.ds(0, rows)], top_ref.at[pl.ds(TOP, rows)], done.at[1]
+    )
+    second = pltpu.make_async_copy(
+        embeddings_ref.at[pl.ds(rows, ROWS - rows)], end_ref, done.at[2]
+    )
+    labels = pltpu.make_async_copy(labels_ref, held, done.at[3])
     labels.start()
-    message_ref[:TOP, :] = jnp.zeros((TOP, message_ref.shape[1]), jnp.float32)
+    whole.start()
+    first.start()
+    second.start()
+    top = jnp.zeros((TOP, DIM), jnp.float32)
+    message_ref[:TOP, :] = top
+    top_ref[:TOP, :] = top
     labels.wait()
-    message_ref[0:1, :rows] = held[...].astype(jnp.float32)
-    copy.wait()
+    row = held[...].astype(jnp.float32)
+    message_ref[0:1, :ROWS] = row
+    top_ref[0:1, :ROWS] = row
+    whole.wait()
+    first.wait()
+    second.wait()
 
 
 def pack(embeddings, labels):
-    rows, dim = embeddings.shape
+    shapes = ((TOP + ROWS, DIM), jnp.float32), *PIECES
     return pl.pallas_call(
         pack_body,
-        out_shape=pltpu.VMEM((TOP + rows, dim), jnp.float32),
+        out_shape=[pltpu.VMEM(*shape) for shape in shapes],
         in_specs=[pl.BlockSpec(memory_space=pltpu.HBM)] * 2,
-        out_specs=pl.BlockSpec(memory_space=pltpu.VMEM),
-        scratch_shapes=[pltpu.VMEM((1, rows), jnp.int32), pltpu.SemaphoreType.DMA((2,))],
+        out_specs=[pl.BlockSpec(memory_space=pltpu.VMEM)] * 3,
+        scratch_shapes=[pltpu.VMEM((1, ROWS), jnp.int32), pltpu.SemaphoreType.DMA((4,))],
         compiler_params=pltpu.CompilerParams(vmem_limit_bytes=16 * 2**20),
     )(
         pltpu.with_memory_space_constraint(embeddings, pltpu.HBM),
@@ -107,9 +124,31 @@
     return jnp.dot(left_hot, kernel, preferred_element_type=jnp.float32)
 
 
+def split_pieces(top_ref, end_ref, parts, norms):
+    split(jnp.concatenate([top_ref[...], end_ref[...]], axis=0), parts, norms)
+
+
 def self_body(own_ref, own_out, parts, norms):
     split(own_ref, parts, norms)
     own_out[...] = left_sums(labels_of(own_ref), kernel_tile(parts, norms, parts, norms))
+
+
+def chip_body(
+    even_ref, own_ref, own_parts, own_norms, top_ref, end_ref, own_in,
+    own_out, for_1_out, parts, norms,
+):
+    own_out[...] = own_in[...]
+
+    @pl.when(even_ref[0] == 1)
+    def _():
+        split_pieces(top_ref, end_ref, parts, norms)
+        kernel = kernel_tile(own_parts, own_norms, parts, norms)
+        own_out[...] += left_sums(labels_of(top_ref), kernel)
+        for_1_out[...] = right_sums(labels_of(own_ref), kernel)
+
+    @pl.when(even_ref[0] == 0)
+    def _():
+        for_1_out[...] = jnp.zeros_like(for_1_out)
 
 
 def pair_body(
@@ -132,21 +171,25 @@
     b2_ref, b2_parts, b2_norms, y_top_ref, y_end_ref,
     own_out, for_m2_out, for_2_out, for_y_out, y_parts, y_norms,
 ):
-    split(jnp.concatenate([y_top_ref[...], y_end_ref[...]], axis=0), y_parts, y_norms)
+    split_pieces(y_top_ref, y_end_ref, y_parts, y_norms)
     y_hot = labels_of(y_top_ref)
     kernel = kernel_tile(own_parts, own_norms, y_parts, y_norms)
     own_out[...] = left_sums(y_hot, kernel)
     for_y_out[...] = right_sums(labels_of(own_ref), kernel)
-    kernel = kernel_tile(b2_parts, b2_norms, y_parts, y_norms)
-    for_2_out[...] = left_sums(y_hot, kernel)
-    for_y_out[...] += right_sums(labels_of(b2_ref), kernel)
-    for_m2_out[...] = jnp.zeros_like(for_m2_out)
 
     @pl.when(even_ref[0] == 1)
     def _():
         kernel = kernel_tile(bm2_parts, bm2_norms, y_parts, y_norms)
         for_m2_out[...] = left_sums(y_hot, kernel)
+        for_2_out[...] = jnp.zeros_like(for_2_out)
         for_y_out[...] += right_sums(labels_of(bm2_ref), kernel)
+
+    @pl.when(even_ref[0] == 0)
+    def _():
+        kernel = kernel_tile(b2_parts, b2_norms, y_parts, y_norms)
+        for_2_out[...] = left_sums(y_hot, kernel)
+        for_m2_out[...] = jnp.zeros_like(for_m2_out)
+        for_y_out[...] += right_sums(labels_of(b2_ref), kernel)
 
 
 def late_body(
@@ -196,19 +239,24 @@
 
 
 def on_device(embeddings, labels):
-    cut = TOP + ROWS // 2
     even = (1 - lax.axis_index("blk") % 2).astype(jnp.int32)[None]
-    own, even = lax.optimization_barrier((pack(embeddings, labels), even))
+    (own, *own_pieces), even = lax.optimization_barrier((pack(embeddings, labels), even))
 
     b2 = pull(own)
-    bm2 = push(own)
     own_0, *own_split = call(self_body, [SUMS, *SPLIT], own, moved=4 * own.size)
-    b2, own_0 = lax.optimization_barrier((b2, own_0))
+    later_own, own_0 = lax.optimization_barrier((own, own_0))
+    bm2 = push(later_own)
+    sibling = [give(piece, 1) for piece in own_pieces]
+    own_0, for_1 = call(
+        chip_body, [SUMS] * 2, even, own, *own_split, *sibling, own_0,
+        scratch=SPLIT, moved=8 * own.size,
+    )
+    back_1 = give(for_1, 0)
+    b2, own_0, back_1 = lax.optimization_barrier((b2, own_0, back_1))
     b4 = pull(b2)
 
     b2, bm2 = lax.optimization_barrier((b2, bm2))
-    pieces = [((rows, DIM), jnp.float32) for rows in (cut, TOP + ROWS - cut)]
-    y_top, y_end = call(choose_body, pieces, even, b2, bm2, moved=8 * own.size)
+    y_top, y_end = call(choose_body, PIECES, even, b2, bm2, moved=8 * own.size)
     y = swap(y_top), swap(y_end)
     own_2, for_m2, for_2, *splits = call(
         pair_body, [SUMS] * 3 + [*SPLIT] * 2, own, *own_split, bm2, b2, moved=16 * own.size
@@ -230,11 +278,14 @@
         scratch=SPLIT, moved=16 * own.size,
     )
     back_4 = push(for_4)
-    home_m2 = pull(for_m2 + for_m2_y + for_m2_4 + back_m2)
     back_2 = give(for_y, 1)
-    back_4, back_2, for_2 = lax.optimization_barrier((back_4, back_2, for_2 + for_2_y))
+    for_m2 = for_m2 + for_m2_y + for_m2_4 + back_m2
+    back_4, back_2, for_2, for_m2 = lax.optimization_barrier(
+        (back_4, back_2, for_2 + for_2_y, for_m2)
+    )
     home_2 = push(for_2 + back_2 + back_4)
-    return (own_0 + own_2 + own_y + home_m2 + home_2).T
+    home_m2 = pull(for_m2)
+    return (own_0 + back_1 + own_2 + own_y + home_m2 + home_2).T
 
 
 def solution(mesh):

time: 114 us -> 117 us (1.026)
  the two profiles are of different devices: /device:TPU:0 before, /device:TPU:1 now
where the time goes in v8:
time: 117 us
  starting transfers between devices  54 us (46%)
  waiting for transfers between devices  42 us (36%)
  Pallas kernels  18.9 us (16%)
    ppermute x3, waiting for transfers between devices, push(): return lax.ppermute(value, 'blk', even_odd(n, 2, -2))  22.3 us
    ppermute x5, starting transfers between devices, give(): return lax.ppermute(value, 'blk', [(i, i ^ 1) for i in range(core, n, 2)])  20.4 us
    ppermute x3, waiting for transfers between devices, pull(): return lax.ppermute(value, 'blk', even_odd(n, -2, 2))  17.2 us
    ppermute x3, starting transfers between devices, push(): return lax.ppermute(value, 'blk', even_odd(n, 2, -2))  17.2 us
    pallas_call x6, Pallas kernels, call(): pl.pallas_call(body, out_shape=[pltpu.VMEM(*out) for out in outs], in_spe...  17 us
    ppermute x2, starting transfers between devices, swap(): return lax.ppermute(value, 'blk', even_odd(n, 1, -1))  8.23 us
    ppermute x3, starting transfers between devices, pull(): return lax.ppermute(value, 'blk', even_odd(n, -2, 2))  8.2 us
    ppermute x5, waiting for transfers between devices, give(): return lax.ppermute(value, 'blk', [(i, i ^ 1) for i in range(core, n, 2)])  2.51 us
  transfers between devices with their start and end apart: 13, of which 6 were waited for; matrix products, arithmetic and copies ran while one was open for 0% of the time, Pallas kernels for 15%

profile of v8, /device:TPU:1, one launch (start us, length us, event | category | flops | bytes accessed | tf_op | source)
XLA Modules:
  0.0 117.0 jit_solution(14893957287151872142)
XLA Ops:
  0.0 1.9 %shard_map.28 = (f32[520,768]{1,0:T(8,128)S(1)}, f32[264,768]{1,0:T(8,128)S(1)}, f32[256,768]{1,0:T(8,128)S(1)}) custom-call(f32[512,768]{1,0:T(8,128)} %embeddings_ref.1, s32[1,512]{1,0:T(1,128)} %bitcast.4), custom_call_target="tpu_custom_call" | custom-call | tf_op jit(solution)/shard_map/pallas_call | solution.py:91
  1.9 4.4 %collective-permute-start = (f32[520,768]{1,0:T(8,128)S(1)}, f32[520,768]{1,0:T(8,128)S(1)}, u32[]{:S(2)}, u32[]{:S(2)}) collective-permute-start(f32[520,768]{1,0:T(8,128)S(1)} %get-tuple-element.72.own_ref), channel_id=1, source_target_pairs={{0,510},{1,3},{2,0},{3,5},{4,2},{5,7},{6,4},{7,9},{8,6},{9,11},{10... | collective-permute-start | bytes 4792328 | tf_op jit(solution)/shard_map/ppermute | solution.py:23
  6.3 15.1 %collective-permute-start.1 = (f32[264,768]{1,0:T(8,128)S(1)}, f32[264,768]{1,0:T(8,128)S(1)}, u32[]{:S(2)}, u32[]{:S(2)}) collective-permute-start(f32[264,768]{1,0:T(8,128)S(1)} %get-tuple-element.63), channel_id=1, source_target_pairs={{1,0},{3,2},{5,4},{7,6},{9,8},{11,10},{13,12},{15,14},{17,16},{19,... | collective-permute-start | bytes 2433032 | tf_op jit(solution)/shard_map/ppermute | solution.py:38
  21.5 1.3 %collective-permute-start.2 = (f32[256,768]{1,0:T(8,128)S(1)}, f32[256,768]{1,0:T(8,128)S(1)}, u32[]{:S(2)}, u32[]{:S(2)}) collective-permute-start(f32[256,768]{1,0:T(8,128)S(1)} %get-tuple-element.64), channel_id=1, source_target_pairs={{1,0},{3,2},{5,4},{7,6},{9,8},{11,10},{13,12},{15,14},{17,16},{19,... | collective-permute-start | bytes 2359304 | tf_op jit(solution)/shard_map/ppermute | solution.py:38
  22.8 2.3 %shard_map.29 = (f32[256,512]{1,0:T(8,128)S(1)}, bf16[512,1536]{1,0:T(8,128)(2,1)S(1)}, f32[512,128]{1,0:T(8,128)S(1)}) custom-call(f32[520,768]{1,0:T(8,128)S(1)} %get-tuple-element.72.own_ref), custom_call_target="tpu_custom_call" | custom-call | flops 1000 | bytes 1597440 | tf_op jit(solution)/shard_map/pallas_call | solution.py:230
  25.1 2.6 %collective-permute-start.4 = (f32[520,768]{1,0:T(8,128)S(1)}, f32[520,768]{1,0:T(8,128)S(1)}, u32[]{:S(2)}, u32[]{:S(2)}) collective-permute-start(f32[520,768]{1,0:T(8,128)S(1)} %get-tuple-element.72.own_ref), channel_id=1, source_target_pairs={{0,2},{1,511},{2,4},{3,1},{4,6},{5,3},{6,8},{7,5},{8,10},{9,7},{10... | collective-permute-start | bytes 4792328 | tf_op jit(solution)/shard_map/ppermute | solution.py:28
  27.9 1.3 %collective-permute-start.3 = (f32[256,512]{1,0:T(8,128)S(1)}, f32[256,512]{1,0:T(8,128)S(1)}, u32[]{:S(2)}, u32[]{:S(2)}) collective-permute-start(f32[256,512]{1,0:T(8,128)S(1)} %get-tuple-element.68), channel_id=1, source_target_pairs={{0,1},{2,3},{4,5},{6,7},{8,9},{10,11},{12,13},{14,15},{16,17},{18,... | collective-permute-start | bytes 1572872 | tf_op jit(solution)/shard_map/ppermute | solution.py:38
  29.2 2.5 %collective-permute-done.3 = f32[256,512]{1,0:T(8,128)S(1)} collective-permute-done((f32[256,512]{1,0:T(8,128)S(1)}, f32[256,512]{1,0:T(8,128)S(1)}, u32[]{:S(2)}, u32[]{:S(2)}) %collective-permute-start.3) | collective-permute-done | bytes 524320 | tf_op jit(solution)/shard_map/ppermute | solution.py:38
  31.7 7.1 %collective-permute-done.b2_ref = f32[520,768]{1,0:T(8,128)S(1)} collective-permute-done((f32[520,768]{1,0:T(8,128)S(1)}, f32[520,768]{1,0:T(8,128)S(1)}, u32[]{:S(2)}, u32[]{:S(2)}) %collective-permute-start) | collective-permute-done | bytes 1597472 | tf_op jit(solution)/shard_map/ppermute | solution.py:23
  38.8 1.9 %collective-permute-start.7 = (f32[520,768]{1,0:T(8,128)S(1)}, f32[520,768]{1,0:T(8,128)S(1)}, u32[]{:S(2)}, u32[]{:S(2)}) collective-permute-start(f32[520,768]{1,0:T(8,128)S(1)} %collective-permute-done.b2_ref), channel_id=1, source_target_pairs={{0,510},{1,3},{2,0},{3,5},{4,2},{5,7},{6,4},{7,9},{8,6},{9,11},{10... | collective-permute-start | bytes 4792328 | tf_op jit(solution)/shard_map/ppermute | solution.py:23
  40.7 13.7 %collective-permute-done.4.bm2_ref = f32[520,768]{1,0:T(8,128)S(1)} collective-permute-done((f32[520,768]{1,0:T(8,128)S(1)}, f32[520,768]{1,0:T(8,128)S(1)}, u32[]{:S(2)}, u32[]{:S(2)}) %collective-permute-start.4) | collective-permute-done | bytes 1597472 | tf_op jit(solution)/shard_map/ppermute | solution.py:28
  54.5 6.3 %collective-permute-start.5 = (f32[264,768]{1,0:T(8,128)S(1)}, f32[264,768]{1,0:T(8,128)S(1)}, u32[]{:S(2)}, u32[]{:S(2)}) collective-permute-start(f32[264,768]{1,0:T(8,128)S(1)} %get-tuple-element.75), channel_id=1, source_target_pairs={{0,1},{1,0},{2,3},{3,2},{4,5},{5,4},{6,7},{7,6},{8,9},{9,8},{10,11... | collective-permute-start | bytes 2433032 | tf_op jit(solution)/shard_map/ppermute | solution.py:33
  60.8 1.9 %collective-permute-start.6 = (f32[256,768]{1,0:T(8,128)S(1)}, f32[256,768]{1,0:T(8,128)S(1)}, u32[]{:S(2)}, u32[]{:S(2)}) collective-permute-start(f32[256,768]{1,0:T(8,128)S(1)} %get-tuple-element.76), channel_id=1, source_target_pairs={{0,1},{1,0},{2,3},{3,2},{4,5},{5,4},{6,7},{7,6},{8,9},{9,8},{10,11... | collective-permute-start | bytes 2359304 | tf_op jit(solution)/shard_map/ppermute | solution.py:33
  62.8 4.7 %shard_map.32 = (f32[256,512]{1,0:T(8,128)S(1)}, f32[256,512]{1,0:T(8,128)S(1)}, f32[256,512]{1,0:T(8,128)S(1)}, bf16[512,1536]{1,0:T(8,128)(2,1)S(1)}, f32[512,...) custom-call(f32[520,768]{1,0:T(8,128)S(1)} %get-tuple-element.72.own_ref, ...), custom_call_target="tpu_custom_call" | custom-call | flops 1000 | bytes 6389760 | tf_op jit(solution)/shard_map/pallas_call | solution.py:230
  67.5 5.0 %shard_map.33 = (f32[256,512]{1,0:T(8,128)S(1)}, f32[256,512]{1,0:T(8,128)S(1)}, f32[256,512]{1,0:T(8,128)S(1)}, f32[256,512]{1,0:T(8,128)S(1)}, bf16[512,1536]{1,0:T(8,128)(2,1)S(1)}, /*index=5*/f32[512,128]{1,0:T(8,128)S(1)}) custom-call(s32[1]{0:T(128)} %bitcast.1.even_ref, f32[520,768]{1,0:T(8,128)S(1)} %get-tuple-element.72.own_ref, ...), custom_call_target="tpu_custom_call" | custom-call | flops 1000 | bytes 3194880 | tf_op jit(solution)/shard_map/pallas_call | solution.py:230
  72.5 1.3 %collective-permute-start.10 = (f32[256,512]{1,0:T(8,128)S(1)}, f32[256,512]{1,0:T(8,128)S(1)}, u32[]{:S(2)}, u32[]{:S(2)}) collective-permute-start(f32[256,512]{1,0:T(8,128)S(1)} %get-tuple-element.95.for_y_in), channel_id=1, source_target_pairs={{0,1},{2,3},{4,5},{6,7},{8,9},{10,11},{12,13},{14,15},{16,17},{18,... | collective-permute-start | bytes 1572872 | tf_op jit(solution)/shard_map/ppermute | solution.py:38
  73.8 4.8 %shard_map.34 = (f32[256,512]{1,0:T(8,128)S(1)}, f32[256,512]{1,0:T(8,128)S(1)}, f32[256,512]{1,0:T(8,128)S(1)}) custom-call(s32[1]{0:T(128)} %bitcast.1.even_ref, f32[520,768]{1,0:T(8,128)S(1)} %collective-permute-done.4.bm2_ref, bf16[512,1536]{1,0:T(8,128)(2,1)S(1)} %get-tuple-element.81.bm2_parts, f32[512,128]{1,0:T(8,128)S(1)} %get-tuple-element.82.bm2_norms, ...), custom_call_target="tpu_custom_call" | custom-call | flops 1000 | bytes 6389760 | tf_op jit(solution)/shard_map/pallas_call | solution.py:230
  78.6 5.3 %collective-permute-start.8 = (f32[256,512]{1,0:T(8,128)S(1)}, f32[256,512]{1,0:T(8,128)S(1)}, u32[]{:S(2)}, u32[]{:S(2)}) collective-permute-start(f32[256,512]{1,0:T(8,128)S(1)} %get-tuple-element.96), channel_id=1, source_target_pairs={{0,2},{1,511},{2,4},{3,1},{4,6},{5,3},{6,8},{7,5},{8,10},{9,7},{10... | collective-permute-start | bytes 1572872 | tf_op jit(solution)/shard_map/ppermute | solution.py:28
  83.9 1.3 %collective-permute-start.9 = (f32[256,512]{1,0:T(8,128)S(1)}, f32[256,512]{1,0:T(8,128)S(1)}, u32[]{:S(2)}, u32[]{:S(2)}) collective-permute-start(f32[256,512]{1,0:T(8,128)S(1)} %get-tuple-element.97), channel_id=1, source_target_pairs={{1,0},{3,2},{5,4},{7,6},{9,8},{11,10},{13,12},{15,14},{17,16},{19,... | collective-permute-start | bytes 1572872 | tf_op jit(solution)/shard_map/ppermute | solution.py:38
  85.6 4.5 %collective-permute-done.8 = f32[256,512]{1,0:T(8,128)S(1)} collective-permute-done((f32[256,512]{1,0:T(8,128)S(1)}, f32[256,512]{1,0:T(8,128)S(1)}, u32[]{:S(2)}, u32[]{:S(2)}) %collective-permute-start.8) | collective-permute-done | bytes 524320 | tf_op jit(solution)/shard_map/ppermute | solution.py:28
  90.2 9.2 %collective-permute-start.12 = (f32[256,512]{1,0:T(8,128)S(1)}, f32[256,512]{1,0:T(8,128)S(1)}, u32[]{:S(2)}, u32[]{:S(2)}) collective-permute-start(f32[256,512]{1,0:T(8,128)S(1)} %add_add_fusion), channel_id=1, source_target_pairs={{0,2},{1,511},{2,4},{3,1},{4,6},{5,3},{6,8},{7,5},{8,10},{9,7},{10... | collective-permute-start | bytes 1572872 | tf_op jit(solution)/shard_map/ppermute | solution.py:28
  99.4 1.9 %collective-permute-start.11 = (f32[256,512]{1,0:T(8,128)S(1)}, f32[256,512]{1,0:T(8,128)S(1)}, u32[]{:S(2)}, u32[]{:S(2)}) collective-permute-start(f32[256,512]{1,0:T(8,128)S(1)} %add_add_fusion.1), channel_id=1, source_target_pairs={{0,510},{1,3},{2,0},{3,5},{4,2},{5,7},{6,4},{7,9},{8,6},{9,11},{10... | collective-permute-start | bytes 1572872 | tf_op jit(solution)/shard_map/ppermute | solution.py:23
  101.4 4.2 %collective-permute-done.12 = f32[256,512]{1,0:T(8,128)S(1)} collective-permute-done((f32[256,512]{1,0:T(8,128)S(1)}, f32[256,512]{1,0:T(8,128)S(1)}, u32[]{:S(2)}, u32[]{:S(2)}) %collective-permute-start.12) | collective-permute-done | bytes 524320 | tf_op jit(solution)/shard_map/ppermute | solution.py:28
  105.5 10.1 %collective-permute-done.11 = f32[256,512]{1,0:T(8,128)S(1)} collective-permute-done((f32[256,512]{1,0:T(8,128)S(1)}, f32[256,512]{1,0:T(8,128)S(1)}, u32[]{:S(2)}, u32[]{:S(2)}) %collective-permute-start.11) | collective-permute-done | bytes 524320 | tf_op jit(solution)/shard_map/ppermute | solution.py:23
  (14 shorter events, 2.0 us)
Async XLA Ops:
  1.9 36.9 %collective-permute-start = (f32[520,768]{1,0:T(8,128)S(1)}, f32[520,768]{1,0:T(8,128)S(1)}, u32[]{:S(2)}, u32[]{:S(2)}) collective-permute-start(f32[520,768]{1,0:T(8,128)S(1)} %get-tuple-element.72.own_ref), channel_id=1, source_target_pairs={{0,510},{1,3},{2,0},{3,5},{4,2},{5,7},{6,4},{7,9},{8,6},{9,11},{10... | collective-permute-start | bytes 4792328 | tf_op jit(solution)/shard_map/ppermute | solution.py:23
  6.3 21.5 %collective-permute-start.1 = (f32[264,768]{1,0:T(8,128)S(1)}, f32[264,768]{1,0:T(8,128)S(1)}, u32[]{:S(2)}, u32[]{:S(2)}) collective-permute-start(f32[264,768]{1,0:T(8,128)S(1)} %get-tuple-element.63), channel_id=1, source_target_pairs={{1,0},{3,2},{5,4},{7,6},{9,8},{11,10},{13,12},{15,14},{17,16},{19,... | collective-permute-start | bytes 2433032 | tf_op jit(solution)/shard_map/ppermute | solution.py:38
  21.5 6.3 %collective-permute-start.2 = (f32[256,768]{1,0:T(8,128)S(1)}, f32[256,768]{1,0:T(8,128)S(1)}, u32[]{:S(2)}, u32[]{:S(2)}) collective-permute-start(f32[256,768]{1,0:T(8,128)S(1)} %get-tuple-element.64), channel_id=1, source_target_pairs={{1,0},{3,2},{5,4},{7,6},{9,8},{11,10},{13,12},{15,14},{17,16},{19,... | collective-permute-start | bytes 2359304 | tf_op jit(solution)/shard_map/ppermute | solution.py:38
  25.1 29.3 %collective-permute-start.4 = (f32[520,768]{1,0:T(8,128)S(1)}, f32[520,768]{1,0:T(8,128)S(1)}, u32[]{:S(2)}, u32[]{:S(2)}) collective-permute-start(f32[520,768]{1,0:T(8,128)S(1)} %get-tuple-element.72.own_ref), channel_id=1, source_target_pairs={{0,2},{1,511},{2,4},{3,1},{4,6},{5,3},{6,8},{7,5},{8,10},{9,7},{10... | collective-permute-start | bytes 4792328 | tf_op jit(solution)/shard_map/ppermute | solution.py:28
  27.9 3.8 %collective-permute-start.3 = (f32[256,512]{1,0:T(8,128)S(1)}, f32[256,512]{1,0:T(8,128)S(1)}, u32[]{:S(2)}, u32[]{:S(2)}) collective-permute-start(f32[256,512]{1,0:T(8,128)S(1)} %get-tuple-element.68), channel_id=1, source_target_pairs={{0,1},{2,3},{4,5},{6,7},{8,9},{10,11},{12,13},{14,15},{16,17},{18,... | collective-permute-start | bytes 1572872 | tf_op jit(solution)/shard_map/ppermute | solution.py:38
  38.8 35.0 %collective-permute-start.7 = (f32[520,768]{1,0:T(8,128)S(1)}, f32[520,768]{1,0:T(8,128)S(1)}, u32[]{:S(2)}, u32[]{:S(2)}) collective-permute-start(f32[520,768]{1,0:T(8,128)S(1)} %collective-permute-done.b2_ref), channel_id=1, source_target_pairs={{0,510},{1,3},{2,0},{3,5},{4,2},{5,7},{6,4},{7,9},{8,6},{9,11},{10... | collective-permute-start | bytes 4792328 | tf_op jit(solution)/shard_map/ppermute | solution.py:23
  54.5 13.0 %collective-permute-start.5 = (f32[264,768]{1,0:T(8,128)S(1)}, f32[264,768]{1,0:T(8,128)S(1)}, u32[]{:S(2)}, u32[]{:S(2)}) collective-permute-start(f32[264,768]{1,0:T(8,128)S(1)} %get-tuple-element.75), channel_id=1, source_target_pairs={{0,1},{1,0},{2,3},{3,2},{4,5},{5,4},{6,7},{7,6},{8,9},{9,8},{10,11... | collective-permute-start | bytes 2433032 | tf_op jit(solution)/shard_map/ppermute | solution.py:33
  60.8 6.6 %collective-permute-start.6 = (f32[256,768]{1,0:T(8,128)S(1)}, f32[256,768]{1,0:T(8,128)S(1)}, u32[]{:S(2)}, u32[]{:S(2)}) collective-permute-start(f32[256,768]{1,0:T(8,128)S(1)} %get-tuple-element.76), channel_id=1, source_target_pairs={{0,1},{1,0},{2,3},{3,2},{4,5},{5,4},{6,7},{7,6},{8,9},{9,8},{10,11... | collective-permute-start | bytes 2359304 | tf_op jit(solution)/shard_map/ppermute | solution.py:33
  72.5 12.8 %collective-permute-start.10 = (f32[256,512]{1,0:T(8,128)S(1)}, f32[256,512]{1,0:T(8,128)S(1)}, u32[]{:S(2)}, u32[]{:S(2)}) collective-permute-start(f32[256,512]{1,0:T(8,128)S(1)} %get-tuple-element.95.for_y_in), channel_id=1, source_target_pairs={{0,1},{2,3},{4,5},{6,7},{8,9},{10,11},{12,13},{14,15},{16,17},{18,... | collective-permute-start | bytes 1572872 | tf_op jit(solution)/shard_map/ppermute | solution.py:38
  78.6 11.4 %collective-permute-start.8 = (f32[256,512]{1,0:T(8,128)S(1)}, f32[256,512]{1,0:T(8,128)S(1)}, u32[]{:S(2)}, u32[]{:S(2)}) collective-permute-start(f32[256,512]{1,0:T(8,128)S(1)} %get-tuple-element.96), channel_id=1, source_target_pairs={{0,2},{1,511},{2,4},{3,1},{4,6},{5,3},{6,8},{7,5},{8,10},{9,7},{10... | collective-permute-start | bytes 1572872 | tf_op jit(solution)/shard_map/ppermute | solution.py:28
  83.9 6.1 %collective-permute-start.9 = (f32[256,512]{1,0:T(8,128)S(1)}, f32[256,512]{1,0:T(8,128)S(1)}, u32[]{:S(2)}, u32[]{:S(2)}) collective-permute-start(f32[256,512]{1,0:T(8,128)S(1)} %get-tuple-element.97), channel_id=1, source_target_pairs={{1,0},{3,2},{5,4},{7,6},{9,8},{11,10},{13,12},{15,14},{17,16},{19,... | collective-permute-start | bytes 1572872 | tf_op jit(solution)/shard_map/ppermute | solution.py:38
  90.2 15.4 %collective-permute-start.12 = (f32[256,512]{1,0:T(8,128)S(1)}, f32[256,512]{1,0:T(8,128)S(1)}, u32[]{:S(2)}, u32[]{:S(2)}) collective-permute-start(f32[256,512]{1,0:T(8,128)S(1)} %add_add_fusion), channel_id=1, source_target_pairs={{0,2},{1,511},{2,4},{3,1},{4,6},{5,3},{6,8},{7,5},{8,10},{9,7},{10... | collective-permute-start | bytes 1572872 | tf_op jit(solution)/shard_map/ppermute | solution.py:28
  99.4 16.2 %collective-permute-start.11 = (f32[256,512]{1,0:T(8,128)S(1)}, f32[256,512]{1,0:T(8,128)S(1)}, u32[]{:S(2)}, u32[]{:S(2)}) collective-permute-start(f32[256,512]{1,0:T(8,128)S(1)} %add_add_fusion.1), channel_id=1, source_target_pairs={{0,510},{1,3},{2,0},{3,5},{4,2},{5,7},{6,4},{7,9},{8,6},{9,11},{10... | collective-permute-start | bytes 1572872 | tf_op jit(solution)/shard_map/ppermute | solution.py:23

commit v9 on v8

--- a/solution.py
+++ b/solution.py
@@ -151,19 +151,20 @@
         for_1_out[...] = jnp.zeros_like(for_1_out)
 
 
-def pair_body(
-    own_ref, own_parts, own_norms, bm2_ref, b2_ref,
-    own_out, for_m2_out, for_2_out, bm2_parts, bm2_norms, b2_parts, b2_norms,
-):
+def near_body(own_ref, own_parts, own_norms, b2_ref, own_out, for_2_out, b2_parts, b2_norms):
     split(b2_ref, b2_parts, b2_norms)
+    kernel = kernel_tile(own_parts, own_norms, b2_parts, b2_norms)
+    own_out[...] = left_sums(labels_of(b2_ref), kernel)
+    for_2_out[...] = right_sums(labels_of(own_ref), kernel)
+
+
+def across_body(
+    bm2_ref, b2_ref, b2_parts, b2_norms, for_2_in, for_m2_out, for_2_out, bm2_parts, bm2_norms
+):
     split(bm2_ref, bm2_parts, bm2_norms)
-    b2_hot = labels_of(b2_ref)
     kernel = kernel_tile(bm2_parts, bm2_norms, b2_parts, b2_norms)
-    for_m2_out[...] = left_sums(b2_hot, kernel)
-    for_2_out[...] = right_sums(labels_of(bm2_ref), kernel)
-    kernel = kernel_tile(own_parts, own_norms, b2_parts, b2_norms)
-    own_out[...] = left_sums(b2_hot, kernel)
-    for_2_out[...] += right_sums(labels_of(own_ref), kernel)
+    for_m2_out[...] = left_sums(labels_of(b2_ref), kernel)
+    for_2_out[...] = for_2_in[...] + right_sums(labels_of(bm2_ref), kernel)
 
 
 def visitor_body(
@@ -255,13 +256,15 @@
     b2, own_0, back_1 = lax.optimization_barrier((b2, own_0, back_1))
     b4 = pull(b2)
 
-    b2, bm2 = lax.optimization_barrier((b2, bm2))
+    own_2, for_2, *b2_split = call(
+        near_body, [SUMS] * 2 + [*SPLIT], own, *own_split, b2, moved=8 * own.size
+    )
+    b2, bm2, for_2 = lax.optimization_barrier((b2, bm2, for_2))
     y_top, y_end = call(choose_body, PIECES, even, b2, bm2, moved=8 * own.size)
     y = swap(y_top), swap(y_end)
-    own_2, for_m2, for_2, *splits = call(
-        pair_body, [SUMS] * 3 + [*SPLIT] * 2, own, *own_split, bm2, b2, moved=16 * own.size
-    )
-    bm2_split, b2_split = splits[:2], splits[2:]
+    for_m2, for_2, *bm2_split = call(
+        across_body, [SUMS] * 2 + [*SPLIT], bm2, b2, *b2_split, for_2, moved=8 * own.size
+    )
 
     y, own_2, for_m2, for_2 = lax.optimization_barrier((y, own_2, for_m2, for_2))
     own_y, for_m2_y, for_2_y, for_y, *y_split = call(
@@ -278,13 +281,10 @@
         scratch=SPLIT, moved=16 * own.size,
     )
     back_4 = push(for_4)
+    home_m2 = pull(for_m2 + for_m2_y + for_m2_4 + back_m2)
     back_2 = give(for_y, 1)
-    for_m2 = for_m2 + for_m2_y + for_m2_4 + back_m2
-    back_4, back_2, for_2, for_m2 = lax.optimization_barrier(
-        (back_4, back_2, for_2 + for_2_y, for_m2)
-    )
+    back_4, back_2, for_2 = lax.optimization_barrier((back_4, back_2, for_2 + for_2_y))
     home_2 = push(for_2 + back_2 + back_4)
-    home_m2 = pull(for_m2)
     return (own_0 + back_1 + own_2 + own_y + home_m2 + home_2).T
 
 

time: 117 us -> 106 us (0.906)
  the two profiles are of different devices: /device:TPU:1 before, /device:TPU:0 now
where the time goes in v9:
time: 106 us
  starting transfers between devices  47.6 us (45%)
  waiting for transfers between devices  36.6 us (35%)
  Pallas kernels  19.2 us (18%)
    ppermute x3, starting transfers between devices, pull(): return lax.ppermute(value, 'blk', even_odd(n, -2, 2))  30.3 us
    ppermute x3, waiting for transfers between devices, push(): return lax.ppermute(value, 'blk', even_odd(n, 2, -2))  17.9 us
    pallas_call x7, Pallas kernels, call(): pl.pallas_call(body, out_shape=[pltpu.VMEM(*out) for out in outs], in_spe...  17.3 us
    ppermute x3, waiting for transfers between devices, pull(): return lax.ppermute(value, 'blk', even_odd(n, -2, 2))  17.2 us
    ppermute x5, starting transfers between devices, give(): return lax.ppermute(value, 'blk', [(i, i ^ 1) for i in range(core, n, 2)])  7.26 us
    ppermute x3, starting transfers between devices, push(): return lax.ppermute(value, 'blk', even_odd(n, 2, -2))  5.76 us
    ppermute x2, starting transfers between devices, swap(): return lax.ppermute(value, 'blk', even_odd(n, 1, -1))  4.33 us
  transfers between devices with their start and end apart: 13, of which 6 were waited for; matrix products, arithmetic and copies ran while one was open for 0% of the time, Pallas kernels for 16%

profile of v9, /device:TPU:0, one launch (start us, length us, event | category | flops | bytes accessed | tf_op | source)
XLA Modules:
  0.0 105.5 jit_solution(9997047585902159665)
XLA Ops:
  0.0 1.9 %shard_map.28 = (f32[520,768]{1,0:T(8,128)S(1)}, f32[264,768]{1,0:T(8,128)S(1)}, f32[256,768]{1,0:T(8,128)S(1)}) custom-call(f32[512,768]{1,0:T(8,128)} %embeddings_ref.1, s32[1,512]{1,0:T(1,128)} %bitcast.4), custom_call_target="tpu_custom_call" | custom-call | tf_op jit(solution)/shard_map/pallas_call | solution.py:91
  1.9 10.7 %collective-permute-start = (f32[520,768]{1,0:T(8,128)S(1)}, f32[520,768]{1,0:T(8,128)S(1)}, u32[]{:S(2)}, u32[]{:S(2)}) collective-permute-start(f32[520,768]{1,0:T(8,128)S(1)} %get-tuple-element.73.own_ref), channel_id=1, source_target_pairs={{0,510},{1,3},{2,0},{3,5},{4,2},{5,7},{6,4},{7,9},{8,6},{9,11},{10... | collective-permute-start | bytes 4792328 | tf_op jit(solution)/shard_map/ppermute | solution.py:23
  12.6 1.3 %collective-permute-start.1 = (f32[264,768]{1,0:T(8,128)S(1)}, f32[264,768]{1,0:T(8,128)S(1)}, u32[]{:S(2)}, u32[]{:S(2)}) collective-permute-start(f32[264,768]{1,0:T(8,128)S(1)} %get-tuple-element.64), channel_id=1, source_target_pairs={{1,0},{3,2},{5,4},{7,6},{9,8},{11,10},{13,12},{15,14},{17,16},{19,... | collective-permute-start | bytes 2433032 | tf_op jit(solution)/shard_map/ppermute | solution.py:38
  15.2 2.3 %shard_map.29 = (f32[256,512]{1,0:T(8,128)S(1)}, bf16[512,1536]{1,0:T(8,128)(2,1)S(1)}, f32[512,128]{1,0:T(8,128)S(1)}) custom-call(f32[520,768]{1,0:T(8,128)S(1)} %get-tuple-element.73.own_ref), custom_call_target="tpu_custom_call" | custom-call | flops 1000 | bytes 1597440 | tf_op jit(solution)/shard_map/pallas_call | solution.py:231
  17.5 1.9 %collective-permute-start.4 = (f32[520,768]{1,0:T(8,128)S(1)}, f32[520,768]{1,0:T(8,128)S(1)}, u32[]{:S(2)}, u32[]{:S(2)}) collective-permute-start(f32[520,768]{1,0:T(8,128)S(1)} %get-tuple-element.73.own_ref), channel_id=1, source_target_pairs={{0,2},{1,511},{2,4},{3,1},{4,6},{5,3},{6,8},{7,5},{8,10},{9,7},{10... | collective-permute-start | bytes 4792328 | tf_op jit(solution)/shard_map/ppermute | solution.py:28
  19.5 2.5 %shard_map.30 = (f32[256,512]{1,0:T(8,128)S(1)}, f32[256,512]{1,0:T(8,128)S(1)}) custom-call(s32[1]{0:T(128)} %bitcast.1.even_ref, f32[520,768]{1,0:T(8,128)S(1)} %get-tuple-element.73.own_ref, bf16[512,1536]{1,0:T(8,128)(2,1)S(1)} %get-tuple-element.62.own_parts, f32[512,128]{1,0:T(8,128)S(1)} %get-tuple-element.63.own_norms, ...), custom_call_target="tpu_custom_call" | custom-call | flops 1000 | bytes 3194880 | tf_op jit(solution)/shard_map/pallas_call | solution.py:231
  22.0 1.4 %collective-permute-start.3 = (f32[256,512]{1,0:T(8,128)S(1)}, f32[256,512]{1,0:T(8,128)S(1)}, u32[]{:S(2)}, u32[]{:S(2)}) collective-permute-start(f32[256,512]{1,0:T(8,128)S(1)} %get-tuple-element.69), channel_id=1, source_target_pairs={{0,1},{2,3},{4,5},{6,7},{8,9},{10,11},{12,13},{14,15},{16,17},{18,... | collective-permute-start | bytes 1572872 | tf_op jit(solution)/shard_map/ppermute | solution.py:38
  23.4 1.5 %collective-permute-done.3 = f32[256,512]{1,0:T(8,128)S(1)} collective-permute-done((f32[256,512]{1,0:T(8,128)S(1)}, f32[256,512]{1,0:T(8,128)S(1)}, u32[]{:S(2)}, u32[]{:S(2)}) %collective-permute-start.3) | collective-permute-done | bytes 524320 | tf_op jit(solution)/shard_map/ppermute | solution.py:38
  24.9 14.9 %collective-permute-done.b2_ref = f32[520,768]{1,0:T(8,128)S(1)} collective-permute-done((f32[520,768]{1,0:T(8,128)S(1)}, f32[520,768]{1,0:T(8,128)S(1)}, u32[]{:S(2)}, u32[]{:S(2)}) %collective-permute-start) | collective-permute-done | bytes 1597472 | tf_op jit(solution)/shard_map/ppermute | solution.py:23
  39.8 9.8 %collective-permute-start.7 = (f32[520,768]{1,0:T(8,128)S(1)}, f32[520,768]{1,0:T(8,128)S(1)}, u32[]{:S(2)}, u32[]{:S(2)}) collective-permute-start(f32[520,768]{1,0:T(8,128)S(1)} %collective-permute-done.b2_ref), channel_id=1, source_target_pairs={{0,510},{1,3},{2,0},{3,5},{4,2},{5,7},{6,4},{7,9},{8,6},{9,11},{10... | collective-permute-start | bytes 4792328 | tf_op jit(solution)/shard_map/ppermute | solution.py:23
  49.6 2.5 %shard_map.31 = (f32[256,512]{1,0:T(8,128)S(1)}, f32[256,512]{1,0:T(8,128)S(1)}, bf16[512,1536]{1,0:T(8,128)(2,1)S(1)}, f32[512,128]{1,0:T(8,128)S(1)}) custom-call(f32[520,768]{1,0:T(8,128)S(1)} %get-tuple-element.73.own_ref, bf16[512,1536]{1,0:T(8,128)(2,1)S(1)} %get-tuple-element.62.own_parts, f32[512,128]{1,0:T(8,128)S(1)} %get-tuple-element.63.own_norms, ...), custom_call_target="tpu_custom_call" | custom-call | flops 1000 | bytes 3194880 | tf_op jit(solution)/shard_map/pallas_call | solution.py:231
  52.2 1.9 %collective-permute-start.5 = (f32[264,768]{1,0:T(8,128)S(1)}, f32[264,768]{1,0:T(8,128)S(1)}, u32[]{:S(2)}, u32[]{:S(2)}) collective-permute-start(f32[264,768]{1,0:T(8,128)S(1)} %get-tuple-element.77), channel_id=1, source_target_pairs={{0,1},{1,0},{2,3},{3,2},{4,5},{5,4},{6,7},{7,6},{8,9},{9,8},{10,11... | collective-permute-start | bytes 2433032 | tf_op jit(solution)/shard_map/ppermute | solution.py:33
  54.1 2.4 %collective-permute-start.6 = (f32[256,768]{1,0:T(8,128)S(1)}, f32[256,768]{1,0:T(8,128)S(1)}, u32[]{:S(2)}, u32[]{:S(2)}) collective-permute-start(f32[256,768]{1,0:T(8,128)S(1)} %get-tuple-element.78), channel_id=1, source_target_pairs={{0,1},{1,0},{2,3},{3,2},{4,5},{5,4},{6,7},{7,6},{8,9},{9,8},{10,11... | collective-permute-start | bytes 2359304 | tf_op jit(solution)/shard_map/ppermute | solution.py:33
  56.6 2.5 %shard_map.33 = (f32[256,512]{1,0:T(8,128)S(1)}, f32[256,512]{1,0:T(8,128)S(1)}, bf16[512,1536]{1,0:T(8,128)(2,1)S(1)}, f32[512,128]{1,0:T(8,128)S(1)}) custom-call(f32[520,768]{1,0:T(8,128)S(1)} %collective-permute-done.4.bm2_ref, f32[520,768]{1,0:T(8,128)S(1)} %collective-permute-done.b2_ref, bf16[512,1536]{1,0:T(8,128)(2,1)S(1)} %get-tuple-element.80.b2_parts, ...), custom_call_target="tpu_custom_call" | custom-call | flops 1000 | bytes 3194880 | tf_op jit(solution)/shard_map/pallas_call | solution.py:231
  59.1 5.0 %shard_map.34 = (f32[256,512]{1,0:T(8,128)S(1)}, f32[256,512]{1,0:T(8,128)S(1)}, f32[256,512]{1,0:T(8,128)S(1)}, f32[256,512]{1,0:T(8,128)S(1)}, bf16[512,1536]{1,0:T(8,128)(2,1)S(1)}, /*index=5*/f32[512,128]{1,0:T(8,128)S(1)}) custom-call(s32[1]{0:T(128)} %bitcast.1.even_ref, f32[520,768]{1,0:T(8,128)S(1)} %get-tuple-element.73.own_ref, ...), custom_call_target="tpu_custom_call" | custom-call | flops 1000 | bytes 3194880 | tf_op jit(solution)/shard_map/pallas_call | solution.py:231
  64.1 2.0 %collective-permute-start.8 = (f32[256,512]{1,0:T(8,128)S(1)}, f32[256,512]{1,0:T(8,128)S(1)}, u32[]{:S(2)}, u32[]{:S(2)}) collective-permute-start(f32[256,512]{1,0:T(8,128)S(1)} %get-tuple-element.100.for_y_in), channel_id=1, source_target_pairs={{0,1},{2,3},{4,5},{6,7},{8,9},{10,11},{12,13},{14,15},{16,17},{18,... | collective-permute-start | bytes 1572872 | tf_op jit(solution)/shard_map/ppermute | solution.py:38
  66.0 1.8 %collective-permute-done.7.b4_ref = f32[520,768]{1,0:T(8,128)S(1)} collective-permute-done((f32[520,768]{1,0:T(8,128)S(1)}, f32[520,768]{1,0:T(8,128)S(1)}, u32[]{:S(2)}, u32[]{:S(2)}) %collective-permute-start.7) | collective-permute-done | bytes 1597472 | tf_op jit(solution)/shard_map/ppermute | solution.py:23
  67.8 2.4 %shard_map.35 = (f32[256,512]{1,0:T(8,128)S(1)}, f32[256,512]{1,0:T(8,128)S(1)}, f32[256,512]{1,0:T(8,128)S(1)}) custom-call(s32[1]{0:T(128)} %bitcast.1.even_ref, f32[520,768]{1,0:T(8,128)S(1)} %collective-permute-done.4.bm2_ref, bf16[512,1536]{1,0:T(8,128)(2,1)S(1)} %get-tuple-element.86.bm2_parts, f32[512,128]{1,0:T(8,128)S(1)} %get-tuple-element.87.bm2_norms, ...), custom_call_target="tpu_custom_call" | custom-call | flops 1000 | bytes 6389760 | tf_op jit(solution)/shard_map/pallas_call | solution.py:231
  70.2 1.9 %collective-permute-start.10 = (f32[256,512]{1,0:T(8,128)S(1)}, f32[256,512]{1,0:T(8,128)S(1)}, u32[]{:S(2)}, u32[]{:S(2)}) collective-permute-start(f32[256,512]{1,0:T(8,128)S(1)} %get-tuple-element.102), channel_id=1, source_target_pairs={{0,2},{1,511},{2,4},{3,1},{4,6},{5,3},{6,8},{7,5},{8,10},{9,7},{10... | collective-permute-start | bytes 1572872 | tf_op jit(solution)/shard_map/ppermute | solution.py:28
  72.1 1.3 %collective-permute-start.11 = (f32[256,512]{1,0:T(8,128)S(1)}, f32[256,512]{1,0:T(8,128)S(1)}, u32[]{:S(2)}, u32[]{:S(2)}) collective-permute-start(f32[256,512]{1,0:T(8,128)S(1)} %get-tuple-element.103), channel_id=1, source_target_pairs={{1,0},{3,2},{5,4},{7,6},{9,8},{11,10},{13,12},{15,14},{17,16},{19,... | collective-permute-start | bytes 1572872 | tf_op jit(solution)/shard_map/ppermute | solution.py:38
  73.7 9.8 %collective-permute-start.9 = (f32[256,512]{1,0:T(8,128)S(1)}, f32[256,512]{1,0:T(8,128)S(1)}, u32[]{:S(2)}, u32[]{:S(2)}) collective-permute-start(f32[256,512]{1,0:T(8,128)S(1)} %add_add_fusion.1), channel_id=1, source_target_pairs={{0,510},{1,3},{2,0},{3,5},{4,2},{5,7},{6,4},{7,9},{8,6},{9,11},{10... | collective-permute-start | bytes 1572872 | tf_op jit(solution)/shard_map/ppermute | solution.py:23
  83.6 3.9 %collective-permute-done.10 = f32[256,512]{1,0:T(8,128)S(1)} collective-permute-done((f32[256,512]{1,0:T(8,128)S(1)}, f32[256,512]{1,0:T(8,128)S(1)}, u32[]{:S(2)}, u32[]{:S(2)}) %collective-permute-start.10) | collective-permute-done | bytes 524320 | tf_op jit(solution)/shard_map/ppermute | solution.py:28
  87.7 1.9 %collective-permute-start.12 = (f32[256,512]{1,0:T(8,128)S(1)}, f32[256,512]{1,0:T(8,128)S(1)}, u32[]{:S(2)}, u32[]{:S(2)}) collective-permute-start(f32[256,512]{1,0:T(8,128)S(1)} %add_add_fusion), channel_id=1, source_target_pairs={{0,2},{1,511},{2,4},{3,1},{4,6},{5,3},{6,8},{7,5},{8,10},{9,7},{10... | collective-permute-start | bytes 1572872 | tf_op jit(solution)/shard_map/ppermute | solution.py:28
  90.2 14.0 %collective-permute-done.12 = f32[256,512]{1,0:T(8,128)S(1)} collective-permute-done((f32[256,512]{1,0:T(8,128)S(1)}, f32[256,512]{1,0:T(8,128)S(1)}, u32[]{:S(2)}, u32[]{:S(2)}) %collective-permute-start.12) | collective-permute-done | bytes 524320 | tf_op jit(solution)/shard_map/ppermute | solution.py:28
  (15 shorter events, 3.9 us)
Async XLA Ops:
  1.9 37.9 %collective-permute-start = (f32[520,768]{1,0:T(8,128)S(1)}, f32[520,768]{1,0:T(8,128)S(1)}, u32[]{:S(2)}, u32[]{:S(2)}) collective-permute-start(f32[520,768]{1,0:T(8,128)S(1)} %get-tuple-element.73.own_ref), channel_id=1, source_target_pairs={{0,510},{1,3},{2,0},{3,5},{4,2},{5,7},{6,4},{7,9},{8,6},{9,11},{10... | collective-permute-start | bytes 4792328 | tf_op jit(solution)/shard_map/ppermute | solution.py:23
  12.6 6.8 %collective-permute-start.1 = (f32[264,768]{1,0:T(8,128)S(1)}, f32[264,768]{1,0:T(8,128)S(1)}, u32[]{:S(2)}, u32[]{:S(2)}) collective-permute-start(f32[264,768]{1,0:T(8,128)S(1)} %get-tuple-element.64), channel_id=1, source_target_pairs={{1,0},{3,2},{5,4},{7,6},{9,8},{11,10},{13,12},{15,14},{17,16},{19,... | collective-permute-start | bytes 2433032 | tf_op jit(solution)/shard_map/ppermute | solution.py:38
  13.9 5.5 %collective-permute-start.2 = (f32[256,768]{1,0:T(8,128)S(1)}, f32[256,768]{1,0:T(8,128)S(1)}, u32[]{:S(2)}, u32[]{:S(2)}) collective-permute-start(f32[256,768]{1,0:T(8,128)S(1)} %get-tuple-element.65), channel_id=1, source_target_pairs={{1,0},{3,2},{5,4},{7,6},{9,8},{11,10},{13,12},{15,14},{17,16},{19,... | collective-permute-start | bytes 2359304 | tf_op jit(solution)/shard_map/ppermute | solution.py:38
  17.5 34.6 %collective-permute-start.4 = (f32[520,768]{1,0:T(8,128)S(1)}, f32[520,768]{1,0:T(8,128)S(1)}, u32[]{:S(2)}, u32[]{:S(2)}) collective-permute-start(f32[520,768]{1,0:T(8,128)S(1)} %get-tuple-element.73.own_ref), channel_id=1, source_target_pairs={{0,2},{1,511},{2,4},{3,1},{4,6},{5,3},{6,8},{7,5},{8,10},{9,7},{10... | collective-permute-start | bytes 4792328 | tf_op jit(solution)/shard_map/ppermute | solution.py:28
  22.0 2.9 %collective-permute-start.3 = (f32[256,512]{1,0:T(8,128)S(1)}, f32[256,512]{1,0:T(8,128)S(1)}, u32[]{:S(2)}, u32[]{:S(2)}) collective-permute-start(f32[256,512]{1,0:T(8,128)S(1)} %get-tuple-element.69), channel_id=1, source_target_pairs={{0,1},{2,3},{4,5},{6,7},{8,9},{10,11},{12,13},{14,15},{16,17},{18,... | collective-permute-start | bytes 1572872 | tf_op jit(solution)/shard_map/ppermute | solution.py:38
  39.8 28.0 %collective-permute-start.7 = (f32[520,768]{1,0:T(8,128)S(1)}, f32[520,768]{1,0:T(8,128)S(1)}, u32[]{:S(2)}, u32[]{:S(2)}) collective-permute-start(f32[520,768]{1,0:T(8,128)S(1)} %collective-permute-done.b2_ref), channel_id=1, source_target_pairs={{0,510},{1,3},{2,0},{3,5},{4,2},{5,7},{6,4},{7,9},{8,6},{9,11},{10... | collective-permute-start | bytes 4792328 | tf_op jit(solution)/shard_map/ppermute | solution.py:23
  52.2 6.8 %collective-permute-start.5 = (f32[264,768]{1,0:T(8,128)S(1)}, f32[264,768]{1,0:T(8,128)S(1)}, u32[]{:S(2)}, u32[]{:S(2)}) collective-permute-start(f32[264,768]{1,0:T(8,128)S(1)} %get-tuple-element.77), channel_id=1, source_target_pairs={{0,1},{1,0},{2,3},{3,2},{4,5},{5,4},{6,7},{7,6},{8,9},{9,8},{10,11... | collective-permute-start | bytes 2433032 | tf_op jit(solution)/shard_map/ppermute | solution.py:33
  54.1 4.9 %collective-permute-start.6 = (f32[256,768]{1,0:T(8,128)S(1)}, f32[256,768]{1,0:T(8,128)S(1)}, u32[]{:S(2)}, u32[]{:S(2)}) collective-permute-start(f32[256,768]{1,0:T(8,128)S(1)} %get-tuple-element.78), channel_id=1, source_target_pairs={{0,1},{1,0},{2,3},{3,2},{4,5},{5,4},{6,7},{7,6},{8,9},{9,8},{10,11... | collective-permute-start | bytes 2359304 | tf_op jit(solution)/shard_map/ppermute | solution.py:33
  64.1 9.4 %collective-permute-start.8 = (f32[256,512]{1,0:T(8,128)S(1)}, f32[256,512]{1,0:T(8,128)S(1)}, u32[]{:S(2)}, u32[]{:S(2)}) collective-permute-start(f32[256,512]{1,0:T(8,128)S(1)} %get-tuple-element.100.for_y_in), channel_id=1, source_target_pairs={{0,1},{2,3},{4,5},{6,7},{8,9},{10,11},{12,13},{14,15},{16,17},{18,... | collective-permute-start | bytes 1572872 | tf_op jit(solution)/shard_map/ppermute | solution.py:38
  70.2 17.3 %collective-permute-start.10 = (f32[256,512]{1,0:T(8,128)S(1)}, f32[256,512]{1,0:T(8,128)S(1)}, u32[]{:S(2)}, u32[]{:S(2)}) collective-permute-start(f32[256,512]{1,0:T(8,128)S(1)} %get-tuple-element.102), channel_id=1, source_target_pairs={{0,2},{1,511},{2,4},{3,1},{4,6},{5,3},{6,8},{7,5},{8,10},{9,7},{10... | collective-permute-start | bytes 1572872 | tf_op jit(solution)/shard_map/ppermute | solution.py:28
  72.1 15.4 %collective-permute-start.11 = (f32[256,512]{1,0:T(8,128)S(1)}, f32[256,512]{1,0:T(8,128)S(1)}, u32[]{:S(2)}, u32[]{:S(2)}) collective-permute-start(f32[256,512]{1,0:T(8,128)S(1)} %get-tuple-element.103), channel_id=1, source_target_pairs={{1,0},{3,2},{5,4},{7,6},{9,8},{11,10},{13,12},{15,14},{17,16},{19,... | collective-permute-start | bytes 1572872 | tf_op jit(solution)/shard_map/ppermute | solution.py:38
  73.7 16.5 %collective-permute-start.9 = (f32[256,512]{1,0:T(8,128)S(1)}, f32[256,512]{1,0:T(8,128)S(1)}, u32[]{:S(2)}, u32[]{:S(2)}) collective-permute-start(f32[256,512]{1,0:T(8,128)S(1)} %add_add_fusion.1), channel_id=1, source_target_pairs={{0,510},{1,3},{2,0},{3,5},{4,2},{5,7},{6,4},{7,9},{8,6},{9,11},{10... | collective-permute-start | bytes 1572872 | tf_op jit(solution)/shard_map/ppermute | solution.py:23
  87.7 16.5 %collective-permute-start.12 = (f32[256,512]{1,0:T(8,128)S(1)}, f32[256,512]{1,0:T(8,128)S(1)}, u32[]{:S(2)}, u32[]{:S(2)}) collective-permute-start(f32[256,512]{1,0:T(8,128)S(1)} %add_add_fusion), channel_id=1, source_target_pairs={{0,2},{1,511},{2,4},{3,1},{4,6},{5,3},{6,8},{7,5},{8,10},{9,7},{10... | collective-permute-start | bytes 1572872 | tf_op jit(solution)/shard_map/ppermute | solution.py:28

commit v10 on v9

--- a/solution.py
+++ b/solution.py
@@ -58,42 +58,26 @@
     norms_out[...] = jnp.broadcast_to(jnp.sum(kept * kept, axis=1, keepdims=True), norms_out.shape)
 
 
-def pack_body(embeddings_ref, labels_ref, message_ref, top_ref, end_ref, held, done):
-    rows = top_ref.shape[0] - TOP
-    whole = pltpu.make_async_copy(
-        embeddings_ref, message_ref.at[pl.ds(TOP, ROWS)], done.at[0]
-    )
-    first = pltpu.make_async_copy(
-        embeddings_ref.at[pl.ds(0, rows)], top_ref.at[pl.ds(TOP, rows)], done.at[1]
-    )
-    second = pltpu.make_async_copy(
-        embeddings_ref.at[pl.ds(rows, ROWS - rows)], end_ref, done.at[2]
-    )
-    labels = pltpu.make_async_copy(labels_ref, held, done.at[3])
+def pack_body(embeddings_ref, labels_ref, message_ref, held, done):
+    rows = embeddings_ref.shape[0]
+    copy = pltpu.make_async_copy(embeddings_ref, message_ref.at[pl.ds(TOP, rows)], done.at[0])
+    copy.start()
+    labels = pltpu.make_async_copy(labels_ref, held, done.at[1])
     labels.start()
-    whole.start()
-    first.start()
-    second.start()
-    top = jnp.zeros((TOP, DIM), jnp.float32)
-    message_ref[:TOP, :] = top
-    top_ref[:TOP, :] = top
+    message_ref[:TOP, :] = jnp.zeros((TOP, message_ref.shape[1]), jnp.float32)
     labels.wait()
-    row = held[...].astype(jnp.float32)
-    message_ref[0:1, :ROWS] = row
-    top_ref[0:1, :ROWS] = row
-    whole.wait()
-    first.wait()
-    second.wait()
+    message_ref[0:1, :rows] = held[...].astype(jnp.float32)
+    copy.wait()
 
 
 def pack(embeddings, labels):
-    shapes = ((TOP + ROWS, DIM), jnp.float32), *PIECES
+    rows, dim = embeddings.shape
     return pl.pallas_call(
         pack_body,
-        out_shape=[pltpu.VMEM(*shape) for shape in shapes],
+        out_shape=pltpu.VMEM((TOP + rows, dim), jnp.float32),
         in_specs=[pl.BlockSpec(memory_space=pltpu.HBM)] * 2,
-        out_specs=[pl.BlockSpec(memory_space=pltpu.VMEM)] * 3,
-        scratch_shapes=[pltpu.VMEM((1, ROWS), jnp.int32), pltpu.SemaphoreType.DMA((4,))],
+        out_specs=pl.BlockSpec(memory_space=pltpu.VMEM),
+        scratch_shapes=[pltpu.VMEM((1, rows), jnp.int32), pltpu.SemaphoreType.DMA((2,))],
         compiler_params=pltpu.CompilerParams(vmem_limit_bytes=16 * 2**20),
     )(
         pltpu.with_memory_space_constraint(embeddings, pltpu.HBM),
@@ -128,9 +112,20 @@
     split(jnp.concatenate([top_ref[...], end_ref[...]], axis=0), parts, norms)
 
 
-def self_body(own_ref, own_out, parts, norms):
+def self_body(own_ref, own_out, parts, norms, top_out, end_out):
+    cut = top_out.shape[0]
+    top_out[...] = own_ref[:cut, :]
+    end_out[...] = own_ref[cut:, :]
     split(own_ref, parts, norms)
     own_out[...] = left_sums(labels_of(own_ref), kernel_tile(parts, norms, parts, norms))
+
+
+def final_body(*refs):
+    *parts, out = refs
+    total = parts[0][...]
+    for part in parts[1:]:
+        total += part[...]
+    out[...] = total.T
 
 
 def chip_body(
@@ -241,13 +236,15 @@
 
 def on_device(embeddings, labels):
     even = (1 - lax.axis_index("blk") % 2).astype(jnp.int32)[None]
-    (own, *own_pieces), even = lax.optimization_barrier((pack(embeddings, labels), even))
+    own, even = lax.optimization_barrier((pack(embeddings, labels), even))
 
     b2 = pull(own)
-    own_0, *own_split = call(self_body, [SUMS, *SPLIT], own, moved=4 * own.size)
+    own_0, *own_split, top, end = call(
+        self_body, [SUMS, *SPLIT, *PIECES], own, moved=8 * own.size
+    )
     later_own, own_0 = lax.optimization_barrier((own, own_0))
     bm2 = push(later_own)
-    sibling = [give(piece, 1) for piece in own_pieces]
+    sibling = [give(piece, 1) for piece in (top, end)]
     own_0, for_1 = call(
         chip_body, [SUMS] * 2, even, own, *own_split, *sibling, own_0,
         scratch=SPLIT, moved=8 * own.size,
@@ -285,7 +282,15 @@
     back_2 = give(for_y, 1)
     back_4, back_2, for_2 = lax.optimization_barrier((back_4, back_2, for_2 + for_2_y))
     home_2 = push(for_2 + back_2 + back_4)
-    return (own_0 + back_1 + own_2 + own_y + home_m2 + home_2).T
+    vmem = pl.BlockSpec(memory_space=pltpu.VMEM)
+    parts = own_0, back_1, own_2, own_y, home_m2, home_2
+    return pl.pallas_call(
+        final_body,
+        out_shape=jax.ShapeDtypeStruct((ROWS, CLUSTERS), jnp.float32),
+        in_specs=[vmem] * len(parts),
+        out_specs=vmem,
+        compiler_params=pltpu.CompilerParams(vmem_limit_bytes=16 * 2**20),
+    )(*(pltpu.with_memory_space_constraint(part, pltpu.VMEM) for part in parts))
 
 
 def solution(mesh):

time: 106 us -> 105 us (level)
    ppermute x3, waiting for transfers between devices: 17.2 us -> 16.1 us  [pull(): return lax.ppermute(value, 'blk', even_odd(n, -2, 2))]
    pallas_call x1 -> x2, Pallas kernels: 1.94 us -> 2.51 us  [the longest x1 1.42 us: pack(): pl.pallas_call(pack_body, out_shape=pltpu.VMEM((TOP + rows, dim), jnp.flo...]
  transfers between devices with their start and end apart: 13 -> 13, of which waited for: 6 -> 8; matrix products, arithmetic and copies ran while one was open for 0% -> 0% of each run, Pallas kernels for 16% -> 17%
where the time goes in v10:
time: 105 us; the launch traced here: 104 us
  starting transfers between devices  47.6 us (45%)
  waiting for transfers between devices  36.3 us (35%)
  Pallas kernels  19.9 us (19%)
    ppermute x3, starting transfers between devices, pull(): return lax.ppermute(value, 'blk', even_odd(n, -2, 2))  30.3 us
    ppermute x3, waiting for transfers between devices, push(): return lax.ppermute(value, 'blk', even_odd(n, 2, -2))  17.7 us
    pallas_call x7, Pallas kernels, call(): pl.pallas_call(body, out_shape=[pltpu.VMEM(*out) for out in outs], in_spe...  17.4 us
    ppermute x3, waiting for transfers between devices, pull(): return lax.ppermute(value, 'blk', even_odd(n, -2, 2))  16.1 us
    ppermute x5, starting transfers between devices, give(): return lax.ppermute(value, 'blk', [(i, i ^ 1) for i in range(core, n, 2)])  7.16 us
    ppermute x3, starting transfers between devices, push(): return lax.ppermute(value, 'blk', even_odd(n, 2, -2))  5.76 us
    ppermute x2, starting transfers between devices, swap(): return lax.ppermute(value, 'blk', even_odd(n, 1, -1))  4.33 us
    ppermute x5, waiting for transfers between devices, give(): return lax.ppermute(value, 'blk', [(i, i ^ 1) for i in range(core, n, 2)])  2.49 us
  transfers between devices with their start and end apart: 13, of which 8 were waited for; matrix products, arithmetic and copies ran while one was open for 0% of the time, Pallas kernels for 17%

profile of v10, /device:TPU:0, one launch (start us, length us, event | category | flops | bytes accessed | tf_op | source)
XLA Modules:
  0.0 104.5 jit_solution(12808766994360301647)
XLA Ops:
  0.0 1.4 %shard_map.28.own_ref = f32[520,768]{1,0:T(8,128)S(1)} custom-call(f32[512,768]{1,0:T(8,128)} %embeddings_ref.1, s32[1,512]{1,0:T(1,128)} %bitcast.2), custom_call_target="tpu_custom_call" | custom-call | tf_op jit(solution)/shard_map/pallas_call | solution.py:75
  1.4 10.7 %collective-permute-start = (f32[520,768]{1,0:T(8,128)S(1)}, f32[520,768]{1,0:T(8,128)S(1)}, u32[]{:S(2)}, u32[]{:S(2)}) collective-permute-start(f32[520,768]{1,0:T(8,128)S(1)} %shard_map.28.own_ref), channel_id=1, source_target_pairs={{0,510},{1,3},{2,0},{3,5},{4,2},{5,7},{6,4},{7,9},{8,6},{9,11},{10... | collective-permute-start | bytes 4792328 | tf_op jit(solution)/shard_map/ppermute | solution.py:23
  12.1 2.4 %shard_map.29 = (f32[256,512]{1,0:T(8,128)S(1)}, bf16[512,1536]{1,0:T(8,128)(2,1)S(1)}, f32[512,128]{1,0:T(8,128)S(1)}, f32[264,768]{1,0:T(8,128)S(1)}, f32[256,768]{1,0:T(8,128)S(1)}) custom-call(f32[520,768]{1,0:T(8,128)S(1)} %shard_map.28.own_ref), custom_call_target="tpu_custom_call" | custom-call | flops 1000 | bytes 3194880 | tf_op jit(solution)/shard_map/pallas_call | solution.py:226
  14.5 1.3 %collective-permute-start.1 = (f32[264,768]{1,0:T(8,128)S(1)}, f32[264,768]{1,0:T(8,128)S(1)}, u32[]{:S(2)}, u32[]{:S(2)}) collective-permute-start(f32[264,768]{1,0:T(8,128)S(1)} %get-tuple-element.58), channel_id=1, source_target_pairs={{1,0},{3,2},{5,4},{7,6},{9,8},{11,10},{13,12},{15,14},{17,16},{19,... | collective-permute-start | bytes 2433032 | tf_op jit(solution)/shard_map/ppermute | solution.py:38
  15.8 1.3 %collective-permute-start.2 = (f32[256,768]{1,0:T(8,128)S(1)}, f32[256,768]{1,0:T(8,128)S(1)}, u32[]{:S(2)}, u32[]{:S(2)}) collective-permute-start(f32[256,768]{1,0:T(8,128)S(1)} %get-tuple-element.59), channel_id=1, source_target_pairs={{1,0},{3,2},{5,4},{7,6},{9,8},{11,10},{13,12},{15,14},{17,16},{19,... | collective-permute-start | bytes 2359304 | tf_op jit(solution)/shard_map/ppermute | solution.py:38
  17.1 1.9 %collective-permute-start.4 = (f32[520,768]{1,0:T(8,128)S(1)}, f32[520,768]{1,0:T(8,128)S(1)}, u32[]{:S(2)}, u32[]{:S(2)}) collective-permute-start(f32[520,768]{1,0:T(8,128)S(1)} %shard_map.28.own_ref), channel_id=1, source_target_pairs={{0,2},{1,511},{2,4},{3,1},{4,6},{5,3},{6,8},{7,5},{8,10},{9,7},{10... | collective-permute-start | bytes 4792328 | tf_op jit(solution)/shard_map/ppermute | solution.py:28
  20.1 2.5 %shard_map.30 = (f32[256,512]{1,0:T(8,128)S(1)}, f32[256,512]{1,0:T(8,128)S(1)}) custom-call(s32[1]{0:T(128)} %bitcast.1.even_ref, f32[520,768]{1,0:T(8,128)S(1)} %shard_map.28.own_ref, bf16[512,1536]{1,0:T(8,128)(2,1)S(1)} %get-tuple-element.56.own_parts, f32[512,128]{1,0:T(8,128)S(1)} %get-tuple-element.57.own_norms, ...), custom_call_target="tpu_custom_call" | custom-call | flops 1000 | bytes 3194880 | tf_op jit(solution)/shard_map/pallas_call | solution.py:226
  22.6 1.3 %collective-permute-start.3 = (f32[256,512]{1,0:T(8,128)S(1)}, f32[256,512]{1,0:T(8,128)S(1)}, u32[]{:S(2)}, u32[]{:S(2)}) collective-permute-start(f32[256,512]{1,0:T(8,128)S(1)} %get-tuple-element.63), channel_id=1, source_target_pairs={{0,1},{2,3},{4,5},{6,7},{8,9},{10,11},{12,13},{14,15},{16,17},{18,... | collective-permute-start | bytes 1572872 | tf_op jit(solution)/shard_map/ppermute | solution.py:38
  23.9 1.5 %collective-permute-done.3.refs_1_ = f32[256,512]{1,0:T(8,128)S(1)} collective-permute-done((f32[256,512]{1,0:T(8,128)S(1)}, f32[256,512]{1,0:T(8,128)S(1)}, u32[]{:S(2)}, u32[]{:S(2)}) %collective-permute-start.3) | collective-permute-done | bytes 524320 | tf_op jit(solution)/shard_map/ppermute | solution.py:38
  25.4 13.7 %collective-permute-done.b2_ref = f32[520,768]{1,0:T(8,128)S(1)} collective-permute-done((f32[520,768]{1,0:T(8,128)S(1)}, f32[520,768]{1,0:T(8,128)S(1)}, u32[]{:S(2)}, u32[]{:S(2)}) %collective-permute-start) | collective-permute-done | bytes 1597472 | tf_op jit(solution)/shard_map/ppermute | solution.py:23
  39.1 9.8 %collective-permute-start.7 = (f32[520,768]{1,0:T(8,128)S(1)}, f32[520,768]{1,0:T(8,128)S(1)}, u32[]{:S(2)}, u32[]{:S(2)}) collective-permute-start(f32[520,768]{1,0:T(8,128)S(1)} %collective-permute-done.b2_ref), channel_id=1, source_target_pairs={{0,510},{1,3},{2,0},{3,5},{4,2},{5,7},{6,4},{7,9},{8,6},{9,11},{10... | collective-permute-start | bytes 4792328 | tf_op jit(solution)/shard_map/ppermute | solution.py:23
  49.0 2.4 %shard_map.31 = (f32[256,512]{1,0:T(8,128)S(1)}, f32[256,512]{1,0:T(8,128)S(1)}, bf16[512,1536]{1,0:T(8,128)(2,1)S(1)}, f32[512,128]{1,0:T(8,128)S(1)}) custom-call(f32[520,768]{1,0:T(8,128)S(1)} %shard_map.28.own_ref, bf16[512,1536]{1,0:T(8,128)(2,1)S(1)} %get-tuple-element.56.own_parts, f32[512,128]{1,0:T(8,128)S(1)} %get-tuple-element.57.own_norms, ...), custom_call_target="tpu_custom_call" | custom-call | flops 1000 | bytes 3194880 | tf_op jit(solution)/shard_map/pallas_call | solution.py:226
  51.6 1.9 %collective-permute-start.5 = (f32[264,768]{1,0:T(8,128)S(1)}, f32[264,768]{1,0:T(8,128)S(1)}, u32[]{:S(2)}, u32[]{:S(2)}) collective-permute-start(f32[264,768]{1,0:T(8,128)S(1)} %get-tuple-element.71), channel_id=1, source_target_pairs={{0,1},{1,0},{2,3},{3,2},{4,5},{5,4},{6,7},{7,6},{8,9},{9,8},{10,11... | collective-permute-start | bytes 2433032 | tf_op jit(solution)/shard_map/ppermute | solution.py:33
  53.6 2.4 %collective-permute-start.6 = (f32[256,768]{1,0:T(8,128)S(1)}, f32[256,768]{1,0:T(8,128)S(1)}, u32[]{:S(2)}, u32[]{:S(2)}) collective-permute-start(f32[256,768]{1,0:T(8,128)S(1)} %get-tuple-element.72), channel_id=1, source_target_pairs={{0,1},{1,0},{2,3},{3,2},{4,5},{5,4},{6,7},{7,6},{8,9},{9,8},{10,11... | collective-permute-start | bytes 2359304 | tf_op jit(solution)/shard_map/ppermute | solution.py:33
  56.0 2.5 %shard_map.33 = (f32[256,512]{1,0:T(8,128)S(1)}, f32[256,512]{1,0:T(8,128)S(1)}, bf16[512,1536]{1,0:T(8,128)(2,1)S(1)}, f32[512,128]{1,0:T(8,128)S(1)}) custom-call(f32[520,768]{1,0:T(8,128)S(1)} %collective-permute-done.4.bm2_ref, f32[520,768]{1,0:T(8,128)S(1)} %collective-permute-done.b2_ref, bf16[512,1536]{1,0:T(8,128)(2,1)S(1)} %get-tuple-element.74.b2_parts, ...), custom_call_target="tpu_custom_call" | custom-call | flops 1000 | bytes 3194880 | tf_op jit(solution)/shard_map/pallas_call | solution.py:226
  58.5 5.0 %shard_map.34 = (f32[256,512]{1,0:T(8,128)S(1)}, f32[256,512]{1,0:T(8,128)S(1)}, f32[256,512]{1,0:T(8,128)S(1)}, f32[256,512]{1,0:T(8,128)S(1)}, bf16[512,1536]{1,0:T(8,128)(2,1)S(1)}, /*index=5*/f32[512,128]{1,0:T(8,128)S(1)}) custom-call(s32[1]{0:T(128)} %bitcast.1.even_ref, f32[520,768]{1,0:T(8,128)S(1)} %shard_map.28.own_ref, ...), custom_call_target="tpu_custom_call" | custom-call | flops 1000 | bytes 3194880 | tf_op jit(solution)/shard_map/pallas_call | solution.py:226
  63.5 2.0 %collective-permute-start.8 = (f32[256,512]{1,0:T(8,128)S(1)}, f32[256,512]{1,0:T(8,128)S(1)}, u32[]{:S(2)}, u32[]{:S(2)}) collective-permute-start(f32[256,512]{1,0:T(8,128)S(1)} %get-tuple-element.94.for_y_in), channel_id=1, source_target_pairs={{0,1},{2,3},{4,5},{6,7},{8,9},{10,11},{12,13},{14,15},{16,17},{18,... | collective-permute-start | bytes 1572872 | tf_op jit(solution)/shard_map/ppermute | solution.py:38
  65.5 1.7 %collective-permute-done.7.b4_ref = f32[520,768]{1,0:T(8,128)S(1)} collective-permute-done((f32[520,768]{1,0:T(8,128)S(1)}, f32[520,768]{1,0:T(8,128)S(1)}, u32[]{:S(2)}, u32[]{:S(2)}) %collective-permute-start.7) | collective-permute-done | bytes 1597472 | tf_op jit(solution)/shard_map/ppermute | solution.py:23
  67.1 2.4 %shard_map.35 = (f32[256,512]{1,0:T(8,128)S(1)}, f32[256,512]{1,0:T(8,128)S(1)}, f32[256,512]{1,0:T(8,128)S(1)}) custom-call(s32[1]{0:T(128)} %bitcast.1.even_ref, f32[520,768]{1,0:T(8,128)S(1)} %collective-permute-done.4.bm2_ref, bf16[512,1536]{1,0:T(8,128)(2,1)S(1)} %get-tuple-element.80.bm2_parts, f32[512,128]{1,0:T(8,128)S(1)} %get-tuple-element.81.bm2_norms, ...), custom_call_target="tpu_custom_call" | custom-call | flops 1000 | bytes 6389760 | tf_op jit(solution)/shard_map/pallas_call | solution.py:226
  69.6 1.9 %collective-permute-start.10 = (f32[256,512]{1,0:T(8,128)S(1)}, f32[256,512]{1,0:T(8,128)S(1)}, u32[]{:S(2)}, u32[]{:S(2)}) collective-permute-start(f32[256,512]{1,0:T(8,128)S(1)} %get-tuple-element.96), channel_id=1, source_target_pairs={{0,2},{1,511},{2,4},{3,1},{4,6},{5,3},{6,8},{7,5},{8,10},{9,7},{10... | collective-permute-start | bytes 1572872 | tf_op jit(solution)/shard_map/ppermute | solution.py:28
  73.0 9.8 %collective-permute-start.9 = (f32[256,512]{1,0:T(8,128)S(1)}, f32[256,512]{1,0:T(8,128)S(1)}, u32[]{:S(2)}, u32[]{:S(2)}) collective-permute-start(f32[256,512]{1,0:T(8,128)S(1)} %add_add_fusion.1), channel_id=1, source_target_pairs={{0,510},{1,3},{2,0},{3,5},{4,2},{5,7},{6,4},{7,9},{8,6},{9,11},{10... | collective-permute-start | bytes 1572872 | tf_op jit(solution)/shard_map/ppermute | solution.py:23
  83.0 3.8 %collective-permute-done.10 = f32[256,512]{1,0:T(8,128)S(1)} collective-permute-done((f32[256,512]{1,0:T(8,128)S(1)}, f32[256,512]{1,0:T(8,128)S(1)}, u32[]{:S(2)}, u32[]{:S(2)}) %collective-permute-start.10) | collective-permute-done | bytes 524320 | tf_op jit(solution)/shard_map/ppermute | solution.py:28
  86.9 1.9 %collective-permute-start.12 = (f32[256,512]{1,0:T(8,128)S(1)}, f32[256,512]{1,0:T(8,128)S(1)}, u32[]{:S(2)}, u32[]{:S(2)}) collective-permute-start(f32[256,512]{1,0:T(8,128)S(1)} %add_add_fusion), channel_id=1, source_target_pairs={{0,2},{1,511},{2,4},{3,1},{4,6},{5,3},{6,8},{7,5},{8,10},{9,7},{10... | collective-permute-start | bytes 1572872 | tf_op jit(solution)/shard_map/ppermute | solution.py:28
  89.6 13.8 %collective-permute-done.12.refs_5_ = f32[256,512]{1,0:T(8,128)S(1)} collective-permute-done((f32[256,512]{1,0:T(8,128)S(1)}, f32[256,512]{1,0:T(8,128)S(1)}, u32[]{:S(2)}, u32[]{:S(2)}) %collective-permute-start.12) | collective-permute-done | bytes 524320 | tf_op jit(solution)/shard_map/ppermute | solution.py:28
  (14 shorter events, 4.8 us)
Async XLA Ops:
  1.4 37.7 %collective-permute-start = (f32[520,768]{1,0:T(8,128)S(1)}, f32[520,768]{1,0:T(8,128)S(1)}, u32[]{:S(2)}, u32[]{:S(2)}) collective-permute-start(f32[520,768]{1,0:T(8,128)S(1)} %shard_map.28.own_ref), channel_id=1, source_target_pairs={{0,510},{1,3},{2,0},{3,5},{4,2},{5,7},{6,4},{7,9},{8,6},{9,11},{10... | collective-permute-start | bytes 4792328 | tf_op jit(solution)/shard_map/ppermute | solution.py:23
  14.5 5.5 %collective-permute-start.1 = (f32[264,768]{1,0:T(8,128)S(1)}, f32[264,768]{1,0:T(8,128)S(1)}, u32[]{:S(2)}, u32[]{:S(2)}) collective-permute-start(f32[264,768]{1,0:T(8,128)S(1)} %get-tuple-element.58), channel_id=1, source_target_pairs={{1,0},{3,2},{5,4},{7,6},{9,8},{11,10},{13,12},{15,14},{17,16},{19,... | collective-permute-start | bytes 2433032 | tf_op jit(solution)/shard_map/ppermute | solution.py:38
  15.8 4.2 %collective-permute-start.2 = (f32[256,768]{1,0:T(8,128)S(1)}, f32[256,768]{1,0:T(8,128)S(1)}, u32[]{:S(2)}, u32[]{:S(2)}) collective-permute-start(f32[256,768]{1,0:T(8,128)S(1)} %get-tuple-element.59), channel_id=1, source_target_pairs={{1,0},{3,2},{5,4},{7,6},{9,8},{11,10},{13,12},{15,14},{17,16},{19,... | collective-permute-start | bytes 2359304 | tf_op jit(solution)/shard_map/ppermute | solution.py:38
  17.1 34.4 %collective-permute-start.4 = (f32[520,768]{1,0:T(8,128)S(1)}, f32[520,768]{1,0:T(8,128)S(1)}, u32[]{:S(2)}, u32[]{:S(2)}) collective-permute-start(f32[520,768]{1,0:T(8,128)S(1)} %shard_map.28.own_ref), channel_id=1, source_target_pairs={{0,2},{1,511},{2,4},{3,1},{4,6},{5,3},{6,8},{7,5},{8,10},{9,7},{10... | collective-permute-start | bytes 4792328 | tf_op jit(solution)/shard_map/ppermute | solution.py:28
  22.6 2.8 %collective-permute-start.3 = (f32[256,512]{1,0:T(8,128)S(1)}, f32[256,512]{1,0:T(8,128)S(1)}, u32[]{:S(2)}, u32[]{:S(2)}) collective-permute-start(f32[256,512]{1,0:T(8,128)S(1)} %get-tuple-element.63), channel_id=1, source_target_pairs={{0,1},{2,3},{4,5},{6,7},{8,9},{10,11},{12,13},{14,15},{16,17},{18,... | collective-permute-start | bytes 1572872 | tf_op jit(solution)/shard_map/ppermute | solution.py:38
  39.1 28.0 %collective-permute-start.7 = (f32[520,768]{1,0:T(8,128)S(1)}, f32[520,768]{1,0:T(8,128)S(1)}, u32[]{:S(2)}, u32[]{:S(2)}) collective-permute-start(f32[520,768]{1,0:T(8,128)S(1)} %collective-permute-done.b2_ref), channel_id=1, source_target_pairs={{0,510},{1,3},{2,0},{3,5},{4,2},{5,7},{6,4},{7,9},{8,6},{9,11},{10... | collective-permute-start | bytes 4792328 | tf_op jit(solution)/shard_map/ppermute | solution.py:23
  51.6 6.8 %collective-permute-start.5 = (f32[264,768]{1,0:T(8,128)S(1)}, f32[264,768]{1,0:T(8,128)S(1)}, u32[]{:S(2)}, u32[]{:S(2)}) collective-permute-start(f32[264,768]{1,0:T(8,128)S(1)} %get-tuple-element.71), channel_id=1, source_target_pairs={{0,1},{1,0},{2,3},{3,2},{4,5},{5,4},{6,7},{7,6},{8,9},{9,8},{10,11... | collective-permute-start | bytes 2433032 | tf_op jit(solution)/shard_map/ppermute | solution.py:33
  53.6 4.9 %collective-permute-start.6 = (f32[256,768]{1,0:T(8,128)S(1)}, f32[256,768]{1,0:T(8,128)S(1)}, u32[]{:S(2)}, u32[]{:S(2)}) collective-permute-start(f32[256,768]{1,0:T(8,128)S(1)} %get-tuple-element.72), channel_id=1, source_target_pairs={{0,1},{1,0},{2,3},{3,2},{4,5},{5,4},{6,7},{7,6},{8,9},{9,8},{10,11... | collective-permute-start | bytes 2359304 | tf_op jit(solution)/shard_map/ppermute | solution.py:33
  63.5 9.3 %collective-permute-start.8 = (f32[256,512]{1,0:T(8,128)S(1)}, f32[256,512]{1,0:T(8,128)S(1)}, u32[]{:S(2)}, u32[]{:S(2)}) collective-permute-start(f32[256,512]{1,0:T(8,128)S(1)} %get-tuple-element.94.for_y_in), channel_id=1, source_target_pairs={{0,1},{2,3},{4,5},{6,7},{8,9},{10,11},{12,13},{14,15},{16,17},{18,... | collective-permute-start | bytes 1572872 | tf_op jit(solution)/shard_map/ppermute | solution.py:38
  69.6 17.2 %collective-permute-start.10 = (f32[256,512]{1,0:T(8,128)S(1)}, f32[256,512]{1,0:T(8,128)S(1)}, u32[]{:S(2)}, u32[]{:S(2)}) collective-permute-start(f32[256,512]{1,0:T(8,128)S(1)} %get-tuple-element.96), channel_id=1, source_target_pairs={{0,2},{1,511},{2,4},{3,1},{4,6},{5,3},{6,8},{7,5},{8,10},{9,7},{10... | collective-permute-start | bytes 1572872 | tf_op jit(solution)/shard_map/ppermute | solution.py:28
  71.5 15.2 %collective-permute-start.11 = (f32[256,512]{1,0:T(8,128)S(1)}, f32[256,512]{1,0:T(8,128)S(1)}, u32[]{:S(2)}, u32[]{:S(2)}) collective-permute-start(f32[256,512]{1,0:T(8,128)S(1)} %get-tuple-element.97), channel_id=1, source_target_pairs={{1,0},{3,2},{5,4},{7,6},{9,8},{11,10},{13,12},{15,14},{17,16},{19,... | collective-permute-start | bytes 1572872 | tf_op jit(solution)/shard_map/ppermute | solution.py:38
  73.0 16.5 %collective-permute-start.9 = (f32[256,512]{1,0:T(8,128)S(1)}, f32[256,512]{1,0:T(8,128)S(1)}, u32[]{:S(2)}, u32[]{:S(2)}) collective-permute-start(f32[256,512]{1,0:T(8,128)S(1)} %add_add_fusion.1), channel_id=1, source_target_pairs={{0,510},{1,3},{2,0},{3,5},{4,2},{5,7},{6,4},{7,9},{8,6},{9,11},{10... | collective-permute-start | bytes 1572872 | tf_op jit(solution)/shard_map/ppermute | solution.py:23
  86.9 16.5 %collective-permute-start.12 = (f32[256,512]{1,0:T(8,128)S(1)}, f32[256,512]{1,0:T(8,128)S(1)}, u32[]{:S(2)}, u32[]{:S(2)}) collective-permute-start(f32[256,512]{1,0:T(8,128)S(1)} %add_add_fusion), channel_id=1, source_target_pairs={{0,2},{1,511},{2,4},{3,1},{4,6},{5,3},{6,8},{7,5},{8,10},{9,7},{10... | collective-permute-start | bytes 1572872 | tf_op jit(solution)/shard_map/ppermute | solution.py:28
